TPU v7x, 32 devices: a whole 2x2x4 slice. The times are simulated.
32 devices in a mesh: seq: 8 (over z, y), tp: 4 (over x, core).
Axes of the slice: x: 2, y: 2, z: 4, core: 2. Of those that a mesh axis runs over, the one named last changes fastest.
Arguments:
- queries: bfloat16 [1536, 2048], P('seq', 'tp'), may hold values from -6 to 6
- keys: bfloat16 [1536, 2048], P('seq', 'tp'), may hold values from -6 to 6
- values: bfloat16 [1536, 2048], P('seq', 'tp'), may hold values from -6 to 6
- lengths: int32 [4], replicated, may hold values from 1 to 768, 1536 in all
- resid: bfloat16 [1536, 2048], P(('seq', 'tp')), may hold values from -6 to 6
- w_out: bfloat16 [2048, 2048], P('tp'), may hold values from -0.5 to 0.5
- moe_gain: float32 [2048], replicated, may hold values from 0.25 to 1.75
- routes: int32 [1536, 8], P(('seq', 'tp')), may hold values from 0 to 15, all different within a row; in each aligned block of 48 rows (0 to 47, 48 to 95, ...) at most 36 rows name the same one
- gates: float32 [1536, 8], P(('seq', 'tp')), may hold values from 0.05 to 0.3
- w_gate_up: bfloat16 [16, 2048, 2, 1024], P('seq', None, None, 'tp'), may hold values from -0.125 to 0.125
- w_down: bfloat16 [16, 1024, 2048], P('seq', 'tp'), may hold values from -0.1875 to 0.1875
Outputs:
- attended: bfloat16 [1536, 2048], P(('seq', 'tp'))
- expert_mix: bfloat16 [1536, 2048], P(('seq', 'tp'))
Inputs may be any that keep to these rules, and one draw needn't show every extreme that they name: The 4 lengths sum to 1536; the largest is exactly 768. `routes`: each row names 8 different experts. Within each aligned block of 48 rows (the rows of one device) no expert is named by more than 36 rows, a bound that some block reaches.
All inputs are finite; a program needn't handle non-finite values.
Results may differ from a plain program's by a relative error of at most 0.03.
Values may be sent and summed in bfloat16 or wider, within the bound.
No kernel may reach another device: no remote copies, remote signals or barrier semaphores. Data moves between devices by JAX's collectives and lax.ppermute only.
A program may use at most 128 MiB of HBM per device.

v0:
```python
import math

import jax
import jax.numpy as jnp
from jax import lax
from jax.sharding import PartitionSpec as P

HEAD_DIM = 128


def tenant_of(positions, lengths):
    bounds = jnp.cumsum(lengths)
    return jnp.sum((positions[:, None] >= bounds[None, :]).astype(jnp.int32), axis=1)


def shards(
    queries, keys, values, lengths, resid, w_out, moe_gain, routes, gates, w_gate_up, w_down
):
    seq_count = lax.axis_size("seq")
    query_rows = queries.shape[0]
    local_heads = queries.shape[1] // HEAD_DIM
    width = resid.shape[1]
    score_scale = 1.0 / math.sqrt(HEAD_DIM)
    query_pos = lax.axis_index("seq") * query_rows + jnp.arange(query_rows, dtype=jnp.int32)
    query_tenant = tenant_of(query_pos, lengths)
    query_heads = queries.reshape(query_rows, local_heads, HEAD_DIM)
    key_piece = lax.all_gather(keys, "seq", axis=0, tiled=True)
    value_piece = lax.all_gather(values, "seq", axis=0, tiled=True)
    row_count = key_piece.shape[0]
    key_pos = jnp.arange(row_count, dtype=jnp.int32)
    key_tenant = tenant_of(key_pos, lengths)
    visible = (key_tenant[None, :] == query_tenant[:, None]) & (
        key_pos[None, :] <= query_pos[:, None]
    )
    run_max = jnp.full((local_heads, query_rows), -1e30, jnp.float32)
    scores = (
        jnp.einsum(
            "qhd,khd->hqk",
            query_heads,
            key_piece.reshape(row_count, local_heads, HEAD_DIM),
            preferred_element_type=jnp.float32,
        )
        * score_scale
    )
    scores = jnp.where(visible[None], scores, -1e30)
    new_max = jnp.maximum(run_max, jnp.max(scores, axis=2))
    exponent = jnp.where(visible[None], jnp.exp(scores - new_max[:, :, None]), 0.0)
    run_sum = jnp.sum(exponent, axis=2)
    value_heads = value_piece.reshape(row_count, local_heads, HEAD_DIM)
    accumulated = jnp.einsum(
        "hqk,khd->hqd",
        exponent.astype(jnp.bfloat16),
        value_heads,
        preferred_element_type=jnp.float32,
    )
    run_max, run_sum, accumulated = (new_max, run_sum, accumulated)
    attention = (
        (accumulated / run_sum[:, :, None])
        .transpose(1, 0, 2)
        .reshape(query_rows, local_heads * HEAD_DIM)
    )
    attention = attention.astype(jnp.bfloat16)
    taken = attention
    projected = lax.psum_scatter(
        jnp.dot(taken, w_out, preferred_element_type=jnp.float32).astype(jnp.bfloat16),
        "tp",
        scatter_dimension=0,
        tiled=True,
    ).astype(jnp.float32)
    attended = (resid.astype(jnp.float32) + projected).astype(jnp.bfloat16)
    widened = attended.astype(jnp.float32)
    meansq = jnp.mean(widened * widened, axis=1, keepdims=True)
    normed = (widened * lax.rsqrt(meansq + 1e-05) * moe_gain[None, :]).astype(jnp.bfloat16)
    local_rows = resid.shape[0]
    top_count = routes.shape[1]
    owned = w_gate_up.shape[0]
    experts_all = owned * seq_count
    capacity = 3 * local_rows * top_count // (2 * experts_all)
    flat_routes = routes.reshape(-1)
    onehot = (flat_routes[:, None] == jnp.arange(experts_all, dtype=jnp.int32)[None, :]).astype(
        jnp.int32
    )
    slot_index = jnp.sum((jnp.cumsum(onehot, axis=0) - 1) * onehot, axis=1)
    token_index = jnp.arange(local_rows * top_count, dtype=jnp.int32) // top_count
    buffer = (
        jnp.zeros((experts_all, capacity, width), jnp.bfloat16)
        .at[flat_routes, slot_index]
        .set(normed[token_index])
    )
    arrived = lax.all_to_all(
        buffer.reshape(seq_count, owned, capacity, width),
        "seq",
        split_axis=0,
        concat_axis=0,
        tiled=True,
    )
    expand_arrived = lax.all_gather(arrived, "tp", axis=0, tiled=True)
    projections = jnp.einsum(
        "nxcd,xdgf->nxcgf", expand_arrived, w_gate_up, preferred_element_type=jnp.float32
    )
    hidden = (jax.nn.silu(projections[..., 0, :]) * projections[..., 1, :]).astype(jnp.bfloat16)
    taken = hidden
    summed = lax.psum_scatter(
        jnp.einsum("nxcf,xfd->nxcd", taken, w_down, preferred_element_type=jnp.float32).astype(
            jnp.bfloat16
        ),
        "tp",
        scatter_dimension=0,
        tiled=True,
    )
    returned = lax.all_to_all(summed, "seq", split_axis=0, concat_axis=0, tiled=True)
    picked = returned.reshape(experts_all, capacity, width)[flat_routes, slot_index]
    picked = picked.reshape(local_rows, top_count, width).astype(jnp.float32)
    expert_mix = jnp.sum(picked * gates[:, :, None], axis=1).astype(jnp.bfloat16)
    return (attended, expert_mix)


def solution(mesh):
    return jax.shard_map(
        shards,
        mesh=mesh,
        in_specs=(
            P("seq", "tp"),
            P("seq", "tp"),
            P("seq", "tp"),
            P(),
            P(("seq", "tp"), None),
            P("tp", None),
            P(),
            P(("seq", "tp"), None),
            P(("seq", "tp"), None),
            P("seq", None, None, "tp"),
            P("seq", "tp", None),
        ),
        out_specs=(P(("seq", "tp"), None), P(("seq", "tp"), None)),
        check_vma=False,
    )
```

profile of v0, /device:TPU:0, one launch (start us, length us, event | category | flops | bytes accessed | tf_op | source)
XLA Modules:
  0.0 653.5 jit_solution(7488797149590824402)
XLA Ops:
  10.2 46.9 %all-gather.4.cloned.1.call-done = bf16[1536,512]{1,0:T(8,128)(2,1)} async-done(((bf16[192,512]{1,0:T(8,128)(2,1)}), bf16[1536,512]{1,0:T(8,128)(2,1)}) %all-gather.4.cloned.1.call-update) | async-done | bytes 1572880 | tf_op jit(solution)/shard_map/all_gather | solution.py:27
  57.1 2.6 copy.49
  65.8 36.5 %all-gather.6.cloned.1.call-done = bf16[1536,512]{1,0:T(8,128)(2,1)} async-done(((bf16[192,512]{1,0:T(8,128)(2,1)}), bf16[1536,512]{1,0:T(8,128)(2,1)}) %all-gather.6.cloned.1.call-update) | async-done | bytes 1572880 | tf_op jit(solution)/shard_map/all_gather | solution.py:28
  102.3 2.6 copy.52
  104.9 4.3 fusion.30
  112.5 20.5 %reduce-scatter.2.cloned.1.call-done = bf16[48,2048]{1,0:T(8,128)(2,1)} async-done(((bf16[192,2048]{1,0:T(8,128)(2,1)}), bf16[48,2048]{1,0:T(8,128)(2,1)}) %reduce-scatter.2.cloned.1.call-update) | async-done | bytes 196624 | tf_op jit(solution)/shard_map/reduce_scatter | solution.py:64
  134.3 3.1 gather_fusion
  139.1 71.5 %scatter_fusion = bf16[16,36,2048]{2,0,1:T(8,128)(2,1)} fusion(bf16[16,36,2048]{2,0,1:T(8,128)(2,1)} %broadcast_in_dim.26, s32[384]{0:T(512)S(1)} %get-tuple-element.3, bf16[384,2048]{1,0:T(8,128)(2,1)} %gather_fusion), kind=kCustom, calls=%fused_computation.2 | custom fusion | bytes 4721664 | tf_op jit(solution)/shard_map/scatter | solution.py:88
  210.6 5.9 reshape.226
  216.5 3.4 copy.59
  219.9 59.2 %all_to_all.10 = bf16[8,2,36,2048]{3,1,2,0:T(2,128)(2,1)S(1)} all-to-all(bf16[8,2,36,2048]{3,1,2,0:T(2,128)(2,1)S(1)} %copy.59), channel_id=1, replica_groups=mesh['seq'=8,'tp'=4] {'seq'}, dimensions={0} | all-to-all | bytes 4718592 | tf_op jit(solution)/shard_map/all_to_all | solution.py:90
  279.1 2.6 copy.60
  281.8 68.4 %all-gather.8.cloned.1.call-done = bf16[32,2,36,2048]{3,2,0,1:T(8,128)(2,1)} async-done(((bf16[8,2,36,2048]{3,2,0,1:T(8,128)(2,1)}), bf16[32,2,36,2048]{3,2,0,1:T(8,128)(2,1)}) %all-gather.8.cloned.1.call-update) | async-done | bytes 9437200 | tf_op jit(solution)/shard_map/all_gather | solution.py:97
  350.2 9.5 %fusion.9 = f32[32,2,36,2,256]{4,2,3,0,1:T(8,128)S(1)} fusion(bf16[2,2048,2,256,1]{3,2,1,0,4:T(2,128)(2,1)} %bitcast.91, bf16[32,2,36,2048]{3,2,0,1:T(8,128)(2,1)} %all-gather.8.cloned.1.call-done), kind=kOutput, calls=%fused_computation.19 | convolution fusion | flops 4831838208 | bytes 18350080 | tf_op jit(solution)/shard_map/nxcd,xdgf->nxcgf/dot_general | solution.py:98
  359.7 5.7 convert_bitcast_fusion
  365.4 18.2 %copy.63 = bf16[32,2,36,2048]{3,1,2,0:T(2,128)(2,1)} copy(bf16[32,2,36,2048]{3,2,0,1:T(8,128)(2,1)} %convert_bitcast_fusion) | data formatting | bytes 18874368 | tf_op jit(solution)/shard_map/convert_element_type | solution.py:104
  385.5 168.1 %all-reduce.3.cloned.1.call-done = bf16[32,2,36,2048]{3,1,2,0:T(2,128)(2,1)} async-done(((bf16[32,2,36,2048]{3,1,2,0:T(2,128)(2,1)}), bf16[32,2,36,2048]{3,1,2,0:T(2,128)(2,1)}) %all-reduce.3.cloned.1.call-update) | async-done | bytes 9437200
  553.6 4.9 constant_dynamic-slice_fusion
  558.5 5.6 all-to-all-start.1
  564.3 53.7 %all-to-all-done.1 = bf16[8,2,36,2048]{3,1,2,0:T(2,128)(2,1)} async-done(((bf16[8,2,36,2048]{3,1,2,0:T(2,128)(2,1)}), bf16[8,2,36,2048]{3,1,2,0:T(2,128)(2,1)}, u32[]{:S(2)}, u32[]{:S(2)}) %all-to-all-start.1) | async-done | bytes 2359328 | tf_op jit(solution)/shard_map/all_to_all | solution.py:111
  618.0 5.6 copy.64
  623.6 6.1 reshape.227
  629.8 13.7 %gather_fusion.1 = bf16[384,2048]{1,0:T(8,128)(2,1)} fusion(bf16[16,36,2048]{2,0,1:T(8,128)(2,1)} %reshape.227, s32[384]{0:T(512)S(1)} %get-tuple-element.2), kind=kCustom, calls=%fused_computation.1 | custom fusion | bytes 3148800 | tf_op jit(solution)/shard_map/gather | solution.py:112
  643.4 3.5 fusion.6
  (57 shorter events, 16.6 us)
Async XLA Ops:
  7.2 352.6 %copy-start = (bf16[2,256,2048]{2,1,0:T(8,128)(2,1)S(1)}, bf16[2,256,2048]{2,1,0:T(8,128)(2,1)}, u32[]{:S(2)}) copy-start(bf16[2,256,2048]{2,1,0:T(8,128)(2,1)} %param.21) | copy-start | bytes 6291460
  7.2 52.5 %copy-start.4 = (bf16[192,512]{1,0:T(8,128)(2,1)S(1)}, bf16[192,512]{1,0:T(8,128)(2,1)}, u32[]{:S(2)}) copy-start(bf16[192,512]{1,0:T(8,128)(2,1)} %param.11) | copy-start | bytes 589828
  7.2 49.9 %all-gather.4.cloned.1.call-start = ((), (), s32[]{:S(2)}) async-start(), calls=%async_computation.3 | async-start | bytes 1769472 | tf_op jit(solution)/shard_map/all_gather | solution.py:27
  7.9 94.4 %all-gather.6.cloned.1.call-start = ((), (), s32[]{:S(2)}) async-start(), calls=%async_computation.4 | async-start | bytes 1769472 | tf_op jit(solution)/shard_map/all_gather | solution.py:28
  8.7 124.3 %reduce-scatter.2.cloned.1.call-start = ((), (), s32[]{:S(2)}) async-start(), calls=%async_computation.5 | async-start | bytes 983040 | tf_op jit(solution)/shard_map/reduce_scatter | solution.py:64
  62.2 2.1 copy-start.1
  104.9 4.3 copy-start.2
  109.2 1.6 copy-start.7
  109.3 23.7 %copy-start.5 = (bf16[48,2048]{1,0:T(8,128)(2,1)S(1)}, bf16[48,2048]{1,0:T(8,128)(2,1)}, u32[]{:S(2)}) copy-start(bf16[48,2048]{1,0:T(8,128)(2,1)} %param.15) | copy-start | bytes 589828
  109.3 24.9 %copy-start.6 = (f32[2048]{0:T(1024)S(1)}, f32[2048]{0:T(1024)}, u32[]{:S(2)}) copy-start(f32[2048]{0:T(1024)} %param.17) | copy-start | bytes 24580
  110.8 239.4 %all-gather.8.cloned.1.call-start = ((), (), s32[]{:S(2)}) async-start(), calls=%async_computation.6 | async-start | bytes 13107200 | tf_op jit(solution)/shard_map/all_gather | solution.py:97
  134.1 3.3 copy-start.3
  281.7 271.9 %all-reduce.3.cloned.1.call-start = ((), (), s32[]{:S(2)}) async-start(), calls=%async_computation.7 | async-start | bytes 18874368
  383.6 0.7 copy-start.9
  558.5 5.7 copy-start.8
  558.5 59.4 %all-to-all-start.1 = ((bf16[8,2,36,2048]{3,1,2,0:T(2,128)(2,1)}), bf16[8,2,36,2048]{3,1,2,0:T(2,128)(2,1)}, u32[]{:S(2)}, u32[]{:S(2)}) async-start(bf16[8,2,36,2048]{3,1,2,0:T(2,128)(2,1)} %constant_dynamic-slice_fusion), calls=%async_computation.2 | async-start | bytes 4718592 | tf_op jit(solution)/shard_map/all_to_all | solution.py:111
Sparse Core Ops, SparseCore 0:
  10.2 46.8 all-gather.3
  59.3 42.9 all-gather.5
  110.9 22.0 reduce-scatter.1
  281.9 68.2 all-gather.7
  383.8 169.7 all-reduce.2
where the time goes:
time: 656 us; the launch traced here: 654 us
  waiting for transfers between devices  396 us (60%)
  local copies, waits for them, and re-layouts  146 us (22%)
  blocking collectives  59.2 us (9%)
  matrix products  23.5 us (4%)
  between operations  14.6 us (2%)
  other arithmetic  8.8 us (1%)
    unnamed x6, waiting for transfers between devices  170 us
    scatter x1, local copies, waits for them, and re-layouts, shards(): buffer = jnp.zeros((experts_all, capacity, width), jnp.bfloat16).at[flat_...  71.5 us
    all_gather x1, waiting for transfers between devices, shards(): expand_arrived = lax.all_gather(arrived, 'tp', axis=0, tiled=True)  68.4 us
    all_to_all x1, blocking collectives, shards(): lax.all_to_all(buffer.reshape(seq_count, owned, capacity, width), 'seq',...  59.2 us
    all_to_all x1, waiting for transfers between devices, shards(): lax.all_to_all(summed, 'seq', split_axis=0, concat_axis=0, tiled=True)  53.7 us
    all_gather x1, waiting for transfers between devices, shards(): key_piece = lax.all_gather(keys, 'seq', axis=0, tiled=True)  46.9 us
    all_gather x1, waiting for transfers between devices, shards(): value_piece = lax.all_gather(values, 'seq', axis=0, tiled=True)  36.5 us
    reduce_scatter x1, waiting for transfers between devices, shards(): lax.psum_scatter(jnp.dot(taken, w_out, preferred_element_type=jnp.float32...  20.5 us
  transfers between devices with their start and end apart: 6, of which 6 were waited for; matrix products, arithmetic and copies ran while one was open for 2% of the time, Pallas kernels for 0%

commit v1 on v0

v1 whole, which is shorter than its diff:
```python
import functools
import math

import jax
import jax.numpy as jnp
from jax import lax
from jax.experimental import pallas as pl
from jax.experimental.pallas import tpu as pltpu
from jax.sharding import PartitionSpec as P

HEAD_DIM = 128
F32 = jnp.float32
BF16 = jnp.bfloat16


def over_y(a):
    count = lax.axis_size("seq")
    return lax.ppermute(a, "seq", [(i, i ^ 1) for i in range(count)])


def over_z(a, step):
    count = lax.axis_size("seq")
    return lax.ppermute(a, "seq", [(i, (i + 2 * step) % count) for i in range(count)])


def over_x(a):
    return lax.ppermute(a, "tp", [(i, i ^ 2) for i in range(4)])


def over_core(a):
    return lax.ppermute(a, "tp", [(i, i ^ 1) for i in range(4)])


def ring_gather(unit, down_from=0):
    half = lax.axis_size("seq") // 4
    middle = unit.shape[0] // 2
    up, down = [unit], [unit[down_from:]]
    for _ in range(1, half):
        up.append(over_z(up[-1], 1))
        down.append(over_z(down[-1], -1))
    far = (over_z(up[-1][:middle], 1), over_z(down[-1][middle - down_from :], -1))
    return up, down, far


def ring_scatter(parts):
    half = lax.axis_size("seq") // 4
    middle = parts.shape[1] // 2
    own, ups, downs, far = parts[0], parts[1:half], parts[half:-1], parts[-1]
    plus = over_z(far[:middle], 1)
    minus = over_z(far[middle:], -1)
    for k in reversed(range(half - 1)):
        high, low = downs[k], ups[k]
        if plus.shape[0] == middle:
            high = jnp.concatenate([add(high[:middle], plus), high[middle:]], 0)
            low = jnp.concatenate([low[:middle], add(low[middle:], minus)], 0)
        else:
            high, low = add(high, plus), add(low, minus)
        plus, minus = over_z(high, 1), over_z(low, -1)
    return (own.astype(F32) + plus.astype(F32) + minus.astype(F32)).astype(BF16)


def add(a, b):
    return (a.astype(F32) + b.astype(F32)).astype(BF16)


def relative_rows(a, x, core):
    blocks = a.reshape((2, 2, a.shape[0] // 4) + a.shape[1:])
    blocks = jnp.where(x == 0, blocks, blocks[::-1])
    blocks = jnp.where(core == 0, blocks, blocks[:, ::-1])
    return jnp.swapaxes(blocks, 0, 1).reshape(a.shape)


def attention_kernel(scale, bases, q_ref, pos_ref, start_ref, *refs):
    kv_refs, out_ref = refs[:-1], refs[-1]
    piece = q_ref.shape[0] // 2
    key_pos, n = [], 0
    for kv in kv_refs:
        rows = kv.shape[0]
        column = lax.broadcasted_iota(jnp.int32, (1, rows), 1)
        if rows == piece:
            key_pos.append(column + bases[n])
            n += 1
        else:
            key_pos.append(
                jnp.where(column < piece, column + bases[n], column + (bases[n + 1] - piece))
            )
            n += 2
    width = q_ref.shape[1]
    for part in range(2):
        rows = pl.ds(part * piece, piece)
        pos, start = pos_ref[rows, :], start_ref[rows, :]
        masks = [(k >= start) & (k <= pos) for k in key_pos]
        for head in range(width // HEAD_DIM):
            lanes = pl.ds(head * HEAD_DIM, HEAD_DIM)
            value_lanes = pl.ds(width + head * HEAD_DIM, HEAD_DIM)
            q = q_ref[rows, lanes]
            scores = [
                jnp.where(
                    mask,
                    lax.dot_general(
                        q, kv[:, lanes], (((1,), (1,)), ((), ())), preferred_element_type=F32
                    )
                    * scale,
                    -1e30,
                )
                for kv, mask in zip(kv_refs, masks)
            ]
            top = functools.reduce(jnp.maximum, [jnp.max(v, axis=1, keepdims=True) for v in scores])
            total, mixed = 0.0, 0.0
            for kv, mask, score in zip(kv_refs, masks, scores):
                weight = jnp.where(mask, jnp.exp(score - top), 0.0)
                total = total + jnp.sum(weight, axis=1, keepdims=True)
                mixed = mixed + jnp.dot(
                    weight.astype(BF16), kv[:, value_lanes], preferred_element_type=F32
                )
            out_ref[rows, lanes] = (mixed / total).astype(BF16)


def attend(q, pos, start, bases, blocks):
    vmem = pl.BlockSpec(memory_space=pltpu.VMEM)
    keys = sum(b.shape[0] for b in blocks)
    return pl.pallas_call(
        functools.partial(attention_kernel, 1.0 / math.sqrt(HEAD_DIM)),
        out_shape=jax.ShapeDtypeStruct(q.shape, BF16),
        in_specs=[pl.BlockSpec(memory_space=pltpu.SMEM)] + [vmem] * (3 + len(blocks)),
        out_specs=vmem,
        compiler_params=pltpu.CompilerParams(vmem_limit_bytes=40 * 1024 * 1024),
        cost_estimate=pl.CostEstimate(
            flops=4 * q.shape[0] * q.shape[1] * keys,
            bytes_accessed=4 * q.size + 4 * keys * q.shape[1],
            transcendentals=q.shape[0] * q.shape[1] // HEAD_DIM * keys,
        ),
    )(bases, q, pos, start, *blocks)


def attention(queries, keys, values, lengths, seq, x, core):
    ring = lax.axis_size("seq") // 2
    y, z = seq % 2, seq // 2
    rows, width = queries.shape
    half = width // 2

    def split(a):
        left, right = a[:, :half], a[:, half:]
        return jnp.where(y == 0, left, right), jnp.where(y == 0, right, left)

    (k_own, k_other), (v_own, v_other) = split(keys), split(values)
    kv = jnp.concatenate([k_own, v_own], 1)
    kv_other = over_y(jnp.concatenate([k_other, v_other], 1))
    q_own, q_other = split(relative_rows(queries, x, core))
    q = jnp.concatenate([q_own, over_y(q_other)], 0)
    up, _, far = ring_gather(jnp.concatenate([kv, kv_other], 0), rows)
    blocks = list(up) + list(far)
    shard = [((z - k) % ring) * 2 + other for k in range(ring // 2 + 1) for other in (y, 1 - y)]
    bases = jnp.stack(shard).astype(jnp.int32) * rows

    local = relative_rows(jnp.arange(rows, dtype=jnp.int32), x, core)
    pos = jnp.concatenate([seq * rows + local, (seq ^ 1) * rows + local])
    bounds = jnp.cumsum(lengths)
    start = jnp.max(jnp.where(bounds[None, :] <= pos[:, None], bounds[None, :], 0), axis=1)
    out = attend(q, pos[:, None], start[:, None], bases, blocks)
    return out[:rows], over_y(out[rows:])


def gather_tokens(unit):
    middle = unit.shape[0] // 2
    up, down, far = ring_gather(unit)
    beside = over_y(unit)
    r_up, r_down, r_far = ring_gather(beside[middle:])
    pieces = [unit, beside]
    for own, right in zip(up[1:] + down[1:], r_up[1:] + r_down[1:]):
        pieces += [own, over_y(own[:middle]), right]
    pieces += [far[0], far[1], over_y(far[0]), r_far[0], r_far[1]]
    return jnp.concatenate(pieces, 0)


def experts(tokens, width, first, w_in, w_down):
    owned = w_down.shape[0]
    inner = w_down.shape[1]
    count = lax.axis_size("seq") * owned
    weight = tokens[:, width : width + count].astype(F32)
    weight = weight + tokens[:, width + count : width + 2 * count].astype(F32)
    column = lax.broadcasted_iota(jnp.int32, (1, count), 1)
    projections = jnp.dot(tokens[:, :width], w_in, preferred_element_type=F32)
    hidden = []
    for e in range(owned):
        factor = jnp.sum(jnp.where(column == first + e, weight, 0.0), axis=1, keepdims=True)
        gate = projections[:, 2 * e * inner : (2 * e + 1) * inner]
        up = projections[:, (2 * e + 1) * inner : (2 * e + 2) * inner]
        hidden.append(jnp.where(factor > 0, jax.nn.silu(gate) * up * factor, 0.0).astype(BF16))
    return jnp.dot(
        jnp.concatenate(hidden, 1),
        w_down.reshape(owned * inner, width),
        preferred_element_type=F32,
    )


def scatter_sums(total, rows):
    width = total.shape[1]
    ring = lax.axis_size("seq") // 2
    first = width * 5 // 16
    total = total.reshape(ring, 2, 2, rows, width)
    a, b, c = total[..., :first], total[..., first : 2 * first], total[..., 2 * first :]
    a = add(a[:, :, 0], over_x(a[:, :, 1]))
    b = add(b[:, 0], over_y(b[:, 1]))
    c = ring_scatter(c.reshape(ring, 4 * rows, -1)).reshape(2, 2 * rows, -1)
    ab = ring_scatter(jnp.concatenate([a, b], 1).reshape(ring, 4 * rows, -1))
    ab = ab.reshape(4, rows, -1)
    c = add(c[0], over_y(c[1])).reshape(2, rows, -1)
    a = add(ab[0], over_y(ab[1]))
    b = add(ab[2], over_x(ab[3]))
    c = add(c[0], over_x(c[1]))
    return jnp.concatenate([a, b, c], 1)


def shards(
    queries, keys, values, lengths, resid, w_out, moe_gain, routes, gates, w_gate_up, w_down
):
    seq, tp = lax.axis_index("seq"), lax.axis_index("tp")
    x, core, y = tp // 2, tp % 2, seq % 2
    rows, width = resid.shape
    owned = w_gate_up.shape[0]
    count = owned * lax.axis_size("seq")
    half = w_out.shape[0] // 2

    own, other = attention(queries, keys, values, lengths, seq, x, core)
    w_own = jnp.where(y == 0, w_out[:half], w_out[half:])
    w_other = jnp.where(y == 0, w_out[half:], w_out[:half])
    projected = jnp.dot(own, w_own, preferred_element_type=F32)
    projected = projected + jnp.dot(other, w_other, preferred_element_type=F32)

    matches = routes[:, :, None] == jnp.arange(count, dtype=jnp.int32)[None, None, :]
    weight = jnp.sum(jnp.where(matches, gates[:, :, None], 0.0), axis=1)
    high = weight.astype(BF16)
    low = (weight - high.astype(F32)).astype(BF16)
    pad = -(-2 * count // 128) * 128 - 2 * count
    packed = jnp.concatenate([high, low, jnp.zeros((rows, pad), BF16)], 1)
    packed = jnp.concatenate([packed, over_x(packed)], 0)

    received = over_core(projected[2 * rows :].astype(BF16))
    partial = projected[: 2 * rows] + received.astype(F32)
    partial = jnp.concatenate([partial[:rows] + resid.astype(F32), partial[rows:]], 0)
    arrived = over_x(partial.astype(BF16)).reshape(2, rows, width)[::-1]
    attended = (partial + arrived.reshape(2 * rows, width).astype(F32)).astype(BF16)
    widened = attended.astype(F32)
    meansq = jnp.mean(widened * widened, axis=1, keepdims=True)
    normed = (widened * lax.rsqrt(meansq + 1e-05) * moe_gain[None, :]).astype(BF16)

    tokens = gather_tokens(jnp.concatenate([normed, packed], 1))
    tokens_other = over_core(tokens)
    w_in = w_gate_up.transpose(1, 0, 2, 3).reshape(width, -1)
    first = owned * seq
    sums_other = experts(tokens_other, width, first, w_in, w_down).astype(BF16)
    sums = experts(tokens, width, first, w_in, w_down)
    sums = (sums + over_core(sums_other).astype(F32)).astype(BF16)
    return attended[:rows], scatter_sums(sums, rows)


def solution(mesh):
    return jax.shard_map(
        shards,
        mesh=mesh,
        in_specs=(
            P("seq", "tp"),
            P("seq", "tp"),
            P("seq", "tp"),
            P(),
            P(("seq", "tp"), None),
            P("tp", None),
            P(),
            P(("seq", "tp"), None),
            P(("seq", "tp"), None),
            P("seq", None, None, "tp"),
            P("seq", "tp", None),
        ),
        out_specs=(P(("seq", "tp"), None), P(("seq", "tp"), None)),
        check_vma=False,
    )
```

time: 656 us -> 199 us (0.30)
  waiting for transfers between devices: 396 us -> 94.1 us
  local copies, waits for them, and re-layouts: 146 us -> 22.8 us
  blocking collectives: 59.2 us -> 0 us
  starting transfers between devices: 5.85 us -> 47.6 us
  between operations: 14.6 us -> 1.29 us
    unnamed x6 -> x0, waiting for transfers between devices: 170 us -> none
    all_gather x3 -> x0, waiting for transfers between devices: 152 us -> none  [the longest x1 68.4 us: shards(): expand_arrived = lax.all_gather(arrived, 'tp', axis=0, tiled=True)]
    ppermute x0 -> x38, waiting for transfers between devices: none -> 94.1 us  [the longest x20 61.5 us: over_z(): lax.ppermute(a, 'seq', [(i, (i + 2 * step) % count) for i in range(count)])]
    scatter x1 -> x0, local copies, waits for them, and re-layouts: 71.5 us -> none  [shards(): buffer = jnp.zeros((experts_all, capacity, width), jnp.bfloat16).at[flat_...]
    all_to_all x1 -> x0, blocking collectives: 59.2 us -> none  [shards(): lax.all_to_all(buffer.reshape(seq_count, owned, capacity, width), 'seq',...]
    all_to_all x1 -> x0, waiting for transfers between devices: 53.7 us -> none  [shards(): lax.all_to_all(summed, 'seq', split_axis=0, concat_axis=0, tiled=True)]
    ppermute x0 -> x38, starting transfers between devices: none -> 47.6 us  [the longest x20 32.3 us: over_z(): lax.ppermute(a, 'seq', [(i, (i + 2 * step) % count) for i in range(count)])]
    reduce_scatter x1 -> x0, waiting for transfers between devices: 20.5 us -> none  [shards(): lax.psum_scatter(jnp.dot(taken, w_out, preferred_element_type=jnp.float32...]
  transfers between devices with their start and end apart: 6 -> 38, of which waited for: 6 -> 21; matrix products, arithmetic and copies ran while one was open for 2% -> 17% of each run, Pallas kernels for 0% -> 0%
where the time goes in v1:
time: 199 us
  waiting for transfers between devices  94.1 us (47%)
  starting transfers between devices  47.6 us (24%)
  local copies, waits for them, and re-layouts  22.8 us (11%)
  matrix products  17.7 us (9%)
  other arithmetic  12.1 us (6%)
  Pallas kernels  3.09 us (2%)
    ppermute x20, waiting for transfers between devices, over_z(): lax.ppermute(a, 'seq', [(i, (i + 2 * step) % count) for i in range(count)])  61.5 us
    ppermute x20, starting transfers between devices, over_z(): lax.ppermute(a, 'seq', [(i, (i + 2 * step) % count) for i in range(count)])  32.3 us
    ppermute x10, waiting for transfers between devices, over_y(): return lax.ppermute(a, 'seq', [(i, i ^ 1) for i in range(count)])  20.6 us
    unnamed x28, local copies, waits for them, and re-layouts  19.2 us
    dot_general x2, matrix products, experts(): projections = jnp.dot(tokens[:, :width], w_in, preferred_element_type=F32)  11.7 us
    ppermute x5, waiting for transfers between devices, over_x(): return lax.ppermute(a, 'tp', [(i, i ^ 2) for i in range(4)])  10.3 us
    ppermute x10, starting transfers between devices, over_y(): return lax.ppermute(a, 'seq', [(i, i ^ 1) for i in range(count)])  9.38 us
    ppermute x5, starting transfers between devices, over_x(): return lax.ppermute(a, 'tp', [(i, i ^ 2) for i in range(4)])  5.28 us
  transfers between devices with their start and end apart: 38, of which 21 were waited for; matrix products, arithmetic and copies ran while one was open for 17% of the time, Pallas kernels for 0%

profile of v1, /device:TPU:0, one launch (start us, length us, event | category | flops | bytes accessed | tf_op | source)
XLA Modules:
  0.0 198.7 jit_solution(1160659444472870147)
XLA Ops:
  1.9 3.0 %collective-permute-start = (bf16[192,256]{1,0:T(8,128)(2,1)S(1)}, bf16[192,256]{1,0:T(8,128)(2,1)}, u32[]{:S(2)}, u32[]{:S(2)}) collective-permute-start(bf16[192,256]{1,0:T(8,128)(2,1)S(1)} %get-tuple-element.45), channel_id=1, source_target_pairs={{0,4},{4,0},{8,12},{12,8},{16,20},{20,16},{24,28},{28,24},{1,5},{5... | collective-permute-start | bytes 294920 | tf_op jit(solution)/shard_map/ppermute | solution.py:18
  6.2 6.3 %collective-permute-done.1 = bf16[192,512]{1,0:T(8,128)(2,1)S(1)} collective-permute-done((bf16[192,512]{1,0:T(8,128)(2,1)S(1)}, bf16[192,512]{1,0:T(8,128)(2,1)S(1)}, u32[]{:S(2)}, u32[]{:S(2)}) %collective-permute-start.1) | collective-permute-done | bytes 196640 | tf_op jit(solution)/shard_map/ppermute | solution.py:18
  17.0 11.3 %collective-permute-done.4 = bf16[192,512]{1,0:T(8,128)(2,1)S(1)} collective-permute-done((bf16[192,512]{1,0:T(8,128)(2,1)S(1)}, bf16[192,512]{1,0:T(8,128)(2,1)S(1)}, u32[]{:S(2)}, u32[]{:S(2)}) %collective-permute-start.4) | collective-permute-done | bytes 196640 | tf_op jit(solution)/shard_map/ppermute | solution.py:23
  31.5 7.8 %collective-permute-done.5.refs_3_ = bf16[192,512]{1,0:T(8,128)(2,1)S(1)} collective-permute-done((bf16[192,512]{1,0:T(8,128)(2,1)S(1)}, bf16[192,512]{1,0:T(8,128)(2,1)S(1)}, u32[]{:S(2)}, u32[]{:S(2)}) %collective-permute-start.5) | collective-permute-done | bytes 196640 | tf_op jit(solution)/shard_map/ppermute | solution.py:23
  39.3 3.1 %shard_map.122 = bf16[384,256]{1,0:T(8,128)(2,1)S(1)} custom-call(s32[6]{0:T(128)S(1)} %broadcast_multiply_fusion.bases, bf16[384,256]{1,0:T(8,128)(2,1)S(1)} %pad_maximum_fusion.10.q_ref, s32[384,1]{1,0:T(8,128)S(1)} %broadcast_in_dim.113.pos_ref, s32[384,1]{1,0:T(8,128)S(1)} %broadcast_in_dim.114.start_ref, ...), custom_call_target="tpu_custom_call" | custom-call | flops 452984832 | bytes 1572864 | tf_op jit(solution)/shard_map/pallas_call | solution.py:122
  44.5 2.6 %collective-permute-done.6 = bf16[192,256]{1,0:T(8,128)(2,1)S(1)} collective-permute-done((bf16[192,256]{1,0:T(8,128)(2,1)S(1)}, bf16[192,256]{1,0:T(8,128)(2,1)S(1)}, u32[]{:S(2)}, u32[]{:S(2)}) %collective-permute-start.6) | collective-permute-done | bytes 98336 | tf_op jit(solution)/shard_map/ppermute | solution.py:18
  54.8 9.1 %collective-permute-done.8 = bf16[96,2048]{1,0:T(8,128)(2,1)S(1)} collective-permute-done((bf16[96,2048]{1,0:T(8,128)(2,1)}, bf16[96,2048]{1,0:T(8,128)(2,1)S(1)}, u32[]{:S(2)}, u32[]{:S(2)}) %collective-permute-start.8) | collective-permute-done | bytes 393248 | tf_op jit(solution)/shard_map/ppermute | solution.py:27
  69.9 3.2 %collective-permute-start.14 = (bf16[96,2176]{1,0:T(8,128)(2,1)S(1)}, bf16[96,2176]{1,0:T(8,128)(2,1)S(1)}, u32[]{:S(2)}, u32[]{:S(2)}) collective-permute-start(bf16[96,2176]{1,0:T(8,128)(2,1)S(1)} %get-tuple-element.9), channel_id=1, source_target_pairs={{0,24},{4,28},{8,0},{12,4},{16,8},{20,12},{24,16},{28,20},{1,25},{... | collective-permute-start | bytes 1253384 | tf_op jit(solution)/shard_map/ppermute | solution.py:23
  73.1 5.2 %collective-permute-done.10 = bf16[96,2176]{1,0:T(8,128)(2,1)S(1)} collective-permute-done((bf16[96,2176]{1,0:T(8,128)(2,1)S(1)}, bf16[96,2176]{1,0:T(8,128)(2,1)S(1)}, u32[]{:S(2)}, u32[]{:S(2)}) %collective-permute-start.10) | collective-permute-done | bytes 417824 | tf_op jit(solution)/shard_map/ppermute | solution.py:18
  79.0 3.2 %collective-permute-start.16 = (bf16[48,2176]{1,0:T(8,128)(2,1)S(1)}, bf16[48,2176]{1,0:T(8,128)(2,1)S(1)}, u32[]{:S(2)}, u32[]{:S(2)}) collective-permute-start(bf16[48,2176]{1,0:T(8,128)(2,1)S(1)} %slice.350), channel_id=1, source_target_pairs={{0,24},{4,28},{8,0},{12,4},{16,8},{20,12},{24,16},{28,20},{1,25},{... | collective-permute-start | bytes 626696 | tf_op jit(solution)/shard_map/ppermute | solution.py:23
  84.0 3.7 %collective-permute-start.17 = (bf16[48,2176]{1,0:T(8,128)(2,1)S(1)}, bf16[48,2176]{1,0:T(8,128)(2,1)S(1)}, u32[]{:S(2)}, u32[]{:S(2)}) collective-permute-start(bf16[48,2176]{1,0:T(8,128)(2,1)S(1)} %slice.349), channel_id=1, source_target_pairs={{0,8},{4,12},{8,16},{12,20},{16,24},{20,28},{24,0},{28,4},{1,9},{5... | collective-permute-start | bytes 626696 | tf_op jit(solution)/shard_map/ppermute | solution.py:23
  87.7 5.6 %collective-permute-done.14 = bf16[96,2176]{1,0:T(8,128)(2,1)S(1)} collective-permute-done((bf16[96,2176]{1,0:T(8,128)(2,1)S(1)}, bf16[96,2176]{1,0:T(8,128)(2,1)S(1)}, u32[]{:S(2)}, u32[]{:S(2)}) %collective-permute-start.14) | collective-permute-done | bytes 417824 | tf_op jit(solution)/shard_map/ppermute | solution.py:23
  97.5 4.1 %collective-permute-done.16 = bf16[48,2176]{1,0:T(8,128)(2,1)S(1)} collective-permute-done((bf16[48,2176]{1,0:T(8,128)(2,1)S(1)}, bf16[48,2176]{1,0:T(8,128)(2,1)S(1)}, u32[]{:S(2)}, u32[]{:S(2)}) %collective-permute-start.16) | collective-permute-done | bytes 208928 | tf_op jit(solution)/shard_map/ppermute | solution.py:23
  102.7 3.0 %collective-permute-start.21 = (bf16[24,2176]{1,0:T(8,128)(2,1)S(1)}, bf16[24,2176]{1,0:T(8,128)(2,1)S(1)}, u32[]{:S(2)}, u32[]{:S(2)}) collective-permute-start(bf16[24,2176]{1,0:T(8,128)(2,1)S(1)} %slice.354), channel_id=1, source_target_pairs={{0,24},{4,28},{8,0},{12,4},{16,8},{20,12},{24,16},{28,20},{1,25},{... | collective-permute-start | bytes 313352 | tf_op jit(solution)/shard_map/ppermute | solution.py:23
  110.7 4.4 %collective-permute-done.19 = bf16[48,2176]{1,0:T(8,128)(2,1)S(1)} collective-permute-done((bf16[48,2176]{1,0:T(8,128)(2,1)S(1)}, bf16[48,2176]{1,0:T(8,128)(2,1)S(1)}, u32[]{:S(2)}, u32[]{:S(2)}) %collective-permute-start.19) | collective-permute-done | bytes 208928 | tf_op jit(solution)/shard_map/ppermute | solution.py:18
  117.2 11.2 %copy.46 = bf16[2,2048,2,256]{1,3,2,0:T(8,128)(2,1)} copy(bf16[2,2048,2,256]{3,2,1,0:T(2,128)(2,1)} %param.20) | data formatting | bytes 8388608 | tf_op args[9]
  130.3 6.2 %fusion = f32[768,1024]{1,0:T(8,128)S(1)} fusion(bf16[2048,1024]{0,1:T(8,128)(2,1)} %bitcast.81, bf16[768,2176]{1,0:T(8,128)(2,1)} %collective-permute-done.22), kind=kOutput, calls=%fused_computation.2 | convolution fusion | flops 3221225472 | bytes 10485760 | tf_op jit(solution)/shard_map/dot_general | solution.py:183
  139.7 5.5 %fusion.2 = f32[768,1024]{1,0:T(8,128)S(1)} fusion(bf16[2048,1024]{0,1:T(8,128)(2,1)S(1)} %bitcast.82, bf16[768,2176]{1,0:T(8,128)(2,1)} %constant_dynamic-update-slice_fusion), kind=kOutput, calls=%fused_computation.4 | convolution fusion | flops 3221225472 | bytes 10485760 | tf_op jit(solution)/shard_map/dot_general | solution.py:183
  150.1 7.1 %collective-permute-done.34 = bf16[96,768]{1,0:T(8,128)(2,1)S(1)} collective-permute-done((bf16[96,768]{1,0:T(8,128)(2,1)S(1)}, bf16[96,768]{1,0:T(8,128)(2,1)S(1)}, u32[]{:S(2)}, u32[]{:S(2)}) %collective-permute-start.34) | collective-permute-done | bytes 147488 | tf_op jit(solution)/shard_map/ppermute | solution.py:23
  161.8 10.3 %collective-permute-done.35 = bf16[192,768]{1,0:T(8,128)(2,1)S(1)} collective-permute-done((bf16[192,768]{1,0:T(8,128)(2,1)S(1)}, bf16[192,768]{1,0:T(8,128)(2,1)S(1)}, u32[]{:S(2)}, u32[]{:S(2)}) %collective-permute-start.35) | collective-permute-done | bytes 294944 | tf_op jit(solution)/shard_map/ppermute | solution.py:23
  175.4 2.9 %collective-permute-done.28 = bf16[96,640]{1,0:T(8,128)(2,1)S(1)} collective-permute-done((bf16[96,640]{1,0:T(8,128)(2,1)S(1)}, bf16[96,640]{1,0:T(8,128)(2,1)S(1)}, u32[]{:S(2)}, u32[]{:S(2)}) %collective-permute-start.28) | collective-permute-done | bytes 122912 | tf_op jit(solution)/shard_map/ppermute | solution.py:23
  178.4 4.1 %collective-permute-start.29 = (bf16[192,640]{1,0:T(8,128)(2,1)S(1)}, bf16[192,640]{1,0:T(8,128)(2,1)S(1)}, u32[]{:S(2)}, u32[]{:S(2)}) collective-permute-start(bf16[192,640]{1,0:T(8,128)(2,1)S(1)} %pad_maximum_fusion.9), channel_id=1, source_target_pairs={{0,24},{4,28},{8,0},{12,4},{16,8},{20,12},{24,16},{28,20},{1,25},{... | collective-permute-start | bytes 737288 | tf_op jit(solution)/shard_map/ppermute | solution.py:23
  184.1 3.6 %collective-permute-done.29 = bf16[192,640]{1,0:T(8,128)(2,1)S(1)} collective-permute-done((bf16[192,640]{1,0:T(8,128)(2,1)S(1)}, bf16[192,640]{1,0:T(8,128)(2,1)S(1)}, u32[]{:S(2)}, u32[]{:S(2)}) %collective-permute-start.29) | collective-permute-done | bytes 245792 | tf_op jit(solution)/shard_map/ppermute | solution.py:23
  187.7 4.7 %collective-permute-done.27 = bf16[192,640]{1,0:T(8,128)(2,1)S(1)} collective-permute-done((bf16[192,640]{1,0:T(8,128)(2,1)S(1)}, bf16[192,640]{1,0:T(8,128)(2,1)S(1)}, u32[]{:S(2)}, u32[]{:S(2)}) %collective-permute-start.27) | collective-permute-done | bytes 245792 | tf_op jit(solution)/shard_map/ppermute | solution.py:23
  (167 shorter events, 66.3 us)
Async XLA Ops:
  1.9 28.7 %collective-permute-start = (bf16[192,256]{1,0:T(8,128)(2,1)S(1)}, bf16[192,256]{1,0:T(8,128)(2,1)}, u32[]{:S(2)}, u32[]{:S(2)}) collective-permute-start(bf16[192,256]{1,0:T(8,128)(2,1)S(1)} %get-tuple-element.45), channel_id=1, source_target_pairs={{0,4},{4,0},{8,12},{12,8},{16,20},{20,16},{24,28},{28,24},{1,5},{5... | collective-permute-start | bytes 294920 | tf_op jit(solution)/shard_map/ppermute | solution.py:18
  12.5 17.5 %collective-permute-start.2 = (bf16[384,512]{1,0:T(8,128)(2,1)S(1)}, bf16[384,512]{1,0:T(8,128)(2,1)S(1)}, u32[]{:S(2)}, u32[]{:S(2)}) collective-permute-start(bf16[384,512]{1,0:T(8,128)(2,1)S(1)} %pad_maximum_fusion.4.refs_0_), channel_id=1, source_target_pairs={{0,8},{4,12},{8,16},{12,20},{16,24},{20,28},{24,0},{28,4},{1,9},{5... | collective-permute-start | bytes 1179656 | tf_op jit(solution)/shard_map/ppermute | solution.py:23
  14.8 13.5 %collective-permute-start.4 = (bf16[192,512]{1,0:T(8,128)(2,1)S(1)}, bf16[192,512]{1,0:T(8,128)(2,1)S(1)}, u32[]{:S(2)}, u32[]{:S(2)}) collective-permute-start(bf16[192,512]{1,0:T(8,128)(2,1)S(1)} %collective-permute-done.1), channel_id=1, source_target_pairs={{0,24},{4,28},{8,0},{12,4},{16,8},{20,12},{24,16},{28,20},{1,25},{... | collective-permute-start | bytes 589832 | tf_op jit(solution)/shard_map/ppermute | solution.py:23
  28.3 11.0 %collective-permute-start.5 = (bf16[192,512]{1,0:T(8,128)(2,1)S(1)}, bf16[192,512]{1,0:T(8,128)(2,1)S(1)}, u32[]{:S(2)}, u32[]{:S(2)}) collective-permute-start(bf16[192,512]{1,0:T(8,128)(2,1)S(1)} %collective-permute-done.4), channel_id=1, source_target_pairs={{0,24},{4,28},{8,0},{12,4},{16,8},{20,12},{24,16},{28,20},{1,25},{... | collective-permute-start | bytes 589832 | tf_op jit(solution)/shard_map/ppermute | solution.py:23
  52.4 11.5 %collective-permute-start.8 = (bf16[96,2048]{1,0:T(8,128)(2,1)}, bf16[96,2048]{1,0:T(8,128)(2,1)S(1)}, u32[]{:S(2)}, u32[]{:S(2)}) collective-permute-start(bf16[96,2048]{1,0:T(8,128)(2,1)} %fusion.49), channel_id=1, source_target_pairs={{0,2},{1,3},{2,0},{3,1},{4,6},{5,7},{6,4},{7,5},{8,10},{9,11},{10,... | collective-permute-start | bytes 1179656 | tf_op jit(solution)/shard_map/ppermute | solution.py:27
  54.2 12.3 %collective-permute-start.9 = (bf16[48,128]{1,0:T(8,128)(2,1)S(1)}, bf16[48,128]{1,0:T(8,128)(2,1)S(1)}, u32[]{:S(2)}, u32[]{:S(2)}) collective-permute-start(bf16[48,128]{1,0:T(8,128)(2,1)S(1)} %pad_maximum_fusion.13), channel_id=1, source_target_pairs={{0,2},{1,3},{2,0},{3,1},{4,6},{5,7},{6,4},{7,5},{8,10},{9,11},{10,... | collective-permute-start | bytes 36872 | tf_op jit(solution)/shard_map/ppermute | solution.py:27
  67.3 11.0 %collective-permute-start.10 = (bf16[96,2176]{1,0:T(8,128)(2,1)S(1)}, bf16[96,2176]{1,0:T(8,128)(2,1)S(1)}, u32[]{:S(2)}, u32[]{:S(2)}) collective-permute-start(bf16[96,2176]{1,0:T(8,128)(2,1)S(1)} %get-tuple-element.9), channel_id=1, source_target_pairs={{0,4},{4,0},{8,12},{12,8},{16,20},{20,16},{24,28},{28,24},{1,5},{5... | collective-permute-start | bytes 1253384 | tf_op jit(solution)/shard_map/ppermute | solution.py:18
  69.3 14.4 %collective-permute-start.11 = (bf16[96,2176]{1,0:T(8,128)(2,1)S(1)}, bf16[96,2176]{1,0:T(8,128)(2,1)S(1)}, u32[]{:S(2)}, u32[]{:S(2)}) collective-permute-start(bf16[96,2176]{1,0:T(8,128)(2,1)S(1)} %get-tuple-element.9), channel_id=1, source_target_pairs={{0,8},{4,12},{8,16},{12,20},{16,24},{20,28},{24,0},{28,4},{1,9},{5... | collective-permute-start | bytes 1253384 | tf_op jit(solution)/shard_map/ppermute | solution.py:23
  69.9 23.4 %collective-permute-start.14 = (bf16[96,2176]{1,0:T(8,128)(2,1)S(1)}, bf16[96,2176]{1,0:T(8,128)(2,1)S(1)}, u32[]{:S(2)}, u32[]{:S(2)}) collective-permute-start(bf16[96,2176]{1,0:T(8,128)(2,1)S(1)} %get-tuple-element.9), channel_id=1, source_target_pairs={{0,24},{4,28},{8,0},{12,4},{16,8},{20,12},{24,16},{28,20},{1,25},{... | collective-permute-start | bytes 1253384 | tf_op jit(solution)/shard_map/ppermute | solution.py:23
  78.3 18.8 %collective-permute-start.13 = (bf16[48,2176]{1,0:T(8,128)(2,1)S(1)}, bf16[48,2176]{1,0:T(8,128)(2,1)S(1)}, u32[]{:S(2)}, u32[]{:S(2)}) collective-permute-start(bf16[48,2176]{1,0:T(8,128)(2,1)S(1)} %slice.350), channel_id=1, source_target_pairs={{0,8},{4,12},{8,16},{12,20},{16,24},{20,28},{24,0},{28,4},{1,9},{5... | collective-permute-start | bytes 626696 | tf_op jit(solution)/shard_map/ppermute | solution.py:23
  79.0 22.7 %collective-permute-start.16 = (bf16[48,2176]{1,0:T(8,128)(2,1)S(1)}, bf16[48,2176]{1,0:T(8,128)(2,1)S(1)}, u32[]{:S(2)}, u32[]{:S(2)}) collective-permute-start(bf16[48,2176]{1,0:T(8,128)(2,1)S(1)} %slice.350), channel_id=1, source_target_pairs={{0,24},{4,28},{8,0},{12,4},{16,8},{20,12},{24,16},{28,20},{1,25},{... | collective-permute-start | bytes 626696 | tf_op jit(solution)/shard_map/ppermute | solution.py:23
  83.7 19.0 %collective-permute-start.12 = (bf16[48,2176]{1,0:T(8,128)(2,1)S(1)}, bf16[48,2176]{1,0:T(8,128)(2,1)S(1)}, u32[]{:S(2)}, u32[]{:S(2)}) collective-permute-start(bf16[48,2176]{1,0:T(8,128)(2,1)S(1)} %slice.349), channel_id=1, source_target_pairs={{0,4},{4,0},{8,12},{12,8},{16,20},{20,16},{24,28},{28,24},{1,5},{5... | collective-permute-start | bytes 626696 | tf_op jit(solution)/shard_map/ppermute | solution.py:18
  84.0 25.3 %collective-permute-start.17 = (bf16[48,2176]{1,0:T(8,128)(2,1)S(1)}, bf16[48,2176]{1,0:T(8,128)(2,1)S(1)}, u32[]{:S(2)}, u32[]{:S(2)}) collective-permute-start(bf16[48,2176]{1,0:T(8,128)(2,1)S(1)} %slice.349), channel_id=1, source_target_pairs={{0,8},{4,12},{8,16},{12,20},{16,24},{20,28},{24,0},{28,4},{1,9},{5... | collective-permute-start | bytes 626696 | tf_op jit(solution)/shard_map/ppermute | solution.py:23
  93.3 14.6 %collective-permute-start.15 = (bf16[48,2176]{1,0:T(8,128)(2,1)S(1)}, bf16[48,2176]{1,0:T(8,128)(2,1)S(1)}, u32[]{:S(2)}, u32[]{:S(2)}) collective-permute-start(bf16[48,2176]{1,0:T(8,128)(2,1)S(1)} %get-tuple-element.35), channel_id=1, source_target_pairs={{0,4},{4,0},{8,12},{12,8},{16,20},{20,16},{24,28},{28,24},{1,5},{5... | collective-permute-start | bytes 626696 | tf_op jit(solution)/shard_map/ppermute | solution.py:18
  97.1 12.9 %collective-permute-start.18 = (bf16[48,2176]{1,0:T(8,128)(2,1)S(1)}, bf16[48,2176]{1,0:T(8,128)(2,1)S(1)}, u32[]{:S(2)}, u32[]{:S(2)}) collective-permute-start(bf16[48,2176]{1,0:T(8,128)(2,1)S(1)} %get-tuple-element.34), channel_id=1, source_target_pairs={{0,24},{4,28},{8,0},{12,4},{16,8},{20,12},{24,16},{28,20},{1,25},{... | collective-permute-start | bytes 626696 | tf_op jit(solution)/shard_map/ppermute | solution.py:23
  101.7 14.2 %collective-permute-start.20 = (bf16[24,2176]{1,0:T(8,128)(2,1)S(1)}, bf16[24,2176]{1,0:T(8,128)(2,1)S(1)}, u32[]{:S(2)}, u32[]{:S(2)}) collective-permute-start(bf16[24,2176]{1,0:T(8,128)(2,1)S(1)} %slice.353), channel_id=1, source_target_pairs={{0,8},{4,12},{8,16},{12,20},{16,24},{20,28},{24,0},{28,4},{1,9},{5... | collective-permute-start | bytes 313352 | tf_op jit(solution)/shard_map/ppermute | solution.py:23
  102.7 13.8 %collective-permute-start.21 = (bf16[24,2176]{1,0:T(8,128)(2,1)S(1)}, bf16[24,2176]{1,0:T(8,128)(2,1)S(1)}, u32[]{:S(2)}, u32[]{:S(2)}) collective-permute-start(bf16[24,2176]{1,0:T(8,128)(2,1)S(1)} %slice.354), channel_id=1, source_target_pairs={{0,24},{4,28},{8,0},{12,4},{16,8},{20,12},{24,16},{28,20},{1,25},{... | collective-permute-start | bytes 313352 | tf_op jit(solution)/shard_map/ppermute | solution.py:23
  117.2 11.2 %collective-permute-start.22 = (bf16[768,2176]{1,0:T(8,128)(2,1)}, bf16[768,2176]{1,0:T(8,128)(2,1)}, u32[]{:S(2)}, u32[]{:S(2)}) collective-permute-start(bf16[768,2176]{1,0:T(8,128)(2,1)} %constant_dynamic-update-slice_fusion), channel_id=1, source_target_pairs={{0,1},{1,0},{2,3},{3,2},{4,5},{5,4},{6,7},{7,6},{8,9},{9,8},{10,11... | collective-permute-start | bytes 10027016 | tf_op jit(solution)/shard_map/ppermute | solution.py:31
  157.3 14.8 %collective-permute-start.35 = (bf16[192,768]{1,0:T(8,128)(2,1)S(1)}, bf16[192,768]{1,0:T(8,128)(2,1)S(1)}, u32[]{:S(2)}, u32[]{:S(2)}) collective-permute-start(bf16[192,768]{1,0:T(8,128)(2,1)S(1)} %pad_maximum_fusion.6), channel_id=1, source_target_pairs={{0,24},{4,28},{8,0},{12,4},{16,8},{20,12},{24,16},{28,20},{1,25},{... | collective-permute-start | bytes 884744 | tf_op jit(solution)/shard_map/ppermute | solution.py:23
  157.5 14.6 %collective-permute-start.33 = (bf16[192,768]{1,0:T(8,128)(2,1)S(1)}, bf16[192,768]{1,0:T(8,128)(2,1)S(1)}, u32[]{:S(2)}, u32[]{:S(2)}) collective-permute-start(bf16[192,768]{1,0:T(8,128)(2,1)S(1)} %pad_maximum_fusion.5), channel_id=1, source_target_pairs={{0,8},{4,12},{8,16},{12,20},{16,24},{20,28},{24,0},{28,4},{1,9},{5... | collective-permute-start | bytes 884744 | tf_op jit(solution)/shard_map/ppermute | solution.py:23
  159.6 12.7 %collective-permute-start.24 = (bf16[4,2,48,640]{3,2,1,0:T(8,128)(2,1)S(1)}, bf16[4,2,48,640]{3,2,1,0:T(8,128)(2,1)S(1)}, u32[]{:S(2)}, u32[]{:S(2)}) collective-permute-start(bf16[4,2,48,640]{3,2,1,0:T(8,128)(2,1)S(1)} %slice_bitcast_fusion.2), channel_id=1, source_target_pairs={{0,2},{1,3},{2,0},{3,1},{4,6},{5,7},{6,4},{7,5},{8,10},{9,11},{10,... | collective-permute-start | bytes 1474568 | tf_op jit(solution)/shard_map/ppermute | solution.py:27
  161.1 11.8 %collective-permute-start.25 = (bf16[4,2,48,640]{3,2,1,0:T(8,128)(2,1)S(1)}, bf16[4,2,48,640]{3,2,1,0:T(8,128)(2,1)S(1)}, u32[]{:S(2)}, u32[]{:S(2)}) collective-permute-start(bf16[4,2,48,640]{3,2,1,0:T(8,128)(2,1)S(1)} %slice_bitcast_fusion), channel_id=1, source_target_pairs={{0,4},{4,0},{8,12},{12,8},{16,20},{20,16},{24,28},{28,24},{1,5},{5... | collective-permute-start | bytes 1474568 | tf_op jit(solution)/shard_map/ppermute | solution.py:18
  172.3 11.3 %collective-permute-start.36 = (bf16[96,768]{1,0:T(8,128)(2,1)S(1)}, bf16[96,768]{1,0:T(8,128)(2,1)S(1)}, u32[]{:S(2)}, u32[]{:S(2)}) collective-permute-start(bf16[96,768]{1,0:T(8,128)(2,1)S(1)} %slice.391), channel_id=1, source_target_pairs={{0,4},{4,0},{8,12},{12,8},{16,20},{20,16},{24,28},{28,24},{1,5},{5... | collective-permute-start | bytes 442376 | tf_op jit(solution)/shard_map/ppermute | solution.py:18
  183.7 11.5 %collective-permute-start.37 = (bf16[48,768]{1,0:T(8,128)(2,1)S(1)}, bf16[48,768]{1,0:T(8,128)(2,1)S(1)}, u32[]{:S(2)}, u32[]{:S(2)}) collective-permute-start(bf16[48,768]{1,0:T(8,128)(2,1)S(1)} %slice.393), channel_id=1, source_target_pairs={{0,2},{1,3},{2,0},{3,1},{4,6},{5,7},{6,4},{7,5},{8,10},{9,11},{10,... | collective-permute-start | bytes 221192 | tf_op jit(solution)/shard_map/ppermute | solution.py:27
  (22 other events, 311.3 us)

commit v2 on v1

v2 whole, which is shorter than its diff:
```python
import functools
import math

import jax
import jax.numpy as jnp
from jax import lax
from jax.experimental import pallas as pl
from jax.experimental.pallas import tpu as pltpu
from jax.sharding import PartitionSpec as P

HEAD_DIM = 128
F32 = jnp.float32
BF16 = jnp.bfloat16


def over_y(a):
    count = lax.axis_size("seq")
    return lax.ppermute(a, "seq", [(i, i ^ 1) for i in range(count)])


def over_z(a, step):
    count = lax.axis_size("seq")
    return lax.ppermute(a, "seq", [(i, (i + 2 * step) % count) for i in range(count)])


def over_x(a):
    return lax.ppermute(a, "tp", [(i, i ^ 2) for i in range(4)])


def over_core(a):
    return lax.ppermute(a, "tp", [(i, i ^ 1) for i in range(4)])


def add(a, b):
    return (a.astype(F32) + b.astype(F32)).astype(BF16)


def relative_rows(a, x, core):
    blocks = a.reshape((2, 2, a.shape[0] // 4) + a.shape[1:])
    blocks = jnp.where(x == 0, blocks, blocks[::-1])
    blocks = jnp.where(core == 0, blocks, blocks[:, ::-1])
    return jnp.swapaxes(blocks, 0, 1).reshape(a.shape)


def attention_kernel(scale, bases, q_ref, pos_ref, start_ref, *refs):
    kv_refs, out_ref = refs[:-1], refs[-1]
    piece = q_ref.shape[0] // 2
    key_pos, n = [], 0
    for kv in kv_refs:
        rows = kv.shape[0]
        column = lax.broadcasted_iota(jnp.int32, (1, rows), 1)
        if rows == piece:
            key_pos.append(column + bases[n])
            n += 1
        else:
            key_pos.append(
                jnp.where(column < piece, column + bases[n], column + (bases[n + 1] - piece))
            )
            n += 2
    width = q_ref.shape[1]
    for part in range(2):
        rows = pl.ds(part * piece, piece)
        pos, start = pos_ref[rows, :], start_ref[rows, :]
        masks = [(k >= start) & (k <= pos) for k in key_pos]
        for head in range(width // HEAD_DIM):
            lanes = pl.ds(head * HEAD_DIM, HEAD_DIM)
            value_lanes = pl.ds(width + head * HEAD_DIM, HEAD_DIM)
            q = q_ref[rows, lanes]
            scores = [
                jnp.where(
                    mask,
                    lax.dot_general(
                        q, kv[:, lanes], (((1,), (1,)), ((), ())), preferred_element_type=F32
                    )
                    * scale,
                    -1e30,
                )
                for kv, mask in zip(kv_refs, masks)
            ]
            top = functools.reduce(jnp.maximum, [jnp.max(v, axis=1, keepdims=True) for v in scores])
            total, mixed = 0.0, 0.0
            for kv, mask, score in zip(kv_refs, masks, scores):
                weight = jnp.where(mask, jnp.exp(score - top), 0.0)
                total = total + jnp.sum(weight, axis=1, keepdims=True)
                mixed = mixed + jnp.dot(
                    weight.astype(BF16), kv[:, value_lanes], preferred_element_type=F32
                )
            out_ref[rows, lanes] = (mixed / total).astype(BF16)


def attend(q, pos, start, bases, blocks):
    vmem = pl.BlockSpec(memory_space=pltpu.VMEM)
    keys = sum(b.shape[0] for b in blocks)
    return pl.pallas_call(
        functools.partial(attention_kernel, 1.0 / math.sqrt(HEAD_DIM)),
        out_shape=jax.ShapeDtypeStruct(q.shape, BF16),
        in_specs=[pl.BlockSpec(memory_space=pltpu.SMEM)] + [vmem] * (3 + len(blocks)),
        out_specs=vmem,
        compiler_params=pltpu.CompilerParams(vmem_limit_bytes=40 * 1024 * 1024),
        cost_estimate=pl.CostEstimate(
            flops=4 * q.shape[0] * q.shape[1] * keys,
            bytes_accessed=4 * q.size + 4 * keys * q.shape[1],
            transcendentals=q.shape[0] * q.shape[1] // HEAD_DIM * keys,
        ),
    )(bases, q, pos, start, *blocks)


def attention(queries, keys, values, lengths, seq, x, core, w_in, w_down):
    ring = lax.axis_size("seq") // 2
    y, z = seq % 2, seq // 2
    rows, width = queries.shape
    half = width // 2

    def split(a):
        left, right = a[:, :half], a[:, half:]
        return jnp.where(y == 0, left, right), jnp.where(y == 0, right, left)

    (k_own, k_other), (v_own, v_other) = split(keys), split(values)
    own, beside = jnp.concatenate([k_own, v_own], 1), jnp.concatenate([k_other, v_other], 1)
    own, beside, queries, w_in, w_down = lax.optimization_barrier(
        (own, beside, queries, w_in, w_down)
    )
    q_own, q_other = split(relative_rows(queries, x, core))
    beside = over_y(beside)
    blocks, shard = [own, beside], [2 * z + y, 2 * z + 1 - y]
    q = jnp.concatenate([q_own, over_y(q_other)], 0)
    w_in = lax.optimization_barrier(w_in.transpose(0, 2, 1, 3))
    weights = (w_in, over_core(w_in)), (w_down, over_core(w_down))
    for k in range(1, ring // 2 + 1):
        own = over_z(own, 1)
        if k == 1:
            own, beside = lax.optimization_barrier((own, beside))
        beside = over_z(beside, 1)
        blocks += [own, beside]
        shard += [2 * (z - k) + y, 2 * (z - k) + 1 - y]
    bases = jnp.stack(shard).astype(jnp.int32) * rows

    local = relative_rows(jnp.arange(rows, dtype=jnp.int32), x, core)
    pos = jnp.concatenate([seq * rows + local, (seq ^ 1) * rows + local])
    bounds = jnp.cumsum(lengths)
    start = jnp.max(jnp.where(bounds[None, :] <= pos[:, None], bounds[None, :], 0), axis=1)
    blocks, weights = lax.optimization_barrier((blocks, weights))
    out = attend(q, pos[:, None], start[:, None], bases, blocks)
    return out[:rows], over_y(out[rows:]), weights


def expert_kernel(
    count,
    first,
    a,
    b,
    y_a,
    x_b,
    x_aa,
    y_bb,
    in_own,
    in_other,
    down_own,
    down_other,
    a_keep,
    a_send,
    b_keep,
    b_send,
    tokens,
    factors,
    total,
):
    step = pl.program_id(0)
    owned = pl.num_programs(0) // 2
    groups, rows, half = a.shape

    @pl.when(step == 0)
    def _():
        column = lax.broadcasted_iota(jnp.int32, (1, count), 1)
        for g in range(groups):
            quarters = (
                (a.at[g], b.at[g]),
                (x_aa.at[g, 0], x_b.at[g]),
                (y_a.at[g], y_bb.at[g, 0]),
                (x_aa.at[g, 1], y_bb.at[g, 1]),
            )
            for i, (left, right) in enumerate(quarters):
                at = pl.ds((4 * g + i) * rows, rows)
                tokens[at, :half] = left[...]
                tokens[at, half:] = right[:, :half]
                packed = right[:, half:].astype(F32)
                weight = packed[:, :count] + packed[:, count : 2 * count]
                for e in range(factors.shape[0]):
                    chosen = jnp.where(column == first[0] + e, weight, 0.0)
                    factor = jnp.sum(chosen, axis=1, keepdims=True)
                    factors[e, at, :] = jnp.broadcast_to(factor, (rows, factors.shape[2]))

    def expert(w_in, w_down):
        gate = jnp.dot(tokens[...], w_in[0, 0], preferred_element_type=F32)
        up = jnp.dot(tokens[...], w_in[0, 1], preferred_element_type=F32)
        factor = factors[lax.rem(step, owned)][:, :1]
        hidden = jnp.where(factor > 0, gate / (1.0 + jnp.exp(-gate)) * up * factor, 0.0)
        return jnp.dot(hidden.astype(BF16), w_down[0], preferred_element_type=F32)

    @pl.when(step == 0)
    def _():
        total[...] = expert(in_own, down_own)

    @pl.when((step > 0) & (step < owned))
    def _():
        total[...] += expert(in_own, down_own)

    @pl.when(step >= owned)
    def _():
        total[...] += expert(in_other, down_other)

    @pl.when(step == 2 * owned - 1)
    def _():
        for g in range(groups):
            for i in range(4):
                at = pl.ds((4 * g + i) * rows, rows)
                y, x = divmod(i, 2)
                (a_send if x else a_keep)[g, y] = total[at, :half].astype(BF16)
                (b_send if y else b_keep)[g, x] = total[at, half:].astype(BF16)


def experts(first, count, pieces, weights):
    (in_own, in_other), (down_own, down_other) = weights
    groups, rows, half = pieces[0].shape
    owned, _, width, inner = in_own.shape
    n = groups * 4 * rows

    def whole(a):
        return pl.BlockSpec(a.shape, lambda i, zeros=(0,) * a.ndim: zeros)

    def early(i):
        return jnp.minimum(i, owned - 1)

    def late(i):
        return jnp.maximum(i - owned, 0)

    out = jax.ShapeDtypeStruct((groups, 2, rows, half), BF16)
    in_block, down_block = (1, 2, width, inner), (1, inner, width)
    return pl.pallas_call(
        functools.partial(expert_kernel, count),
        grid=(2 * owned,),
        out_shape=[out] * 4,
        in_specs=[pl.BlockSpec(memory_space=pltpu.SMEM)]
        + [whole(a) for a in pieces]
        + [
            pl.BlockSpec(in_block, lambda i: (early(i), 0, 0, 0)),
            pl.BlockSpec(in_block, lambda i: (late(i), 0, 0, 0)),
            pl.BlockSpec(down_block, lambda i: (early(i), 0, 0)),
            pl.BlockSpec(down_block, lambda i: (late(i), 0, 0)),
        ],
        out_specs=[whole(out)] * 4,
        scratch_shapes=[
            pltpu.VMEM((n, width), BF16),
            pltpu.VMEM((owned, n, 128), F32),
            pltpu.VMEM((n, width), F32),
        ],
        compiler_params=pltpu.CompilerParams(vmem_limit_bytes=40 * 1024 * 1024),
        cost_estimate=pl.CostEstimate(
            flops=12 * n * owned * width * inner,
            bytes_accessed=12 * owned * width * inner + 4 * n * width,
            transcendentals=2 * n * owned * inner,
        ),
    )(first, *pieces, in_own, in_other, down_own, down_other)


def plane_first(unit):
    half = (unit.shape[2] - 128) // 2
    a, b = unit[..., :half], unit[..., half:]
    return a, b, over_y(a), over_x(b)


def plane_second(a, b, y_a, x_b):
    return a, b, y_a, x_b, over_x(jnp.stack([a, y_a], 1)), over_y(jnp.stack([b, x_b], 1))


def gather_tokens(unit, use):
    half = lax.axis_size("seq") // 4
    middle = (unit.shape[1] - 128) // 2
    own_first = plane_first(unit[None])
    up, down, pairs = unit, unit, []
    for _ in range(1, half):
        up, down = over_z(up, 1), over_z(down, -1)
        pairs.append(jnp.stack([up, down]))
    far_a, far_b = over_z(up[:, :middle], 1)[None], over_z(down[:, middle:], -1)[None]
    used = use(plane_second(*own_first))
    done = [used]
    for pair in pairs:
        first = plane_first(pair)
        first, done[-1] = lax.optimization_barrier((first, done[-1]))
        done.append(use(plane_second(*first)))
    first = far_a, far_b, over_y(far_a), over_x(far_b)
    first, done[-1] = lax.optimization_barrier((first, done[-1]))
    return done[0], use(plane_second(*first)), done[1:]


def plane_scatter(a_keep, a_send, b_keep, b_send):
    a = add(a_keep, over_x(a_send))
    b = add(b_keep, over_y(b_send))
    return add(a[:, 0], over_y(a[:, 1])), add(b[:, 0], over_x(b[:, 1]))


def ring_scatter(own, far, pairs):
    (far_a, far_b) = far
    plus, minus = over_z(far_a[0], 1), over_z(far_b[0], -1)
    last = len(pairs) - 1
    for k in reversed(range(last + 1)):
        a, b = pairs[k]
        if k == last:
            high = jnp.concatenate([add(a[1], plus), b[1]], 1)
            low = jnp.concatenate([a[0], add(b[0], minus)], 1)
        else:
            high = add(jnp.concatenate([a[1], b[1]], 1), plus)
            low = add(jnp.concatenate([a[0], b[0]], 1), minus)
        plus, minus = over_z(high, 1), over_z(low, -1)
    own = jnp.concatenate([own[0][0], own[1][0]], 1)
    return (own.astype(F32) + plus.astype(F32) + minus.astype(F32)).astype(BF16)


def shards(
    queries, keys, values, lengths, resid, w_out, moe_gain, routes, gates, w_gate_up, w_down
):
    seq, tp = lax.axis_index("seq"), lax.axis_index("tp")
    x, core, y = tp // 2, tp % 2, seq % 2
    rows = resid.shape[0]
    owned = w_gate_up.shape[0]
    count = owned * lax.axis_size("seq")
    half = w_out.shape[0] // 2

    own, other, weights = attention(
        queries, keys, values, lengths, seq, x, core, w_gate_up, w_down
    )
    w_own = jnp.where(y == 0, w_out[:half], w_out[half:])
    w_other = jnp.where(y == 0, w_out[half:], w_out[:half])
    projected = jnp.dot(own, w_own, preferred_element_type=F32)
    projected = projected + jnp.dot(other, w_other, preferred_element_type=F32)

    matches = routes[:, :, None] == jnp.arange(count, dtype=jnp.int32)[None, None, :]
    weight = jnp.sum(jnp.where(matches, gates[:, :, None], 0.0), axis=1)
    high = weight.astype(BF16)
    low = (weight - high.astype(F32)).astype(BF16)
    pad = -(-2 * count // 128) * 128 - 2 * count
    packed = jnp.concatenate([high, low, jnp.zeros((rows, pad), BF16)], 1)

    received = over_core(projected[2 * rows :].astype(BF16))
    partial = projected[: 2 * rows] + received.astype(F32)
    arrived = over_x(partial[rows:].astype(BF16))
    attended = (resid.astype(F32) + partial[:rows] + arrived.astype(F32)).astype(BF16)
    widened = attended.astype(F32)
    meansq = jnp.mean(widened * widened, axis=1, keepdims=True)
    normed = (widened * lax.rsqrt(meansq + 1e-05) * moe_gain[None, :]).astype(BF16)

    first = (owned * seq).astype(jnp.int32).reshape(1)
    own, far, pairs = gather_tokens(
        jnp.concatenate([normed, packed], 1),
        lambda pieces: experts(first, count, pieces, weights),
    )
    far = plane_scatter(*far)
    pairs = [plane_scatter(*pair) for pair in pairs]
    return attended, ring_scatter(plane_scatter(*own), far, pairs)


def solution(mesh):
    return jax.shard_map(
        shards,
        mesh=mesh,
        in_specs=(
            P("seq", "tp"),
            P("seq", "tp"),
            P("seq", "tp"),
            P(),
            P(("seq", "tp"), None),
            P("tp", None),
            P(),
            P(("seq", "tp"), None),
            P(("seq", "tp"), None),
            P("seq", None, None, "tp"),
            P("seq", "tp", None),
        ),
        out_specs=(P(("seq", "tp"), None), P(("seq", "tp"), None)),
        check_vma=False,
    )
```

time: 199 us -> 151 us (0.76)
  waiting for transfers between devices: 94.1 us -> 62 us
  Pallas kernels: 3.09 us -> 27 us
  matrix products: 17.7 us -> 0.92 us
  local copies, waits for them, and re-layouts: 22.8 us -> 7.14 us
  other arithmetic: 12.1 us -> 4.84 us
    ppermute x20 -> x12, waiting for transfers between devices: 61.5 us -> 26.9 us  [over_z(): lax.ppermute(a, 'seq', [(i, (i + 2 * step) % count) for i in range(count)])]
    pallas_call x0 -> x3, Pallas kernels: none -> 23.7 us  [experts(): pl.pallas_call(functools.partial(expert_kernel, count), grid=(2 * owned,)...]
    unnamed x28 -> x20, local copies, waits for them, and re-layouts: 19.2 us -> 1.2 us
    ppermute x20 -> x12, starting transfers between devices: 32.3 us -> 14.9 us  [over_z(): lax.ppermute(a, 'seq', [(i, (i + 2 * step) % count) for i in range(count)])]
    dot_general x4 -> x0, matrix products: 15.3 us -> none  [the longest x2 11.7 us: experts(): projections = jnp.dot(tokens[:, :width], w_in, preferred_element_type=F32)]
    ppermute x5 -> x13, starting transfers between devices: 5.28 us -> 15.5 us  [over_x(): return lax.ppermute(a, 'tp', [(i, i ^ 2) for i in range(4)])]
    ppermute x10 -> x15, starting transfers between devices: 9.38 us -> 16.3 us  [over_y(): return lax.ppermute(a, 'seq', [(i, i ^ 1) for i in range(count)])]
    ppermute x5 -> x13, waiting for transfers between devices: 10.3 us -> 16.7 us  [over_x(): return lax.ppermute(a, 'tp', [(i, i ^ 2) for i in range(4)])]
  transfers between devices with their start and end apart: 38 -> 43, of which waited for: 21 -> 24; matrix products, arithmetic and copies ran while one was open for 17% -> 2% of each run, Pallas kernels for 0% -> 16%
where the time goes in v2:
time: 151 us; the launch traced here: 150 us
  waiting for transfers between devices  62 us (41%)
  starting transfers between devices  47.3 us (31%)
  Pallas kernels  27 us (18%)
  local copies, waits for them, and re-layouts  7.14 us (5%)
  other arithmetic  4.84 us (3%)
    ppermute x12, waiting for transfers between devices, over_z(): lax.ppermute(a, 'seq', [(i, (i + 2 * step) % count) for i in range(count)])  26.9 us
    pallas_call x3, Pallas kernels, experts(): pl.pallas_call(functools.partial(expert_kernel, count), grid=(2 * owned,)...  23.7 us
    ppermute x15, waiting for transfers between devices, over_y(): return lax.ppermute(a, 'seq', [(i, i ^ 1) for i in range(count)])  16.8 us
    ppermute x13, waiting for transfers between devices, over_x(): return lax.ppermute(a, 'tp', [(i, i ^ 2) for i in range(4)])  16.7 us
    ppermute x15, starting transfers between devices, over_y(): return lax.ppermute(a, 'seq', [(i, i ^ 1) for i in range(count)])  16.3 us
    ppermute x13, starting transfers between devices, over_x(): return lax.ppermute(a, 'tp', [(i, i ^ 2) for i in range(4)])  15.5 us
    ppermute x12, starting transfers between devices, over_z(): lax.ppermute(a, 'seq', [(i, (i + 2 * step) % count) for i in range(count)])  14.9 us
    optimization_barrier x1, local copies, waits for them, and re-layouts, attention(): lax.optimization_barrier((own, beside, queries, w_in, w_down))  4.84 us
  transfers between devices with their start and end apart: 43, of which 24 were waited for; matrix products, arithmetic and copies ran while one was open for 2% of the time, Pallas kernels for 16%

profile of v2, /device:TPU:0, one launch (start us, length us, event | category | flops | bytes accessed | tf_op | source)
XLA Modules:
  0.0 150.4 jit_solution(9719822291182893103)
XLA Ops:
  1.8 4.8 %copy.67 = bf16[2,2048,2,256]{3,1,2,0:T(8,128)(2,1)} copy(bf16[2,2048,2,256]{3,2,1,0:T(2,128)(2,1)} %param.20) | data formatting | bytes 8388608 | tf_op jit(solution)/shard_map/optimization_barrier | solution.py:120
  7.3 3.0 %collective-permute-start = (bf16[192,256]{1,0:T(8,128)(2,1)S(1)}, bf16[192,256]{1,0:T(8,128)(2,1)S(1)}, u32[]{:S(2)}, u32[]{:S(2)}) collective-permute-start(bf16[192,256]{1,0:T(8,128)(2,1)S(1)} %get-tuple-element.99), channel_id=1, source_target_pairs={{0,4},{4,0},{8,12},{12,8},{16,20},{20,16},{24,28},{28,24},{1,5},{5... | collective-permute-start | bytes 294920 | tf_op jit(solution)/shard_map/ppermute | solution.py:18
  10.4 2.0 %collective-permute-start.2 = (bf16[192,512]{1,0:T(8,128)(2,1)S(1)}, bf16[192,512]{1,0:T(8,128)(2,1)S(1)}, u32[]{:S(2)}, u32[]{:S(2)}) collective-permute-start(bf16[192,512]{1,0:T(8,128)(2,1)S(1)} %pad_maximum_fusion.6.refs_0_), channel_id=1, source_target_pairs={{0,8},{4,12},{8,16},{12,20},{16,24},{20,28},{24,0},{28,4},{1,9},{5... | collective-permute-start | bytes 589832 | tf_op jit(solution)/shard_map/ppermute | solution.py:23
  13.1 4.4 %collective-permute-done.1.refs_1_ = bf16[192,512]{1,0:T(8,128)(2,1)S(1)} collective-permute-done((bf16[192,512]{1,0:T(8,128)(2,1)S(1)}, bf16[192,512]{1,0:T(8,128)(2,1)S(1)}, u32[]{:S(2)}, u32[]{:S(2)}) %collective-permute-start.1) | collective-permute-done | bytes 196640 | tf_op jit(solution)/shard_map/ppermute | solution.py:18
  20.9 7.6 %collective-permute-done.3.refs_3_ = bf16[192,512]{1,0:T(8,128)(2,1)S(1)} collective-permute-done((bf16[192,512]{1,0:T(8,128)(2,1)S(1)}, bf16[192,512]{1,0:T(8,128)(2,1)S(1)}, u32[]{:S(2)}, u32[]{:S(2)}) %collective-permute-start.3) | collective-permute-done | bytes 196640 | tf_op jit(solution)/shard_map/ppermute | solution.py:23
  28.7 3.9 %collective-permute-done.4.refs_4_ = bf16[192,512]{1,0:T(8,128)(2,1)S(1)} collective-permute-done((bf16[192,512]{1,0:T(8,128)(2,1)S(1)}, bf16[192,512]{1,0:T(8,128)(2,1)S(1)}, u32[]{:S(2)}, u32[]{:S(2)}) %collective-permute-start.4) | collective-permute-done | bytes 196640 | tf_op jit(solution)/shard_map/ppermute | solution.py:23
  32.6 3.3 %collective-permute-done.5.refs_5_ = bf16[192,512]{1,0:T(8,128)(2,1)S(1)} collective-permute-done((bf16[192,512]{1,0:T(8,128)(2,1)S(1)}, bf16[192,512]{1,0:T(8,128)(2,1)S(1)}, u32[]{:S(2)}, u32[]{:S(2)}) %collective-permute-start.5) | collective-permute-done | bytes 196640 | tf_op jit(solution)/shard_map/ppermute | solution.py:23
  36.0 3.3 %shard_map.122 = bf16[384,256]{1,0:T(8,128)(2,1)S(1)} custom-call(s32[6]{0:T(128)S(1)} %broadcast_multiply_fusion.bases, bf16[384,256]{1,0:T(8,128)(2,1)S(1)} %pad_maximum_fusion.8.q_ref, s32[384,1]{1,0:T(8,128)S(1)} %broadcast_in_dim.57.pos_ref, s32[384,1]{1,0:T(8,128)S(1)} %broadcast_in_dim.58.start_ref, bf16[192,512]{1,0:T(8,128)(2,1)S(1)} %pad_maximum_fusion.6.refs_0_, ...), custom_call_target="tpu_custom_call" | custom-call | flops 452984832 | bytes 1572864 | tf_op jit(solution)/shard_map/pallas_call | solution.py:94
  40.6 3.3 %collective-permute-done.8 = bf16[192,256]{1,0:T(8,128)(2,1)S(1)} collective-permute-done((bf16[192,256]{1,0:T(8,128)(2,1)S(1)}, bf16[192,256]{1,0:T(8,128)(2,1)S(1)}, u32[]{:S(2)}, u32[]{:S(2)}) %collective-permute-start.8) | collective-permute-done | bytes 98336 | tf_op jit(solution)/shard_map/ppermute | solution.py:18
  50.5 5.7 %collective-permute-done.10 = bf16[48,2048]{1,0:T(8,128)(2,1)S(1)} collective-permute-done((bf16[48,2048]{1,0:T(8,128)(2,1)S(1)}, bf16[48,2048]{1,0:T(8,128)(2,1)S(1)}, u32[]{:S(2)}, u32[]{:S(2)}) %collective-permute-start.10) | collective-permute-done | bytes 196640 | tf_op jit(solution)/shard_map/ppermute | solution.py:27
  56.7 2.0 %collective-permute-start.11 = (bf16[48,2176]{1,0:T(8,128)(2,1)S(1)}, bf16[48,2176]{1,0:T(8,128)(2,1)S(1)}, u32[]{:S(2)}, u32[]{:S(2)}) collective-permute-start(bf16[48,2176]{1,0:T(8,128)(2,1)S(1)} %concatenate.28), channel_id=1, source_target_pairs={{0,8},{4,12},{8,16},{12,20},{16,24},{20,28},{24,0},{28,4},{1,9},{5... | collective-permute-start | bytes 626696 | tf_op jit(solution)/shard_map/ppermute | solution.py:23
  66.4 2.3 %collective-permute-done.12 = bf16[48,2176]{1,0:T(8,128)(2,1)S(1)} collective-permute-done((bf16[48,2176]{1,0:T(8,128)(2,1)S(1)}, bf16[48,2176]{1,0:T(8,128)(2,1)S(1)}, u32[]{:S(2)}, u32[]{:S(2)}) %collective-permute-start.12) | collective-permute-done | bytes 208928 | tf_op jit(solution)/shard_map/ppermute | solution.py:23
  68.8 2.2 %collective-permute-start.23 = (bf16[48,1024]{1,0:T(8,128)(2,1)S(1)}, bf16[48,1024]{1,0:T(8,128)(2,1)S(1)}, u32[]{:S(2)}, u32[]{:S(2)}) collective-permute-start(bf16[48,1024]{1,0:T(8,128)(2,1)S(1)} %slice.162), channel_id=1, source_target_pairs={{0,8},{4,12},{8,16},{12,20},{16,24},{20,28},{24,0},{28,4},{1,9},{5... | collective-permute-start | bytes 294920 | tf_op jit(solution)/shard_map/ppermute | solution.py:23
  78.3 7.3 %shard_map.123 = (bf16[1,2,48,1024]{3,2,1,0:T(8,128)(2,1)S(1)}, bf16[1,2,48,1024]{3,2,1,0:T(8,128)(2,1)S(1)}, bf16[1,2,48,1024]{3,2,1,0:T(8,128)(2,1)S(1)}, bf16[1,2,48,1024]{3,2,1,0:T(8,128)(2,1)S(1)}) custom-call(s32[1]{0:T(128)} %bitcast.17.first, bf16[1,48,1024]{2,1,0:T(8,128)(2,1)S(1)} %get-tuple-element.97.a, ...), custom_call_target="tpu_custom_call" | custom-call | flops 2415919104 | bytes 14155776 | tf_op jit(solution)/shard_map/pallas_call | solution.py:239
  88.4 3.7 %collective-permute-done.19 = bf16[1,2,48,1024]{3,2,1,0:T(8,128)(2,1)S(1)} collective-permute-done((bf16[1,2,48,1024]{3,2,1,0:T(8,128)(2,1)S(1)}, bf16[1,2,48,1024]{3,2,1,0:T(8,128)(2,1)S(1)}, u32[]{:S(2)}, u32[]{:S(2)}) %collective-permute-start.19) | collective-permute-done | bytes 196640 | tf_op jit(solution)/shard_map/ppermute | solution.py:27
  94.8 2.5 %collective-permute-done.27 = bf16[2,2,48,1024]{3,2,0,1:T(8,128)(2,1)S(1)} collective-permute-done((bf16[2,2,48,1024]{3,2,0,1:T(8,128)(2,1)S(1)}, bf16[2,2,48,1024]{3,2,0,1:T(8,128)(2,1)S(1)}, u32[]{:S(2)}, u32[]{:S(2)}) %collective-permute-start.27) | collective-permute-done | bytes 393248 | tf_op jit(solution)/shard_map/ppermute | solution.py:27
  98.0 2.8 %collective-permute-done.28 = bf16[2,2,48,1152]{3,2,0,1:T(8,128)(2,1)S(1)} collective-permute-done((bf16[2,2,48,1152]{3,2,0,1:T(8,128)(2,1)S(1)}, bf16[2,2,48,1152]{3,2,0,1:T(8,128)(2,1)S(1)}, u32[]{:S(2)}, u32[]{:S(2)}) %collective-permute-start.28) | collective-permute-done | bytes 442400 | tf_op jit(solution)/shard_map/ppermute | solution.py:18
  100.8 9.1 %shard_map.124 = (bf16[2,2,48,1024]{3,2,1,0:T(8,128)(2,1)S(1)}, bf16[2,2,48,1024]{3,2,1,0:T(8,128)(2,1)S(1)}, bf16[2,2,48,1024]{3,2,1,0:T(8,128)(2,1)S(1)}, bf16[2,2,48,1024]{3,2,1,0:T(8,128)(2,1)S(1)}) custom-call(s32[1]{0:T(128)} %bitcast.17.first, bf16[2,48,1024]{2,1,0:T(8,128)(2,1)S(1)} %pad_maximum_fusion.5.a, ...), custom_call_target="tpu_custom_call" | custom-call | flops 4831838208 | bytes 15728640 | tf_op jit(solution)/shard_map/pallas_call | solution.py:239
  116.7 7.3 %shard_map.125 = (bf16[1,2,48,1024]{3,2,1,0:T(8,128)(2,1)S(1)}, bf16[1,2,48,1024]{3,2,1,0:T(8,128)(2,1)S(1)}, bf16[1,2,48,1024]{3,2,1,0:T(8,128)(2,1)S(1)}, bf16[1,2,48,1024]{3,2,1,0:T(8,128)(2,1)S(1)}) custom-call(s32[1]{0:T(128)} %bitcast.17.first, bf16[1,48,1024]{2,1,0:T(8,128)(2,1)S(1)} %bitcast.113, bf16[1,48,1152]{2,1,0:T(8,128)(2,1)S(1)} %bitcast.108, ...), custom_call_target="tpu_custom_call" | custom-call | flops 2415919104 | bytes 14155776 | tf_op jit(solution)/shard_map/pallas_call | solution.py:239
  132.2 2.4 %collective-permute-done.34 = bf16[1,48,1024]{2,1,0:T(8,128)(2,1)S(1)} collective-permute-done((bf16[1,48,1024]{2,1,0:T(8,128)(2,1)S(1)}, bf16[1,48,1024]{2,1,0:T(8,128)(2,1)S(1)}, u32[]{:S(2)}, u32[]{:S(2)}) %collective-permute-start.34) | collective-permute-done | bytes 98336 | tf_op jit(solution)/shard_map/ppermute | solution.py:18
  136.0 2.6 %collective-permute-start.41 = (bf16[48,1024]{1,0:T(8,128)(2,1)S(1)}, bf16[48,1024]{1,0:T(8,128)(2,1)S(1)}, u32[]{:S(2)}, u32[]{:S(2)}) collective-permute-start(bf16[48,1024]{1,0:T(8,128)(2,1)S(1)} %fusion.25), channel_id=1, source_target_pairs={{0,24},{4,28},{8,0},{12,4},{16,8},{20,12},{24,16},{28,20},{1,25},{... | collective-permute-start | bytes 294920 | tf_op jit(solution)/shard_map/ppermute | solution.py:23
  138.7 3.0 %collective-permute-done.35 = bf16[48,1024]{1,0:T(8,128)(2,1)S(1)} collective-permute-done((bf16[48,1024]{1,0:T(8,128)(2,1)S(1)}, bf16[48,1024]{1,0:T(8,128)(2,1)S(1)}, u32[]{:S(2)}, u32[]{:S(2)}) %collective-permute-start.35) | collective-permute-done | bytes 98336 | tf_op jit(solution)/shard_map/ppermute | solution.py:23
  141.9 3.9 %collective-permute-start.42 = (bf16[48,2048]{1,0:T(8,128)(2,1)S(1)}, bf16[48,2048]{1,0:T(8,128)(2,1)S(1)}, u32[]{:S(2)}, u32[]{:S(2)}) collective-permute-start(bf16[48,2048]{1,0:T(8,128)(2,1)S(1)} %pad_maximum_fusion.12), channel_id=1, source_target_pairs={{0,24},{4,28},{8,0},{12,4},{16,8},{20,12},{24,16},{28,20},{1,25},{... | collective-permute-start | bytes 589832 | tf_op jit(solution)/shard_map/ppermute | solution.py:23
  145.7 3.7 %collective-permute-done.38 = bf16[48,2048]{1,0:T(8,128)(2,1)S(1)} collective-permute-done((bf16[48,2048]{1,0:T(8,128)(2,1)S(1)}, bf16[48,2048]{1,0:T(8,128)(2,1)S(1)}, u32[]{:S(2)}, u32[]{:S(2)}) %collective-permute-start.38) | collective-permute-done | bytes 196640 | tf_op jit(solution)/shard_map/ppermute | solution.py:23
  (165 shorter events, 53.0 us)
Async XLA Ops:
  6.6 29.3 %collective-permute-start.6 = (bf16[2,2,2048,256]{3,2,1,0:T(8,128)(2,1)}, bf16[2,2,2048,256]{3,2,1,0:T(8,128)(2,1)}, u32[]{:S(2)}, u32[]{:S(2)}) collective-permute-start(bf16[2,2,2048,256]{3,2,1,0:T(8,128)(2,1)} %bitcast.103.in_own), channel_id=1, source_target_pairs={{0,1},{1,0},{2,3},{3,2},{4,5},{5,4},{6,7},{7,6},{8,9},{9,8},{10,11... | collective-permute-start | bytes 12582920 | tf_op jit(solution)/shard_map/ppermute | solution.py:31
  7.1 28.9 %collective-permute-start.7 = (bf16[2,256,2048]{2,1,0:T(8,128)(2,1)S(1)}, bf16[2,256,2048]{2,1,0:T(8,128)(2,1)}, u32[]{:S(2)}, u32[]{:S(2)}) collective-permute-start(bf16[2,256,2048]{2,1,0:T(8,128)(2,1)S(1)} %copy-done), channel_id=1, source_target_pairs={{0,1},{1,0},{2,3},{3,2},{4,5},{5,4},{6,7},{7,6},{8,9},{9,8},{10,11... | collective-permute-start | bytes 6291464 | tf_op jit(solution)/shard_map/ppermute | solution.py:31
  7.3 21.4 %collective-permute-start = (bf16[192,256]{1,0:T(8,128)(2,1)S(1)}, bf16[192,256]{1,0:T(8,128)(2,1)S(1)}, u32[]{:S(2)}, u32[]{:S(2)}) collective-permute-start(bf16[192,256]{1,0:T(8,128)(2,1)S(1)} %get-tuple-element.99), channel_id=1, source_target_pairs={{0,4},{4,0},{8,12},{12,8},{16,20},{20,16},{24,28},{28,24},{1,5},{5... | collective-permute-start | bytes 294920 | tf_op jit(solution)/shard_map/ppermute | solution.py:18
  10.4 8.5 %collective-permute-start.2 = (bf16[192,512]{1,0:T(8,128)(2,1)S(1)}, bf16[192,512]{1,0:T(8,128)(2,1)S(1)}, u32[]{:S(2)}, u32[]{:S(2)}) collective-permute-start(bf16[192,512]{1,0:T(8,128)(2,1)S(1)} %pad_maximum_fusion.6.refs_0_), channel_id=1, source_target_pairs={{0,8},{4,12},{8,16},{12,20},{16,24},{20,28},{24,0},{28,4},{1,9},{5... | collective-permute-start | bytes 589832 | tf_op jit(solution)/shard_map/ppermute | solution.py:23
  18.9 9.6 %collective-permute-start.3 = (bf16[192,512]{1,0:T(8,128)(2,1)S(1)}, bf16[192,512]{1,0:T(8,128)(2,1)S(1)}, u32[]{:S(2)}, u32[]{:S(2)}) collective-permute-start(bf16[192,512]{1,0:T(8,128)(2,1)S(1)} %collective-permute-done.1.refs_1_), channel_id=1, source_target_pairs={{0,8},{4,12},{8,16},{12,20},{16,24},{20,28},{24,0},{28,4},{1,9},{5... | collective-permute-start | bytes 589832 | tf_op jit(solution)/shard_map/ppermute | solution.py:23
  19.3 13.3 %collective-permute-start.4 = (bf16[192,512]{1,0:T(8,128)(2,1)S(1)}, bf16[192,512]{1,0:T(8,128)(2,1)S(1)}, u32[]{:S(2)}, u32[]{:S(2)}) collective-permute-start(bf16[192,512]{1,0:T(8,128)(2,1)S(1)} %collective-permute-done.2.refs_2_), channel_id=1, source_target_pairs={{0,8},{4,12},{8,16},{12,20},{16,24},{20,28},{24,0},{28,4},{1,9},{5... | collective-permute-start | bytes 589832 | tf_op jit(solution)/shard_map/ppermute | solution.py:23
  56.7 12.0 %collective-permute-start.12 = (bf16[48,2176]{1,0:T(8,128)(2,1)S(1)}, bf16[48,2176]{1,0:T(8,128)(2,1)S(1)}, u32[]{:S(2)}, u32[]{:S(2)}) collective-permute-start(bf16[48,2176]{1,0:T(8,128)(2,1)S(1)} %concatenate.28), channel_id=1, source_target_pairs={{0,24},{4,28},{8,0},{12,4},{16,8},{20,12},{24,16},{28,20},{1,25},{... | collective-permute-start | bytes 626696 | tf_op jit(solution)/shard_map/ppermute | solution.py:23
  56.7 12.0 %collective-permute-start.11 = (bf16[48,2176]{1,0:T(8,128)(2,1)S(1)}, bf16[48,2176]{1,0:T(8,128)(2,1)S(1)}, u32[]{:S(2)}, u32[]{:S(2)}) collective-permute-start(bf16[48,2176]{1,0:T(8,128)(2,1)S(1)} %concatenate.28), channel_id=1, source_target_pairs={{0,8},{4,12},{8,16},{12,20},{16,24},{20,28},{24,0},{28,4},{1,9},{5... | collective-permute-start | bytes 626696 | tf_op jit(solution)/shard_map/ppermute | solution.py:23
  63.5 9.0 %collective-permute-start.17 = (bf16[1,2,48,1024]{3,2,1,0:T(8,128)(2,1)S(1)}, bf16[1,2,48,1024]{3,2,1,0:T(8,128)(2,1)S(1)}, u32[]{:S(2)}, u32[]{:S(2)}) collective-permute-start(bf16[1,2,48,1024]{3,2,1,0:T(8,128)(2,1)S(1)} %pad_maximum_fusion.9), channel_id=1, source_target_pairs={{0,2},{1,3},{2,0},{3,1},{4,6},{5,7},{6,4},{7,5},{8,10},{9,11},{10,... | collective-permute-start | bytes 589832 | tf_op jit(solution)/shard_map/ppermute | solution.py:27
  65.9 12.4 %collective-permute-start.18 = (bf16[1,2,48,1152]{3,2,1,0:T(8,128)(2,1)S(1)}, bf16[1,2,48,1152]{3,2,1,0:T(8,128)(2,1)S(1)}, u32[]{:S(2)}, u32[]{:S(2)}) collective-permute-start(bf16[1,2,48,1152]{3,2,1,0:T(8,128)(2,1)S(1)} %pad_maximum_fusion.3), channel_id=1, source_target_pairs={{0,4},{4,0},{8,12},{12,8},{16,20},{20,16},{24,28},{28,24},{1,5},{5... | collective-permute-start | bytes 663560 | tf_op jit(solution)/shard_map/ppermute | solution.py:18
  68.7 8.1 %collective-permute-start.24 = (bf16[48,1152]{1,0:T(8,128)(2,1)S(1)}, bf16[48,1152]{1,0:T(8,128)(2,1)S(1)}, u32[]{:S(2)}, u32[]{:S(2)}) collective-permute-start(bf16[48,1152]{1,0:T(8,128)(2,1)S(1)} %slice.163), channel_id=1, source_target_pairs={{0,24},{4,28},{8,0},{12,4},{16,8},{20,12},{24,16},{28,20},{1,25},{... | collective-permute-start | bytes 331784 | tf_op jit(solution)/shard_map/ppermute | solution.py:23
  71.1 14.5 %collective-permute-start.13 = (bf16[2,48,1024]{2,1,0:T(8,128)(2,1)S(1)}, bf16[2,48,1024]{2,1,0:T(8,128)(2,1)S(1)}, u32[]{:S(2)}, u32[]{:S(2)}) collective-permute-start(bf16[2,48,1024]{2,1,0:T(8,128)(2,1)S(1)} %pad_maximum_fusion.5.a), channel_id=1, source_target_pairs={{0,4},{4,0},{8,12},{12,8},{16,20},{20,16},{24,28},{28,24},{1,5},{5... | collective-permute-start | bytes 589832 | tf_op jit(solution)/shard_map/ppermute | solution.py:18
  72.5 13.1 %collective-permute-start.14 = (bf16[2,48,1152]{2,1,0:T(8,128)(2,1)S(1)}, bf16[2,48,1152]{2,1,0:T(8,128)(2,1)S(1)}, u32[]{:S(2)}, u32[]{:S(2)}) collective-permute-start(bf16[2,48,1152]{2,1,0:T(8,128)(2,1)S(1)} %pad_maximum_fusion.2.b), channel_id=1, source_target_pairs={{0,2},{1,3},{2,0},{3,1},{4,6},{5,7},{6,4},{7,5},{8,10},{9,11},{10,... | collective-permute-start | bytes 663560 | tf_op jit(solution)/shard_map/ppermute | solution.py:27
  75.4 34.5 %collective-permute-start.25 = (bf16[1,48,1024]{2,1,0:T(8,128)(2,1)S(1)}, bf16[1,48,1024]{2,1,0:T(8,128)(2,1)S(1)}, u32[]{:S(2)}, u32[]{:S(2)}) collective-permute-start(bf16[1,48,1024]{2,1,0:T(8,128)(2,1)S(1)} %bitcast.111), channel_id=1, source_target_pairs={{0,4},{4,0},{8,12},{12,8},{16,20},{20,16},{24,28},{28,24},{1,5},{5... | collective-permute-start | bytes 294920 | tf_op jit(solution)/shard_map/ppermute | solution.py:18
  76.8 33.1 %collective-permute-start.26 = (bf16[1,48,1152]{2,1,0:T(8,128)(2,1)S(1)}, bf16[1,48,1152]{2,1,0:T(8,128)(2,1)S(1)}, u32[]{:S(2)}, u32[]{:S(2)}) collective-permute-start(bf16[1,48,1152]{2,1,0:T(8,128)(2,1)S(1)} %bitcast.106), channel_id=1, source_target_pairs={{0,2},{1,3},{2,0},{3,1},{4,6},{5,7},{6,4},{7,5},{8,10},{9,11},{10,... | collective-permute-start | bytes 331784 | tf_op jit(solution)/shard_map/ppermute | solution.py:27
  86.2 7.8 %collective-permute-start.21 = (bf16[1,2,48,1024]{3,2,1,0:T(8,128)(2,1)S(1)}, bf16[1,2,48,1024]{3,2,1,0:T(8,128)(2,1)S(1)}, u32[]{:S(2)}, u32[]{:S(2)}) collective-permute-start(bf16[1,2,48,1024]{3,2,1,0:T(8,128)(2,1)S(1)} %get-tuple-element.71), channel_id=1, source_target_pairs={{0,4},{4,0},{8,12},{12,8},{16,20},{20,16},{24,28},{28,24},{1,5},{5... | collective-permute-start | bytes 589832 | tf_op jit(solution)/shard_map/ppermute | solution.py:18
  86.9 10.4 %collective-permute-start.27 = (bf16[2,2,48,1024]{3,2,0,1:T(8,128)(2,1)S(1)}, bf16[2,2,48,1024]{3,2,0,1:T(8,128)(2,1)S(1)}, u32[]{:S(2)}, u32[]{:S(2)}) collective-permute-start(bf16[2,2,48,1024]{3,2,0,1:T(8,128)(2,1)S(1)} %pad_maximum_fusion.1), channel_id=1, source_target_pairs={{0,2},{1,3},{2,0},{3,1},{4,6},{5,7},{6,4},{7,5},{8,10},{9,11},{10,... | collective-permute-start | bytes 1179656 | tf_op jit(solution)/shard_map/ppermute | solution.py:27
  92.1 8.7 %collective-permute-start.28 = (bf16[2,2,48,1152]{3,2,0,1:T(8,128)(2,1)S(1)}, bf16[2,2,48,1152]{3,2,0,1:T(8,128)(2,1)S(1)}, u32[]{:S(2)}, u32[]{:S(2)}) collective-permute-start(bf16[2,2,48,1152]{3,2,0,1:T(8,128)(2,1)S(1)} %pad_maximum_fusion), channel_id=1, source_target_pairs={{0,4},{4,0},{8,12},{12,8},{16,20},{20,16},{24,28},{28,24},{1,5},{5... | collective-permute-start | bytes 1327112 | tf_op jit(solution)/shard_map/ppermute | solution.py:18
  94.1 18.8 %collective-permute-start.20 = (bf16[1,48,1024]{2,1,0:T(8,128)(2,1)S(1)}, bf16[1,48,1024]{2,1,0:T(8,128)(2,1)S(1)}, u32[]{:S(2)}, u32[]{:S(2)}) collective-permute-start(bf16[1,48,1024]{2,1,0:T(8,128)(2,1)S(1)} %slice_bitcast_fusion.14), channel_id=1, source_target_pairs={{0,4},{4,0},{8,12},{12,8},{16,20},{20,16},{24,28},{28,24},{1,5},{5... | collective-permute-start | bytes 294920 | tf_op jit(solution)/shard_map/ppermute | solution.py:18
  97.3 48.4 %collective-permute-start.22 = (bf16[1,48,1024]{2,1,0:T(8,128)(2,1)S(1)}, bf16[1,48,1024]{2,1,0:T(8,128)(2,1)S(1)}, u32[]{:S(2)}, u32[]{:S(2)}) collective-permute-start(bf16[1,48,1024]{2,1,0:T(8,128)(2,1)S(1)} %slice_bitcast_fusion.12), channel_id=1, source_target_pairs={{0,2},{1,3},{2,0},{3,1},{4,6},{5,7},{6,4},{7,5},{8,10},{9,11},{10,... | collective-permute-start | bytes 294920 | tf_op jit(solution)/shard_map/ppermute | solution.py:27
  112.1 14.2 %collective-permute-start.36 = (bf16[2,2,48,1024]{3,2,0,1:T(8,128)(2,1)S(1)}, bf16[2,2,48,1024]{3,2,0,1:T(8,128)(2,1)S(1)}, u32[]{:S(2)}, u32[]{:S(2)}) collective-permute-start(bf16[2,2,48,1024]{3,2,0,1:T(8,128)(2,1)S(1)} %copy.63), channel_id=1, source_target_pairs={{0,4},{4,0},{8,12},{12,8},{16,20},{20,16},{24,28},{28,24},{1,5},{5... | collective-permute-start | bytes 1179656 | tf_op jit(solution)/shard_map/ppermute | solution.py:18
  113.0 14.7 %collective-permute-start.29 = (bf16[2,2,48,1024]{3,2,0,1:T(8,128)(2,1)S(1)}, bf16[2,2,48,1024]{3,2,0,1:T(8,128)(2,1)S(1)}, u32[]{:S(2)}, u32[]{:S(2)}) collective-permute-start(bf16[2,2,48,1024]{3,2,0,1:T(8,128)(2,1)S(1)} %copy.61), channel_id=1, source_target_pairs={{0,2},{1,3},{2,0},{3,1},{4,6},{5,7},{6,4},{7,5},{8,10},{9,11},{10,... | collective-permute-start | bytes 1179656 | tf_op jit(solution)/shard_map/ppermute | solution.py:27
  126.4 12.1 %collective-permute-start.37 = (bf16[2,48,1024]{2,1,0:T(8,128)(2,1)S(1)}, bf16[2,48,1024]{2,1,0:T(8,128)(2,1)S(1)}, u32[]{:S(2)}, u32[]{:S(2)}) collective-permute-start(bf16[2,48,1024]{2,1,0:T(8,128)(2,1)S(1)} %slice_bitcast_fusion), channel_id=1, source_target_pairs={{0,2},{1,3},{2,0},{3,1},{4,6},{5,7},{6,4},{7,5},{8,10},{9,11},{10,... | collective-permute-start | bytes 589832 | tf_op jit(solution)/shard_map/ppermute | solution.py:27
  127.8 10.9 %collective-permute-start.30 = (bf16[2,48,1024]{2,1,0:T(8,128)(2,1)S(1)}, bf16[2,48,1024]{2,1,0:T(8,128)(2,1)S(1)}, u32[]{:S(2)}, u32[]{:S(2)}) collective-permute-start(bf16[2,48,1024]{2,1,0:T(8,128)(2,1)S(1)} %slice_bitcast_fusion.2), channel_id=1, source_target_pairs={{0,4},{4,0},{8,12},{12,8},{16,20},{20,16},{24,28},{28,24},{1,5},{5... | collective-permute-start | bytes 589832 | tf_op jit(solution)/shard_map/ppermute | solution.py:18
  (29 other events, 219.3 us)

commit v3 on v1

v3 whole, which is shorter than its diff:
```python
import functools
import math

import jax
import jax.numpy as jnp
from jax import lax
from jax.experimental import pallas as pl
from jax.experimental.pallas import tpu as pltpu
from jax.sharding import PartitionSpec as P

HEAD_DIM = 128
F32 = jnp.float32
BF16 = jnp.bfloat16
VMEM_LIMIT = 20 * 1024 * 1024


def over_y(a):
    count = lax.axis_size("seq")
    return lax.ppermute(a, "seq", [(i, i ^ 1) for i in range(count)])


def over_z(a, step):
    count = lax.axis_size("seq")
    return lax.ppermute(a, "seq", [(i, (i + 2 * step) % count) for i in range(count)])


def over_x(a):
    return lax.ppermute(a, "tp", [(i, i ^ 2) for i in range(4)])


def over_core(a):
    return lax.ppermute(a, "tp", [(i, i ^ 1) for i in range(4)])


def add(a, b):
    return (a.astype(F32) + b.astype(F32)).astype(BF16)


def relative_rows(a, x, core):
    blocks = a.reshape((2, 2, a.shape[0] // 4) + a.shape[1:])
    blocks = jnp.where(x == 0, blocks, blocks[::-1])
    blocks = jnp.where(core == 0, blocks, blocks[:, ::-1])
    return jnp.swapaxes(blocks, 0, 1).reshape(a.shape)


def attention_kernel(scale, bases, q_own, q_beside, pos_ref, start_ref, *refs):
    kv_refs, out_ref = refs[:-1], refs[-1]
    piece, width = q_own.shape
    key_pos, n = [], 0
    for kv in kv_refs:
        rows = kv.shape[0]
        column = lax.broadcasted_iota(jnp.int32, (1, rows), 1)
        if rows == piece:
            key_pos.append(column + bases[n])
            n += 1
        else:
            key_pos.append(
                jnp.where(column < piece, column + bases[n], column + (bases[n + 1] - piece))
            )
            n += 2
    for part, q_ref in enumerate((q_own, q_beside)):
        rows = pl.ds(part * piece, piece)
        pos, start = pos_ref[rows, :], start_ref[rows, :]
        masks = [(k >= start) & (k <= pos) for k in key_pos]
        for head in range(width // HEAD_DIM):
            lanes = pl.ds(head * HEAD_DIM, HEAD_DIM)
            value_lanes = pl.ds(width + head * HEAD_DIM, HEAD_DIM)
            q = q_ref[:, lanes]
            scores = [
                jnp.where(
                    mask,
                    lax.dot_general(
                        q, kv[:, lanes], (((1,), (1,)), ((), ())), preferred_element_type=F32
                    )
                    * scale,
                    -1e30,
                )
                for kv, mask in zip(kv_refs, masks)
            ]
            top = functools.reduce(jnp.maximum, [jnp.max(v, axis=1, keepdims=True) for v in scores])
            total, mixed = 0.0, 0.0
            for kv, mask, score in zip(kv_refs, masks, scores):
                weight = jnp.where(mask, jnp.exp(score - top), 0.0)
                total = total + jnp.sum(weight, axis=1, keepdims=True)
                mixed = mixed + jnp.dot(
                    weight.astype(BF16), kv[:, value_lanes], preferred_element_type=F32
                )
            out_ref[rows, lanes] = (mixed / total).astype(BF16)


def attend(q, beside, pos, start, bases, blocks):
    vmem = pl.BlockSpec(memory_space=pltpu.VMEM)
    keys = sum(b.shape[0] for b in blocks)
    return pl.pallas_call(
        functools.partial(attention_kernel, 1.0 / math.sqrt(HEAD_DIM)),
        out_shape=jax.ShapeDtypeStruct((2 * q.shape[0], q.shape[1]), BF16),
        in_specs=[pl.BlockSpec(memory_space=pltpu.SMEM)] + [vmem] * (4 + len(blocks)),
        out_specs=vmem,
        compiler_params=pltpu.CompilerParams(vmem_limit_bytes=VMEM_LIMIT),
        cost_estimate=pl.CostEstimate(
            flops=8 * q.size * keys,
            bytes_accessed=8 * q.size + 4 * keys * q.shape[1],
            transcendentals=2 * q.size // HEAD_DIM * keys,
        ),
    )(bases, q, beside, pos, start, *blocks)


def attention(queries, keys, values, lengths, seq, x, core, w_in, w_down):
    ring = lax.axis_size("seq") // 2
    y, z = seq % 2, seq // 2
    rows, width = queries.shape
    half = width // 2

    def split(a):
        left, right = a[:, :half], a[:, half:]
        return jnp.where(y == 0, left, right), jnp.where(y == 0, right, left)

    (k_own, k_other), (v_own, v_other) = split(keys), split(values)
    own, beside = jnp.concatenate([k_own, v_own], 1), jnp.concatenate([k_other, v_other], 1)
    own, beside, queries = lax.optimization_barrier((own, beside, queries))
    q_own, q_other = split(relative_rows(queries, x, core))
    beside = over_y(beside)
    blocks, shard = [own, beside], [2 * z + y, 2 * z + 1 - y]
    q_beside = over_y(q_other)
    for k in range(1, ring // 2 + 1):
        own = over_z(own, 1)
        if k == 1:
            own, beside = lax.optimization_barrier((own, beside))
        if k == 2:
            own, q_beside, w_in, w_down = lax.optimization_barrier((own, q_beside, w_in, w_down))
            beside, q_beside = lax.optimization_barrier((beside, q_beside))
        beside = over_z(beside, 1)
        blocks += [own, beside]
        shard += [2 * (z - k) + y, 2 * (z - k) + 1 - y]
    bases = jnp.stack(shard).astype(jnp.int32) * rows

    local = relative_rows(jnp.arange(rows, dtype=jnp.int32), x, core)
    pos = jnp.concatenate([seq * rows + local, (seq ^ 1) * rows + local])
    bounds = jnp.cumsum(lengths)
    start = jnp.max(jnp.where(bounds[None, :] <= pos[:, None], bounds[None, :], 0), axis=1)
    w_in = lax.optimization_barrier(w_in.transpose(0, 2, 1, 3))
    blocks, w_in, w_down = lax.optimization_barrier((blocks, w_in, w_down))
    weights = (w_in, over_core(w_in)), (w_down, over_core(w_down))
    out = attend(q_own, q_beside, pos[:, None], start[:, None], bases, blocks)
    return out[:rows], over_y(out[rows:]), weights


def expert_kernel(layout, ways, count, first, *refs):
    pieces, refs = refs[: -(len(ways) * 2 + 9)], refs[-(len(ways) * 2 + 9) :]
    ins, downs = refs[:2], refs[2:4]
    outs, (tokens, total, w_in, w_down, sems) = refs[4:-5], refs[-5:]
    owned, width = ins[0].shape[0], ins[0].shape[2]
    copies = []
    for k in range(2 * owned):
        core, e = divmod(k, owned)
        copies.append(
            [
                pltpu.make_async_copy(ins[core].at[e], w_in.at[k % 2], sems.at[0, k]),
                pltpu.make_async_copy(downs[core].at[e], w_down.at[k % 2], sems.at[1, k]),
            ]
        )
        if k < 2:
            for copy in copies[-1]:
                copy.start()
    rows = pieces[0].shape[-2]
    column = lax.broadcasted_iota(jnp.int32, (1, count), 1)
    factors = [[] for _ in range(owned)]
    for i, quarter in enumerate(layout):
        at, start = pl.ds(i * rows, rows), 0
        for index, place in quarter:
            part = pieces[index].at[place] if place else pieces[index]
            size = min(part.shape[1], width - start)
            tokens[at, start : start + size] = part[:, :size]
            start += size
        packed = part[:, size:].astype(F32)
        weight = packed[:, :count] + packed[:, count : 2 * count]
        for e in range(owned):
            chosen = jnp.where(column == first[0] + e, weight, 0.0)
            factors[e].append(jnp.sum(chosen, axis=1, keepdims=True))
    factors = [jnp.concatenate(f, 0) for f in factors]
    for k in range(2 * owned):
        factor = factors[k % owned]
        copies[k][0].wait()
        gate = jnp.dot(tokens[...], w_in[k % 2, 0], preferred_element_type=F32)
        up = jnp.dot(tokens[...], w_in[k % 2, 1], preferred_element_type=F32)
        hidden = gate / (1.0 + jnp.exp(-gate)) * up * factor
        hidden = jnp.where(factor > 0, hidden, 0.0).astype(BF16)
        copies[k][1].wait()
        if k + 2 < 2 * owned:
            copies[k + 2][0].start()
        out = jnp.dot(hidden, w_down[k % 2], preferred_element_type=F32)
        if k == 0:
            total[...] = out
        else:
            total[...] += out
        if k + 2 < 2 * owned:
            copies[k + 2][1].start()
    for k, (group, by, start, size) in enumerate(ways):
        keep, send = outs[2 * k], outs[2 * k + 1]
        for i in range(4):
            at = pl.ds((4 * group + i) * rows, rows)
            y, x = divmod(i, 2)
            part = total[at, start : start + size].astype(BF16)
            if by == "x":
                (send if x else keep)[y] = part
            else:
                (send if y else keep)[x] = part


def experts(first, count, pieces, layout, ways, weights):
    (in_own, in_other), (down_own, down_other) = weights
    owned, _, width, inner = in_own.shape
    rows = pieces[0].shape[-2]
    n = len(layout) * rows
    vmem = pl.BlockSpec(memory_space=pltpu.VMEM)
    return pl.pallas_call(
        functools.partial(expert_kernel, layout, ways, count),
        out_shape=[
            jax.ShapeDtypeStruct((2, rows, size), BF16) for *_, size in ways for _ in range(2)
        ],
        in_specs=[pl.BlockSpec(memory_space=pltpu.SMEM)]
        + [vmem] * len(pieces)
        + [pl.BlockSpec(memory_space=pltpu.HBM)] * 4,
        out_specs=[vmem] * (2 * len(ways)),
        scratch_shapes=[
            pltpu.VMEM((n, width), BF16),
            pltpu.VMEM((n, width), F32),
            pltpu.VMEM((2, 2, width, inner), BF16),
            pltpu.VMEM((2, inner, width), BF16),
            pltpu.SemaphoreType.DMA((2, 2 * owned)),
        ],
        compiler_params=pltpu.CompilerParams(vmem_limit_bytes=VMEM_LIMIT),
        cost_estimate=pl.CostEstimate(
            flops=12 * n * owned * width * inner,
            bytes_accessed=12 * owned * width * inner + 4 * n * width,
            transcendentals=2 * n * owned * inner,
        ),
    )(first, *pieces, in_own, in_other, down_own, down_other)


HALVES = (
    ((0, ()), (1, ())),
    ((4, (0,)), (3, ())),
    ((2, ()), (5, (0,))),
    ((4, (1,)), (5, (1,))),
)
GROUPS = (
    ((0, ()),),
    ((4, (0,)),),
    ((2, ()),),
    ((4, (1,)),),
    ((1, ()),),
    ((3, ()),),
    ((5, (0,)),),
    ((5, (1,)),),
)


def plane_first(a, b):
    return a, b, over_y(a), over_x(b)


def plane_second(a, b, y_a, x_b):
    return a, b, y_a, x_b, over_x(jnp.stack([a, y_a])), over_y(jnp.stack([b, x_b]))


def gather_tokens(unit, use_halves, use_groups):
    half = lax.axis_size("seq") // 4
    middle = (unit.shape[1] - 128) // 2
    own = plane_first(unit[:, :middle], unit[:, middle:])
    up, down, pairs = unit, unit, []
    for _ in range(1, half):
        up, down = over_z(up, 1), over_z(down, -1)
        pairs.append((up, down))
    far_a, far_b = over_z(up[:, :middle], 1), over_z(down[:, middle:], -1)
    own = plane_second(*own)
    pairs = [plane_first(*pair) for pair in pairs]
    far = plane_first(far_a, far_b)
    far, pairs = lax.optimization_barrier((far, pairs))
    far = plane_second(*far)
    pairs = [plane_second(*pair) for pair in pairs]
    own = use_halves(own)
    pairs, own = lax.optimization_barrier((pairs, own))
    pairs = [use_groups(pair) for pair in pairs]
    own = scatter_first(*own)
    own, pairs = lax.optimization_barrier((own, pairs))
    far, pairs = lax.optimization_barrier((far, pairs))
    pairs = [scatter_first(*pair) for pair in pairs]
    far = use_halves(far)
    far, pairs = lax.optimization_barrier((far, pairs))
    far = scatter_first(*far)
    far, pairs = lax.optimization_barrier((far, pairs))
    far = scatter_second(*far)
    pairs = [scatter_second(*pair) for pair in pairs]
    own, far = lax.optimization_barrier((own, far))
    return scatter_second(*own), far, pairs


def scatter_first(a_keep, a_send, b_keep, b_send):
    return add(a_keep, over_x(a_send)), add(b_keep, over_y(b_send))


def scatter_second(a, b):
    return add(a[0], over_y(a[1])), add(b[0], over_x(b[1]))


def mix(own, far, pairs):
    half = lax.axis_size("seq") // 4
    total = jnp.concatenate(own, 1).astype(F32)
    for k, (low, high) in enumerate(pairs):
        total = total + over_z(low, -1 - k).astype(F32) + over_z(high, 1 + k).astype(F32)
    return (total + over_z(jnp.concatenate(far, 1), half).astype(F32)).astype(BF16)


def shards(
    queries, keys, values, lengths, resid, w_out, moe_gain, routes, gates, w_gate_up, w_down
):
    seq, tp = lax.axis_index("seq"), lax.axis_index("tp")
    x, core, y = tp // 2, tp % 2, seq % 2
    rows = resid.shape[0]
    owned = w_gate_up.shape[0]
    count = owned * lax.axis_size("seq")

    own, other, weights = attention(
        queries, keys, values, lengths, seq, x, core, w_gate_up, w_down
    )
    heads = jnp.where(
        y == 0, jnp.concatenate([own, other], 1), jnp.concatenate([other, own], 1)
    )
    received = over_core(
        jnp.dot(heads[2 * rows :], w_out, preferred_element_type=F32).astype(BF16)
    )
    partial = jnp.dot(heads[: 2 * rows], w_out, preferred_element_type=F32)
    partial = partial + received.astype(F32)

    matches = routes[:, :, None] == jnp.arange(count, dtype=jnp.int32)[None, None, :]
    weight = jnp.sum(jnp.where(matches, gates[:, :, None], 0.0), axis=1)
    high = weight.astype(BF16)
    low = (weight - high.astype(F32)).astype(BF16)
    pad = -(-2 * count // 128) * 128 - 2 * count
    packed = jnp.concatenate([high, low, jnp.zeros((rows, pad), BF16)], 1)

    arrived = over_x(partial[rows:].astype(BF16))
    arrived, weights = lax.optimization_barrier((arrived, weights))
    attended = (resid.astype(F32) + partial[:rows] + arrived.astype(F32)).astype(BF16)
    widened = attended.astype(F32)
    meansq = jnp.mean(widened * widened, axis=1, keepdims=True)
    normed = (widened * lax.rsqrt(meansq + 1e-05) * moe_gain[None, :]).astype(BF16)

    first = (owned * seq).astype(jnp.int32).reshape(1)
    half = resid.shape[1] // 2
    halves = ((0, "x", 0, half), (0, "y", half, half))
    groups = ((0, "x", 0, 2 * half), (1, "y", 0, 2 * half))
    return attended, mix(
        *gather_tokens(
            jnp.concatenate([normed, packed], 1),
            lambda pieces: experts(first, count, pieces, HALVES, halves, weights),
            lambda pieces: experts(first, count, pieces, GROUPS, groups, weights),
        )
    )


def solution(mesh):
    return jax.shard_map(
        shards,
        mesh=mesh,
        in_specs=(
            P("seq", "tp"),
            P("seq", "tp"),
            P("seq", "tp"),
            P(),
            P(("seq", "tp"), None),
            P("tp", None),
            P(),
            P(("seq", "tp"), None),
            P(("seq", "tp"), None),
            P("seq", None, None, "tp"),
            P("seq", "tp", None),
        ),
        out_specs=(P(("seq", "tp"), None), P(("seq", "tp"), None)),
        check_vma=False,
    )
```

time: 199 us -> 142 us (0.71)
  waiting for transfers between devices: 94.1 us -> 52.4 us
  Pallas kernels: 3.09 us -> 23.2 us
  matrix products: 17.7 us -> 0.94 us
  local copies, waits for them, and re-layouts: 22.8 us -> 8.53 us
  other arithmetic: 12.1 us -> 3.7 us
  starting transfers between devices: 47.6 us -> 51.7 us
    ppermute x20 -> x11, waiting for transfers between devices: 61.5 us -> 21.2 us  [over_z(): lax.ppermute(a, 'seq', [(i, (i + 2 * step) % count) for i in range(count)])]
    pallas_call x0 -> x3, Pallas kernels: none -> 20 us  [experts(): pl.pallas_call(functools.partial(expert_kernel, layout, ways, count), out...]
    unnamed x28 -> x24, local copies, waits for them, and re-layouts: 19.2 us -> 1.91 us
    dot_general x6 -> x2, matrix products: 17.7 us -> 0.94 us  [the longest x1 0.47 us: shards(): jnp.dot(heads[2 * rows:], w_out, preferred_element_type=F32).astype(BF16)]
    ppermute x20 -> x11, starting transfers between devices: 32.3 us -> 16.8 us  [over_z(): lax.ppermute(a, 'seq', [(i, (i + 2 * step) % count) for i in range(count)])]
    ppermute x5 -> x13, starting transfers between devices: 5.28 us -> 16.9 us  [over_x(): return lax.ppermute(a, 'tp', [(i, i ^ 2) for i in range(4)])]
    ppermute x10 -> x15, starting transfers between devices: 9.38 us -> 17.5 us  [over_y(): return lax.ppermute(a, 'seq', [(i, i ^ 1) for i in range(count)])]
    ppermute x10 -> x15, waiting for transfers between devices: 20.6 us -> 15.2 us  [over_y(): return lax.ppermute(a, 'seq', [(i, i ^ 1) for i in range(count)])]
  transfers between devices with their start and end apart: 38 -> 42, of which waited for: 21 -> 22; matrix products, arithmetic and copies ran while one was open for 17% -> 6% of each run, Pallas kernels for 0% -> 16%
where the time goes in v3:
time: 142 us
  waiting for transfers between devices  52.4 us (37%)
  starting transfers between devices  51.7 us (36%)
  Pallas kernels  23.2 us (16%)
  local copies, waits for them, and re-layouts  8.53 us (6%)
  other arithmetic  3.7 us (3%)
    ppermute x11, waiting for transfers between devices, over_z(): lax.ppermute(a, 'seq', [(i, (i + 2 * step) % count) for i in range(count)])  21.2 us
    pallas_call x3, Pallas kernels, experts(): pl.pallas_call(functools.partial(expert_kernel, layout, ways, count), out...  20 us
    ppermute x15, starting transfers between devices, over_y(): return lax.ppermute(a, 'seq', [(i, i ^ 1) for i in range(count)])  17.5 us
    ppermute x13, starting transfers between devices, over_x(): return lax.ppermute(a, 'tp', [(i, i ^ 2) for i in range(4)])  16.9 us
    ppermute x11, starting transfers between devices, over_z(): lax.ppermute(a, 'seq', [(i, (i + 2 * step) % count) for i in range(count)])  16.8 us
    ppermute x15, waiting for transfers between devices, over_y(): return lax.ppermute(a, 'seq', [(i, i ^ 1) for i in range(count)])  15.2 us
    ppermute x13, waiting for transfers between devices, over_x(): return lax.ppermute(a, 'tp', [(i, i ^ 2) for i in range(4)])  14.5 us
    optimization_barrier x1, local copies, waits for them, and re-layouts, attention(): lax.optimization_barrier((own, q_beside, w_in, w_down))  4.76 us
  transfers between devices with their start and end apart: 42, of which 22 were waited for; matrix products, arithmetic and copies ran while one was open for 6% of the time, Pallas kernels for 16%

profile of v3, /device:TPU:0, one launch (start us, length us, event | category | flops | bytes accessed | tf_op | source)
XLA Modules:
  0.0 141.7 jit_solution(614172077766641820)
XLA Ops:
  1.9 3.1 %collective-permute-start = (bf16[192,512]{1,0:T(8,128)(2,1)S(1)}, bf16[192,512]{1,0:T(8,128)(2,1)S(1)}, u32[]{:S(2)}, u32[]{:S(2)}) collective-permute-start(bf16[192,512]{1,0:T(8,128)(2,1)S(1)} %pad_maximum_fusion.4.refs_0_), channel_id=1, source_target_pairs={{0,8},{4,12},{8,16},{12,20},{16,24},{20,28},{24,0},{28,4},{1,9},{5... | collective-permute-start | bytes 589832 | tf_op jit(solution)/shard_map/ppermute | solution.py:24
  7.6 4.3 %collective-permute-done.refs_2_ = bf16[192,512]{1,0:T(8,128)(2,1)S(1)} collective-permute-done((bf16[192,512]{1,0:T(8,128)(2,1)S(1)}, bf16[192,512]{1,0:T(8,128)(2,1)S(1)}, u32[]{:S(2)}, u32[]{:S(2)}) %collective-permute-start) | collective-permute-done | bytes 196640 | tf_op jit(solution)/shard_map/ppermute | solution.py:24
  16.1 3.1 %collective-permute-done.4.q_beside = bf16[192,256]{1,0:T(8,128)(2,1)S(1)} collective-permute-done((bf16[192,256]{1,0:T(8,128)(2,1)S(1)}, bf16[192,256]{1,0:T(8,128)(2,1)S(1)}, u32[]{:S(2)}, u32[]{:S(2)}) %collective-permute-start.4) | collective-permute-done | bytes 98336 | tf_op jit(solution)/shard_map/ppermute | solution.py:19
  19.2 4.8 %collective-permute-done.3.refs_4_ = bf16[192,512]{1,0:T(8,128)(2,1)S(1)} collective-permute-done((bf16[192,512]{1,0:T(8,128)(2,1)S(1)}, bf16[192,512]{1,0:T(8,128)(2,1)S(1)}, u32[]{:S(2)}, u32[]{:S(2)}) %collective-permute-start.3) | collective-permute-done | bytes 196640 | tf_op jit(solution)/shard_map/ppermute | solution.py:24
  24.0 4.8 %copy.41 = bf16[2,2048,2,256]{3,1,2,0:T(8,128)(2,1)} copy(bf16[2,2048,2,256]{3,2,1,0:T(2,128)(2,1)} %param.20) | data formatting | bytes 8388608 | tf_op jit(solution)/shard_map/optimization_barrier | solution.py:130
  28.8 2.7 %collective-permute-done.5.refs_5_ = bf16[192,512]{1,0:T(8,128)(2,1)S(1)} collective-permute-done((bf16[192,512]{1,0:T(8,128)(2,1)S(1)}, bf16[192,512]{1,0:T(8,128)(2,1)S(1)}, u32[]{:S(2)}, u32[]{:S(2)}) %collective-permute-start.5) | collective-permute-done | bytes 196640 | tf_op jit(solution)/shard_map/ppermute | solution.py:24
  34.8 3.2 %shard_map.122 = bf16[384,256]{1,0:T(8,128)(2,1)S(1)} custom-call(s32[6]{0:T(128)S(1)} %broadcast_multiply_fusion.bases, bf16[192,256]{1,0:T(8,128)(2,1)S(1)} %get-tuple-element.179.q_own, bf16[192,256]{1,0:T(8,128)(2,1)S(1)} %collective-permute-done.4.q_beside, s32[384,1]{1,0:T(8,128)S(1)} %broadcast_in_dim.45.pos_ref, ...), custom_call_target="tpu_custom_call" | custom-call | flops 452984832 | bytes 1572864 | tf_op jit(solution)/shard_map/pallas_call | solution.py:94
  39.4 3.4 %collective-permute-done.6 = bf16[192,256]{1,0:T(8,128)(2,1)S(1)} collective-permute-done((bf16[192,256]{1,0:T(8,128)(2,1)S(1)}, bf16[192,256]{1,0:T(8,128)(2,1)S(1)}, u32[]{:S(2)}, u32[]{:S(2)}) %collective-permute-start.6) | collective-permute-done | bytes 98336 | tf_op jit(solution)/shard_map/ppermute | solution.py:19
  47.0 5.7 %collective-permute-done.8 = bf16[48,2048]{1,0:T(8,128)(2,1)S(1)} collective-permute-done((bf16[48,2048]{1,0:T(8,128)(2,1)S(1)}, bf16[48,2048]{1,0:T(8,128)(2,1)S(1)}, u32[]{:S(2)}, u32[]{:S(2)}) %collective-permute-start.8) | collective-permute-done | bytes 196640 | tf_op jit(solution)/shard_map/ppermute | solution.py:28
  53.2 3.8 %collective-permute-start.13 = (bf16[48,2176]{1,0:T(8,128)(2,1)S(1)}, bf16[48,2176]{1,0:T(8,128)(2,1)S(1)}, u32[]{:S(2)}, u32[]{:S(2)}) collective-permute-start(bf16[48,2176]{1,0:T(8,128)(2,1)S(1)} %concatenate.29), channel_id=1, source_target_pairs={{0,24},{4,28},{8,0},{12,4},{16,8},{20,12},{24,16},{28,20},{1,25},{... | collective-permute-start | bytes 626696 | tf_op jit(solution)/shard_map/ppermute | solution.py:24
  60.0 3.2 %collective-permute-done.11.refs_0_ = bf16[48,2176]{1,0:T(8,128)(2,1)S(1)} collective-permute-done((bf16[48,2176]{1,0:T(8,128)(2,1)S(1)}, bf16[48,2176]{1,0:T(8,128)(2,1)S(1)}, u32[]{:S(2)}, u32[]{:S(2)}) %collective-permute-start.11) | collective-permute-done | bytes 208928 | tf_op jit(solution)/shard_map/ppermute | solution.py:24
  64.2 3.2 %collective-permute-start.14 = (bf16[48,1152]{1,0:T(8,128)(2,1)S(1)}, bf16[48,1152]{1,0:T(8,128)(2,1)S(1)}, u32[]{:S(2)}, u32[]{:S(2)}) collective-permute-start(bf16[48,1152]{1,0:T(8,128)(2,1)S(1)} %slice.122), channel_id=1, source_target_pairs={{0,24},{4,28},{8,0},{12,4},{16,8},{20,12},{24,16},{28,20},{1,25},{... | collective-permute-start | bytes 331784 | tf_op jit(solution)/shard_map/ppermute | solution.py:24
  72.8 3.6 %collective-permute-done.15.refs_2_ = bf16[48,1024]{1,0:T(8,128)(2,1)S(1)} collective-permute-done((bf16[48,1024]{1,0:T(8,128)(2,1)S(1)}, bf16[48,1024]{1,0:T(8,128)(2,1)S(1)}, u32[]{:S(2)}, u32[]{:S(2)}) %collective-permute-start.15) | collective-permute-done | bytes 98336 | tf_op jit(solution)/shard_map/ppermute | solution.py:19
  82.2 2.4 %collective-permute-done.24.refs_5_ = bf16[2,48,1152]{2,1,0:T(8,128)(2,1)S(1)} collective-permute-done((bf16[2,48,1152]{2,1,0:T(8,128)(2,1)S(1)}, bf16[2,48,1152]{2,1,0:T(8,128)(2,1)S(1)}, u32[]{:S(2)}, u32[]{:S(2)}) %collective-permute-start.24) | collective-permute-done | bytes 221216 | tf_op jit(solution)/shard_map/ppermute | solution.py:19
  84.7 6.0 %shard_map.123 = (bf16[2,48,1024]{2,1,0:T(8,128)(2,1)S(1)}, bf16[2,48,1024]{2,1,0:T(8,128)(2,1)S(1)}, bf16[2,48,1024]{2,1,0:T(8,128)(2,1)S(1)}, bf16[2,48,1024]{2,1,0:T(8,128)(2,1)S(1)}) custom-call(s32[1]{0:T(128)} %bitcast.19.first, bf16[48,1024]{1,0:T(8,128)(2,1)S(1)} %get-tuple-element.175.refs_0_, bf16[48,1152]{1,0:T(8,128)(2,1)S(1)} %get-tuple-element.173.refs_1_, ...), custom_call_target="tpu_custom_call" | custom-call | flops 2415919104 | bytes 14155776 | tf_op jit(solution)/shard_map/pallas_call | solution.py:216
  95.1 7.9 %shard_map.124 = (bf16[2,48,2048]{2,1,0:T(8,128)(2,1)S(1)}, bf16[2,48,2048]{2,1,0:T(8,128)(2,1)S(1)}, bf16[2,48,2048]{2,1,0:T(8,128)(2,1)S(1)}, bf16[2,48,2048]{2,1,0:T(8,128)(2,1)S(1)}) custom-call(s32[1]{0:T(128)} %bitcast.19.first, bf16[48,2176]{1,0:T(8,128)(2,1)S(1)} %collective-permute-done.11.refs_0_, ...), custom_call_target="tpu_custom_call" | custom-call | flops 4831838208 | bytes 15728640 | tf_op jit(solution)/shard_map/pallas_call | solution.py:216
  103.2 2.1 %collective-permute-start.29 = (bf16[2,48,2048]{2,1,0:T(8,128)(2,1)S(1)}, bf16[2,48,2048]{2,1,0:T(8,128)(2,1)S(1)}, u32[]{:S(2)}, u32[]{:S(2)}) collective-permute-start(bf16[2,48,2048]{2,1,0:T(8,128)(2,1)S(1)} %get-tuple-element.153), channel_id=1, source_target_pairs={{0,2},{1,3},{2,0},{3,1},{4,6},{5,7},{6,4},{7,5},{8,10},{9,11},{10,... | collective-permute-start | bytes 1179656 | tf_op jit(solution)/shard_map/ppermute | solution.py:28
  105.7 6.0 %shard_map.125 = (bf16[2,48,1024]{2,1,0:T(8,128)(2,1)S(1)}, bf16[2,48,1024]{2,1,0:T(8,128)(2,1)S(1)}, bf16[2,48,1024]{2,1,0:T(8,128)(2,1)S(1)}, bf16[2,48,1024]{2,1,0:T(8,128)(2,1)S(1)}) custom-call(s32[1]{0:T(128)} %bitcast.19.first, bf16[48,1024]{1,0:T(8,128)(2,1)S(1)} %collective-permute-done.12.refs_0_, ...), custom_call_target="tpu_custom_call" | custom-call | flops 2415919104 | bytes 14155776 | tf_op jit(solution)/shard_map/pallas_call | solution.py:216
  116.7 5.5 %collective-permute-done.31 = bf16[2,48,1024]{2,1,0:T(8,128)(2,1)S(1)} collective-permute-done((bf16[2,48,1024]{2,1,0:T(8,128)(2,1)S(1)}, bf16[2,48,1024]{2,1,0:T(8,128)(2,1)S(1)}, u32[]{:S(2)}, u32[]{:S(2)}) %collective-permute-start.31) | collective-permute-done | bytes 196640 | tf_op jit(solution)/shard_map/ppermute | solution.py:28
  123.6 1.8 %collective-permute-start.34 = (bf16[48,1024]{1,0:T(8,128)(2,1)S(1)}, bf16[48,1024]{1,0:T(8,128)(2,1)S(1)}, u32[]{:S(2)}, u32[]{:S(2)}) collective-permute-start(bf16[48,1024]{1,0:T(8,128)(2,1)S(1)} %slice_bitcast_fusion.4), channel_id=1, source_target_pairs={{0,2},{1,3},{2,0},{3,1},{4,6},{5,7},{6,4},{7,5},{8,10},{9,11},{10,... | collective-permute-start | bytes 294920 | tf_op jit(solution)/shard_map/ppermute | solution.py:28
  128.4 1.8 %collective-permute-start.36 = (bf16[48,1024]{1,0:T(8,128)(2,1)S(1)}, bf16[48,1024]{1,0:T(8,128)(2,1)S(1)}, u32[]{:S(2)}, u32[]{:S(2)}) collective-permute-start(bf16[48,1024]{1,0:T(8,128)(2,1)S(1)} %slice_bitcast_fusion.2), channel_id=1, source_target_pairs={{0,2},{1,3},{2,0},{3,1},{4,6},{5,7},{6,4},{7,5},{8,10},{9,11},{10,... | collective-permute-start | bytes 294920 | tf_op jit(solution)/shard_map/ppermute | solution.py:28
  132.9 2.6 %collective-permute-start.38 = (bf16[48,2048]{1,0:T(8,128)(2,1)S(1)}, bf16[48,2048]{1,0:T(8,128)(2,1)S(1)}, u32[]{:S(2)}, u32[]{:S(2)}) collective-permute-start(bf16[48,2048]{1,0:T(8,128)(2,1)S(1)} %fusion.6), channel_id=1, source_target_pairs={{0,24},{4,28},{8,0},{12,4},{16,8},{20,12},{24,16},{28,20},{1,25},{... | collective-permute-start | bytes 589832 | tf_op jit(solution)/shard_map/ppermute | solution.py:24
  135.7 3.5 %collective-permute-done.40 = bf16[48,2048]{1,0:T(8,128)(2,1)S(1)} collective-permute-done((bf16[48,2048]{1,0:T(8,128)(2,1)S(1)}, bf16[48,2048]{1,0:T(8,128)(2,1)S(1)}, u32[]{:S(2)}, u32[]{:S(2)}) %collective-permute-start.40) | collective-permute-done | bytes 196640 | tf_op jit(solution)/shard_map/ppermute | solution.py:24
  139.2 1.7 %collective-permute-done.38 = bf16[48,2048]{1,0:T(8,128)(2,1)S(1)} collective-permute-done((bf16[48,2048]{1,0:T(8,128)(2,1)S(1)}, bf16[48,2048]{1,0:T(8,128)(2,1)S(1)}, u32[]{:S(2)}, u32[]{:S(2)}) %collective-permute-start.38) | collective-permute-done | bytes 196640 | tf_op jit(solution)/shard_map/ppermute | solution.py:24
  (154 shorter events, 50.1 us)
Async XLA Ops:
  1.9 10.0 %collective-permute-start = (bf16[192,512]{1,0:T(8,128)(2,1)S(1)}, bf16[192,512]{1,0:T(8,128)(2,1)S(1)}, u32[]{:S(2)}, u32[]{:S(2)}) collective-permute-start(bf16[192,512]{1,0:T(8,128)(2,1)S(1)} %pad_maximum_fusion.4.refs_0_), channel_id=1, source_target_pairs={{0,8},{4,12},{8,16},{12,20},{16,24},{20,28},{24,0},{28,4},{1,9},{5... | collective-permute-start | bytes 589832 | tf_op jit(solution)/shard_map/ppermute | solution.py:24
  11.9 12.1 %collective-permute-start.2 = (bf16[192,512]{1,0:T(8,128)(2,1)S(1)}, bf16[192,512]{1,0:T(8,128)(2,1)S(1)}, u32[]{:S(2)}, u32[]{:S(2)}) collective-permute-start(bf16[192,512]{1,0:T(8,128)(2,1)S(1)} %collective-permute-done.1.refs_1_), channel_id=1, source_target_pairs={{0,8},{4,12},{8,16},{12,20},{16,24},{20,28},{24,0},{28,4},{1,9},{5... | collective-permute-start | bytes 589832 | tf_op jit(solution)/shard_map/ppermute | solution.py:24
  12.9 11.1 %collective-permute-start.3 = (bf16[192,512]{1,0:T(8,128)(2,1)S(1)}, bf16[192,512]{1,0:T(8,128)(2,1)S(1)}, u32[]{:S(2)}, u32[]{:S(2)}) collective-permute-start(bf16[192,512]{1,0:T(8,128)(2,1)S(1)} %collective-permute-done.refs_2_), channel_id=1, source_target_pairs={{0,8},{4,12},{8,16},{12,20},{16,24},{20,28},{24,0},{28,4},{1,9},{5... | collective-permute-start | bytes 589832 | tf_op jit(solution)/shard_map/ppermute | solution.py:24
  31.5 21.2 %collective-permute-start.9 = (bf16[2,2,2048,256]{3,2,1,0:T(8,128)(2,1)}, bf16[2,2,2048,256]{3,2,1,0:T(8,128)(2,1)}, u32[]{:S(2)}, u32[]{:S(2)}) collective-permute-start(bf16[2,2,2048,256]{3,2,1,0:T(8,128)(2,1)} %bitcast.65.refs_6_), channel_id=1, source_target_pairs={{0,1},{1,0},{2,3},{3,2},{4,5},{5,4},{6,7},{7,6},{8,9},{9,8},{10,11... | collective-permute-start | bytes 12582920 | tf_op jit(solution)/shard_map/ppermute | solution.py:32
  31.7 21.0 %collective-permute-start.10 = (bf16[2,256,2048]{2,1,0:T(8,128)(2,1)}, bf16[2,256,2048]{2,1,0:T(8,128)(2,1)}, u32[]{:S(2)}, u32[]{:S(2)}) collective-permute-start(bf16[2,256,2048]{2,1,0:T(8,128)(2,1)} %refs_8_.2), channel_id=1, source_target_pairs={{0,1},{1,0},{2,3},{3,2},{4,5},{5,4},{6,7},{7,6},{8,9},{9,8},{10,11... | collective-permute-start | bytes 6291464 | tf_op jit(solution)/shard_map/ppermute | solution.py:32
  53.2 10.0 %collective-permute-start.11 = (bf16[48,2176]{1,0:T(8,128)(2,1)S(1)}, bf16[48,2176]{1,0:T(8,128)(2,1)S(1)}, u32[]{:S(2)}, u32[]{:S(2)}) collective-permute-start(bf16[48,2176]{1,0:T(8,128)(2,1)S(1)} %concatenate.29), channel_id=1, source_target_pairs={{0,8},{4,12},{8,16},{12,20},{16,24},{20,28},{24,0},{28,4},{1,9},{5... | collective-permute-start | bytes 626696 | tf_op jit(solution)/shard_map/ppermute | solution.py:24
  53.2 10.9 %collective-permute-start.13 = (bf16[48,2176]{1,0:T(8,128)(2,1)S(1)}, bf16[48,2176]{1,0:T(8,128)(2,1)S(1)}, u32[]{:S(2)}, u32[]{:S(2)}) collective-permute-start(bf16[48,2176]{1,0:T(8,128)(2,1)S(1)} %concatenate.29), channel_id=1, source_target_pairs={{0,24},{4,28},{8,0},{12,4},{16,8},{20,12},{24,16},{28,20},{1,25},{... | collective-permute-start | bytes 626696 | tf_op jit(solution)/shard_map/ppermute | solution.py:24
  57.1 10.3 %collective-permute-start.21 = (bf16[48,1024]{1,0:T(8,128)(2,1)S(1)}, bf16[48,1024]{1,0:T(8,128)(2,1)S(1)}, u32[]{:S(2)}, u32[]{:S(2)}) collective-permute-start(bf16[48,1024]{1,0:T(8,128)(2,1)S(1)} %get-tuple-element.175.refs_0_), channel_id=1, source_target_pairs={{0,4},{4,0},{8,12},{12,8},{16,20},{20,16},{24,28},{28,24},{1,5},{5... | collective-permute-start | bytes 294920 | tf_op jit(solution)/shard_map/ppermute | solution.py:19
  58.4 11.8 %collective-permute-start.22 = (bf16[48,1152]{1,0:T(8,128)(2,1)S(1)}, bf16[48,1152]{1,0:T(8,128)(2,1)S(1)}, u32[]{:S(2)}, u32[]{:S(2)}) collective-permute-start(bf16[48,1152]{1,0:T(8,128)(2,1)S(1)} %get-tuple-element.173.refs_1_), channel_id=1, source_target_pairs={{0,2},{1,3},{2,0},{3,1},{4,6},{5,7},{6,4},{7,5},{8,10},{9,11},{10,... | collective-permute-start | bytes 331784 | tf_op jit(solution)/shard_map/ppermute | solution.py:28
  67.4 14.9 %collective-permute-start.23 = (bf16[2,48,1024]{2,1,0:T(8,128)(2,1)S(1)}, bf16[2,48,1024]{2,1,0:T(8,128)(2,1)S(1)}, u32[]{:S(2)}, u32[]{:S(2)}) collective-permute-start(bf16[2,48,1024]{2,1,0:T(8,128)(2,1)S(1)} %pad_maximum_fusion.6), channel_id=1, source_target_pairs={{0,2},{1,3},{2,0},{3,1},{4,6},{5,7},{6,4},{7,5},{8,10},{9,11},{10,... | collective-permute-start | bytes 589832 | tf_op jit(solution)/shard_map/ppermute | solution.py:28
  68.7 9.2 %collective-permute-start.17 = (bf16[48,2176]{1,0:T(8,128)(2,1)S(1)}, bf16[48,2176]{1,0:T(8,128)(2,1)S(1)}, u32[]{:S(2)}, u32[]{:S(2)}) collective-permute-start(bf16[48,2176]{1,0:T(8,128)(2,1)S(1)} %collective-permute-done.11.refs_0_), channel_id=1, source_target_pairs={{0,4},{4,0},{8,12},{12,8},{16,20},{20,16},{24,28},{28,24},{1,5},{5... | collective-permute-start | bytes 626696 | tf_op jit(solution)/shard_map/ppermute | solution.py:19
  70.2 7.7 %collective-permute-start.18 = (bf16[48,2176]{1,0:T(8,128)(2,1)S(1)}, bf16[48,2176]{1,0:T(8,128)(2,1)S(1)}, u32[]{:S(2)}, u32[]{:S(2)}) collective-permute-start(bf16[48,2176]{1,0:T(8,128)(2,1)S(1)} %collective-permute-done.13.refs_1_), channel_id=1, source_target_pairs={{0,2},{1,3},{2,0},{3,1},{4,6},{5,7},{6,4},{7,5},{8,10},{9,11},{10,... | collective-permute-start | bytes 626696 | tf_op jit(solution)/shard_map/ppermute | solution.py:28
  76.4 8.3 %collective-permute-start.24 = (bf16[2,48,1152]{2,1,0:T(8,128)(2,1)S(1)}, bf16[2,48,1152]{2,1,0:T(8,128)(2,1)S(1)}, u32[]{:S(2)}, u32[]{:S(2)}) collective-permute-start(bf16[2,48,1152]{2,1,0:T(8,128)(2,1)S(1)} %pad_maximum_fusion.2), channel_id=1, source_target_pairs={{0,4},{4,0},{8,12},{12,8},{16,20},{20,16},{24,28},{28,24},{1,5},{5... | collective-permute-start | bytes 663560 | tf_op jit(solution)/shard_map/ppermute | solution.py:19
  79.2 13.7 %collective-permute-start.19 = (bf16[2,48,2176]{2,1,0:T(8,128)(2,1)S(1)}, bf16[2,48,2176]{2,1,0:T(8,128)(2,1)S(1)}, u32[]{:S(2)}, u32[]{:S(2)}) collective-permute-start(bf16[2,48,2176]{2,1,0:T(8,128)(2,1)S(1)} %pad_maximum_fusion), channel_id=1, source_target_pairs={{0,2},{1,3},{2,0},{3,1},{4,6},{5,7},{6,4},{7,5},{8,10},{9,11},{10,... | collective-permute-start | bytes 1253384 | tf_op jit(solution)/shard_map/ppermute | solution.py:28
  80.6 12.9 %collective-permute-start.20 = (bf16[2,48,2176]{2,1,0:T(8,128)(2,1)S(1)}, bf16[2,48,2176]{2,1,0:T(8,128)(2,1)S(1)}, u32[]{:S(2)}, u32[]{:S(2)}) collective-permute-start(bf16[2,48,2176]{2,1,0:T(8,128)(2,1)S(1)} %pad_maximum_fusion.1), channel_id=1, source_target_pairs={{0,4},{4,0},{8,12},{12,8},{16,20},{20,16},{24,28},{28,24},{1,5},{5... | collective-permute-start | bytes 1253384 | tf_op jit(solution)/shard_map/ppermute | solution.py:19
  90.7 12.5 %collective-permute-start.27 = (bf16[2,48,1024]{2,1,0:T(8,128)(2,1)S(1)}, bf16[2,48,1024]{2,1,0:T(8,128)(2,1)S(1)}, u32[]{:S(2)}, u32[]{:S(2)}) collective-permute-start(bf16[2,48,1024]{2,1,0:T(8,128)(2,1)S(1)} %pad_maximum_fusion.7), channel_id=1, source_target_pairs={{0,2},{1,3},{2,0},{3,1},{4,6},{5,7},{6,4},{7,5},{8,10},{9,11},{10,... | collective-permute-start | bytes 589832 | tf_op jit(solution)/shard_map/ppermute | solution.py:28
  92.3 11.0 %collective-permute-start.28 = (bf16[2,48,1152]{2,1,0:T(8,128)(2,1)S(1)}, bf16[2,48,1152]{2,1,0:T(8,128)(2,1)S(1)}, u32[]{:S(2)}, u32[]{:S(2)}) collective-permute-start(bf16[2,48,1152]{2,1,0:T(8,128)(2,1)S(1)} %pad_maximum_fusion.3), channel_id=1, source_target_pairs={{0,4},{4,0},{8,12},{12,8},{16,20},{20,16},{24,28},{28,24},{1,5},{5... | collective-permute-start | bytes 663560 | tf_op jit(solution)/shard_map/ppermute | solution.py:19
  93.5 9.6 %collective-permute-start.25 = (bf16[2,48,1024]{2,1,0:T(8,128)(2,1)S(1)}, bf16[2,48,1024]{2,1,0:T(8,128)(2,1)S(1)}, u32[]{:S(2)}, u32[]{:S(2)}) collective-permute-start(bf16[2,48,1024]{2,1,0:T(8,128)(2,1)S(1)} %get-tuple-element.119), channel_id=1, source_target_pairs={{0,2},{1,3},{2,0},{3,1},{4,6},{5,7},{6,4},{7,5},{8,10},{9,11},{10,... | collective-permute-start | bytes 589832 | tf_op jit(solution)/shard_map/ppermute | solution.py:28
  94.4 8.7 %collective-permute-start.26 = (bf16[2,48,1024]{2,1,0:T(8,128)(2,1)S(1)}, bf16[2,48,1024]{2,1,0:T(8,128)(2,1)S(1)}, u32[]{:S(2)}, u32[]{:S(2)}) collective-permute-start(bf16[2,48,1024]{2,1,0:T(8,128)(2,1)S(1)} %get-tuple-element.121), channel_id=1, source_target_pairs={{0,4},{4,0},{8,12},{12,8},{16,20},{20,16},{24,28},{28,24},{1,5},{5... | collective-permute-start | bytes 589832 | tf_op jit(solution)/shard_map/ppermute | solution.py:19
  103.2 10.0 %collective-permute-start.29 = (bf16[2,48,2048]{2,1,0:T(8,128)(2,1)S(1)}, bf16[2,48,2048]{2,1,0:T(8,128)(2,1)S(1)}, u32[]{:S(2)}, u32[]{:S(2)}) collective-permute-start(bf16[2,48,2048]{2,1,0:T(8,128)(2,1)S(1)} %get-tuple-element.153), channel_id=1, source_target_pairs={{0,2},{1,3},{2,0},{3,1},{4,6},{5,7},{6,4},{7,5},{8,10},{9,11},{10,... | collective-permute-start | bytes 1179656 | tf_op jit(solution)/shard_map/ppermute | solution.py:28
  105.4 9.0 %collective-permute-start.30 = (bf16[2,48,2048]{2,1,0:T(8,128)(2,1)S(1)}, bf16[2,48,2048]{2,1,0:T(8,128)(2,1)S(1)}, u32[]{:S(2)}, u32[]{:S(2)}) collective-permute-start(bf16[2,48,2048]{2,1,0:T(8,128)(2,1)S(1)} %get-tuple-element.155), channel_id=1, source_target_pairs={{0,4},{4,0},{8,12},{12,8},{16,20},{20,16},{24,28},{28,24},{1,5},{5... | collective-permute-start | bytes 1179656 | tf_op jit(solution)/shard_map/ppermute | solution.py:19
  114.5 7.8 %collective-permute-start.31 = (bf16[2,48,1024]{2,1,0:T(8,128)(2,1)S(1)}, bf16[2,48,1024]{2,1,0:T(8,128)(2,1)S(1)}, u32[]{:S(2)}, u32[]{:S(2)}) collective-permute-start(bf16[2,48,1024]{2,1,0:T(8,128)(2,1)S(1)} %get-tuple-element.157), channel_id=1, source_target_pairs={{0,2},{1,3},{2,0},{3,1},{4,6},{5,7},{6,4},{7,5},{8,10},{9,11},{10,... | collective-permute-start | bytes 589832 | tf_op jit(solution)/shard_map/ppermute | solution.py:28
  131.5 7.7 %collective-permute-start.40 = (bf16[48,2048]{1,0:T(8,128)(2,1)S(1)}, bf16[48,2048]{1,0:T(8,128)(2,1)S(1)}, u32[]{:S(2)}, u32[]{:S(2)}) collective-permute-start(bf16[48,2048]{1,0:T(8,128)(2,1)S(1)} %fusion.5), channel_id=1, source_target_pairs={{0,8},{4,12},{8,16},{12,20},{16,24},{20,28},{24,0},{28,4},{1,9},{5... | collective-permute-start | bytes 589832 | tf_op jit(solution)/shard_map/ppermute | solution.py:24
  132.9 8.0 %collective-permute-start.38 = (bf16[48,2048]{1,0:T(8,128)(2,1)S(1)}, bf16[48,2048]{1,0:T(8,128)(2,1)S(1)}, u32[]{:S(2)}, u32[]{:S(2)}) collective-permute-start(bf16[48,2048]{1,0:T(8,128)(2,1)S(1)} %fusion.6), channel_id=1, source_target_pairs={{0,24},{4,28},{8,0},{12,4},{16,8},{20,12},{24,16},{28,20},{1,25},{... | collective-permute-start | bytes 589832 | tf_op jit(solution)/shard_map/ppermute | solution.py:24
  (30 other events, 267.1 us)

commit v4 on v3

--- a/solution.py
+++ b/solution.py
@@ -105,7 +105,7 @@
     )(bases, q, beside, pos, start, *blocks)
 
 
-def attention(queries, keys, values, lengths, seq, x, core, w_in, w_down):
+def attention(queries, keys, values, lengths, seq, x, core):
     ring = lax.axis_size("seq") // 2
     y, z = seq % 2, seq // 2
     rows, width = queries.shape
@@ -127,7 +127,6 @@
         if k == 1:
             own, beside = lax.optimization_barrier((own, beside))
         if k == 2:
-            own, q_beside, w_in, w_down = lax.optimization_barrier((own, q_beside, w_in, w_down))
             beside, q_beside = lax.optimization_barrier((beside, q_beside))
         beside = over_z(beside, 1)
         blocks += [own, beside]
@@ -138,11 +137,8 @@
     pos = jnp.concatenate([seq * rows + local, (seq ^ 1) * rows + local])
     bounds = jnp.cumsum(lengths)
     start = jnp.max(jnp.where(bounds[None, :] <= pos[:, None], bounds[None, :], 0), axis=1)
-    w_in = lax.optimization_barrier(w_in.transpose(0, 2, 1, 3))
-    blocks, w_in, w_down = lax.optimization_barrier((blocks, w_in, w_down))
-    weights = (w_in, over_core(w_in)), (w_down, over_core(w_down))
     out = attend(q_own, q_beside, pos[:, None], start[:, None], bases, blocks)
-    return out[:rows], over_y(out[rows:]), weights
+    return out[:rows], over_y(out[rows:])
 
 
 def expert_kernel(layout, ways, count, first, *refs):
@@ -275,10 +271,11 @@
     far_a, far_b = over_z(up[:, :middle], 1), over_z(down[:, middle:], -1)
     own = plane_second(*own)
     pairs = [plane_first(*pair) for pair in pairs]
+    far_a, far_b, pairs = lax.optimization_barrier((far_a, far_b, pairs))
     far = plane_first(far_a, far_b)
-    far, pairs = lax.optimization_barrier((far, pairs))
+    pairs = [plane_second(*pair) for pair in pairs]
+    far, own = lax.optimization_barrier((far, own))
     far = plane_second(*far)
-    pairs = [plane_second(*pair) for pair in pairs]
     own = use_halves(own)
     pairs, own = lax.optimization_barrier((pairs, own))
     pairs = [use_groups(pair) for pair in pairs]
@@ -321,9 +318,7 @@
     owned = w_gate_up.shape[0]
     count = owned * lax.axis_size("seq")
 
-    own, other, weights = attention(
-        queries, keys, values, lengths, seq, x, core, w_gate_up, w_down
-    )
+    own, other = attention(queries, keys, values, lengths, seq, x, core)
     heads = jnp.where(
         y == 0, jnp.concatenate([own, other], 1), jnp.concatenate([other, own], 1)
     )
@@ -331,6 +326,8 @@
         jnp.dot(heads[2 * rows :], w_out, preferred_element_type=F32).astype(BF16)
     )
     partial = jnp.dot(heads[: 2 * rows], w_out, preferred_element_type=F32)
+    received, w_in = lax.optimization_barrier((received, w_gate_up))
+    w_in = lax.optimization_barrier(w_in.transpose(0, 2, 1, 3))
     partial = partial + received.astype(F32)
 
     matches = routes[:, :, None] == jnp.arange(count, dtype=jnp.int32)[None, None, :]
@@ -341,7 +338,8 @@
     packed = jnp.concatenate([high, low, jnp.zeros((rows, pad), BF16)], 1)
 
     arrived = over_x(partial[rows:].astype(BF16))
-    arrived, weights = lax.optimization_barrier((arrived, weights))
+    arrived, w_in, w_down = lax.optimization_barrier((arrived, w_in, w_down))
+    weights = (w_in, over_core(w_in)), (w_down, over_core(w_down))
     attended = (resid.astype(F32) + partial[:rows] + arrived.astype(F32)).astype(BF16)
     widened = attended.astype(F32)
     meansq = jnp.mean(widened * widened, axis=1, keepdims=True)

time: 142 us -> 138 us (0.972)
  local copies, waits for them, and re-layouts: 8.53 us -> 4.47 us
  waiting for transfers between devices: 52.4 us -> 50.8 us
  starting transfers between devices: 51.7 us -> 53.2 us
    ppermute x15, waiting for transfers between devices: 15.2 us -> 6.77 us  [over_y(): return lax.ppermute(a, 'seq', [(i, i ^ 1) for i in range(count)])]
    ppermute x11, waiting for transfers between devices: 21.2 us -> 28 us  [over_z(): lax.ppermute(a, 'seq', [(i, (i + 2 * step) % count) for i in range(count)])]
    ppermute x13, starting transfers between devices: 16.9 us -> 13.9 us  [over_x(): return lax.ppermute(a, 'tp', [(i, i ^ 2) for i in range(4)])]
    ppermute x15, starting transfers between devices: 17.5 us -> 19.9 us  [over_y(): return lax.ppermute(a, 'seq', [(i, i ^ 1) for i in range(count)])]
    optimization_barrier x1, local copies, waits for them, and re-layouts: 4.76 us -> 2.56 us  [shards(): received, w_in = lax.optimization_barrier((received, w_gate_up))]
    ppermute x11, starting transfers between devices: 16.8 us -> 18.7 us  [over_z(): lax.ppermute(a, 'seq', [(i, (i + 2 * step) % count) for i in range(count)])]
    unnamed x24 -> x18, local copies, waits for them, and re-layouts: 1.91 us -> 0.06 us
  transfers between devices with their start and end apart: 42 -> 42, of which waited for: 22 -> 24; matrix products, arithmetic and copies ran while one was open for 6% -> 5% of each run, Pallas kernels for 16% -> 14%
where the time goes in v4:
time: 138 us
  starting transfers between devices  53.2 us (39%)
  waiting for transfers between devices  50.8 us (37%)
  Pallas kernels  23.2 us (17%)
  local copies, waits for them, and re-layouts  4.47 us (3%)
  other arithmetic  4.34 us (3%)
    ppermute x11, waiting for transfers between devices, over_z(): lax.ppermute(a, 'seq', [(i, (i + 2 * step) % count) for i in range(count)])  28 us
    pallas_call x3, Pallas kernels, experts(): pl.pallas_call(functools.partial(expert_kernel, layout, ways, count), out...  20 us
    ppermute x15, starting transfers between devices, over_y(): return lax.ppermute(a, 'seq', [(i, i ^ 1) for i in range(count)])  19.9 us
    ppermute x11, starting transfers between devices, over_z(): lax.ppermute(a, 'seq', [(i, (i + 2 * step) % count) for i in range(count)])  18.7 us
    ppermute x13, waiting for transfers between devices, over_x(): return lax.ppermute(a, 'tp', [(i, i ^ 2) for i in range(4)])  14.4 us
    ppermute x13, starting transfers between devices, over_x(): return lax.ppermute(a, 'tp', [(i, i ^ 2) for i in range(4)])  13.9 us
    ppermute x15, waiting for transfers between devices, over_y(): return lax.ppermute(a, 'seq', [(i, i ^ 1) for i in range(count)])  6.77 us
    pallas_call x1, Pallas kernels, attend(): pl.pallas_call(functools.partial(attention_kernel, 1.0 / math.sqrt(HEAD_D...  3.22 us
  transfers between devices with their start and end apart: 42, of which 24 were waited for; matrix products, arithmetic and copies ran while one was open for 5% of the time, Pallas kernels for 14%

profile of v4, /device:TPU:0, one launch (start us, length us, event | category | flops | bytes accessed | tf_op | source)
XLA Modules:
  0.0 138.1 jit_solution(3684701326730249343)
XLA Ops:
  1.9 3.1 %collective-permute-start = (bf16[192,512]{1,0:T(8,128)(2,1)S(1)}, bf16[192,512]{1,0:T(8,128)(2,1)S(1)}, u32[]{:S(2)}, u32[]{:S(2)}) collective-permute-start(bf16[192,512]{1,0:T(8,128)(2,1)S(1)} %pad_maximum_fusion.4.refs_0_), channel_id=1, source_target_pairs={{0,8},{4,12},{8,16},{12,20},{16,24},{20,28},{24,0},{28,4},{1,9},{5... | collective-permute-start | bytes 589832 | tf_op jit(solution)/shard_map/ppermute | solution.py:24
  9.0 3.0 %collective-permute-done.refs_2_ = bf16[192,512]{1,0:T(8,128)(2,1)S(1)} collective-permute-done((bf16[192,512]{1,0:T(8,128)(2,1)S(1)}, bf16[192,512]{1,0:T(8,128)(2,1)S(1)}, u32[]{:S(2)}, u32[]{:S(2)}) %collective-permute-start) | collective-permute-done | bytes 196640 | tf_op jit(solution)/shard_map/ppermute | solution.py:24
  16.2 5.8 %collective-permute-done.2.refs_3_ = bf16[192,512]{1,0:T(8,128)(2,1)S(1)} collective-permute-done((bf16[192,512]{1,0:T(8,128)(2,1)S(1)}, bf16[192,512]{1,0:T(8,128)(2,1)S(1)}, u32[]{:S(2)}, u32[]{:S(2)}) %collective-permute-start.2) | collective-permute-done | bytes 196640 | tf_op jit(solution)/shard_map/ppermute | solution.py:24
  21.9 4.1 %collective-permute-done.4.refs_4_ = bf16[192,512]{1,0:T(8,128)(2,1)S(1)} collective-permute-done((bf16[192,512]{1,0:T(8,128)(2,1)S(1)}, bf16[192,512]{1,0:T(8,128)(2,1)S(1)}, u32[]{:S(2)}, u32[]{:S(2)}) %collective-permute-start.4) | collective-permute-done | bytes 196640 | tf_op jit(solution)/shard_map/ppermute | solution.py:24
  26.1 3.3 %collective-permute-done.5.refs_5_ = bf16[192,512]{1,0:T(8,128)(2,1)S(1)} collective-permute-done((bf16[192,512]{1,0:T(8,128)(2,1)S(1)}, bf16[192,512]{1,0:T(8,128)(2,1)S(1)}, u32[]{:S(2)}, u32[]{:S(2)}) %collective-permute-start.5) | collective-permute-done | bytes 196640 | tf_op jit(solution)/shard_map/ppermute | solution.py:24
  29.4 3.2 %shard_map.122 = bf16[384,256]{1,0:T(8,128)(2,1)S(1)} custom-call(s32[6]{0:T(128)S(1)} %broadcast_multiply_fusion.bases, bf16[192,256]{1,0:T(8,128)(2,1)S(1)} %get-tuple-element.171.q_own, bf16[192,256]{1,0:T(8,128)(2,1)S(1)} %collective-permute-done.3.q_beside, s32[384,1]{1,0:T(8,128)S(1)} %broadcast_in_dim.45.pos_ref, ...), custom_call_target="tpu_custom_call" | custom-call | flops 452984832 | bytes 1572864 | tf_op jit(solution)/shard_map/pallas_call | solution.py:94
  34.0 3.3 %collective-permute-done.6 = bf16[192,256]{1,0:T(8,128)(2,1)S(1)} collective-permute-done((bf16[192,256]{1,0:T(8,128)(2,1)S(1)}, bf16[192,256]{1,0:T(8,128)(2,1)S(1)}, u32[]{:S(2)}, u32[]{:S(2)}) %collective-permute-start.6) | collective-permute-done | bytes 98336 | tf_op jit(solution)/shard_map/ppermute | solution.py:19
  41.6 2.6 %copy.41 = bf16[2,2048,2,256]{3,1,2,0:T(8,128)(2,1)} copy(bf16[2,2048,2,256]{3,2,1,0:T(2,128)(2,1)S(1)} %copy-done.2) | data formatting | bytes 8388608 | tf_op jit(solution)/shard_map/optimization_barrier | solution.py:329
  44.1 3.1 %collective-permute-done.8 = bf16[48,2048]{1,0:T(8,128)(2,1)S(1)} collective-permute-done((bf16[48,2048]{1,0:T(8,128)(2,1)S(1)}, bf16[48,2048]{1,0:T(8,128)(2,1)S(1)}, u32[]{:S(2)}, u32[]{:S(2)}) %collective-permute-start.8) | collective-permute-done | bytes 196640 | tf_op jit(solution)/shard_map/ppermute | solution.py:28
  48.6 3.8 %collective-permute-start.11 = (bf16[48,2176]{1,0:T(8,128)(2,1)S(1)}, bf16[48,2176]{1,0:T(8,128)(2,1)S(1)}, u32[]{:S(2)}, u32[]{:S(2)}) collective-permute-start(bf16[48,2176]{1,0:T(8,128)(2,1)S(1)} %concatenate.29), channel_id=1, source_target_pairs={{0,24},{4,28},{8,0},{12,4},{16,8},{20,12},{24,16},{28,20},{1,25},{... | collective-permute-start | bytes 626696 | tf_op jit(solution)/shard_map/ppermute | solution.py:24
  53.8 4.7 %collective-permute-done.9.refs_0_ = bf16[48,2176]{1,0:T(8,128)(2,1)S(1)} collective-permute-done((bf16[48,2176]{1,0:T(8,128)(2,1)S(1)}, bf16[48,2176]{1,0:T(8,128)(2,1)S(1)}, u32[]{:S(2)}, u32[]{:S(2)}) %collective-permute-start.9) | collective-permute-done | bytes 208928 | tf_op jit(solution)/shard_map/ppermute | solution.py:24
  60.2 3.5 %collective-permute-start.12 = (bf16[48,1152]{1,0:T(8,128)(2,1)S(1)}, bf16[48,1152]{1,0:T(8,128)(2,1)S(1)}, u32[]{:S(2)}, u32[]{:S(2)}) collective-permute-start(bf16[48,1152]{1,0:T(8,128)(2,1)S(1)} %slice.122), channel_id=1, source_target_pairs={{0,24},{4,28},{8,0},{12,4},{16,8},{20,12},{24,16},{28,20},{1,25},{... | collective-permute-start | bytes 331784 | tf_op jit(solution)/shard_map/ppermute | solution.py:24
  69.8 1.8 %collective-permute-start.22 = (bf16[2,48,1152]{2,1,0:T(8,128)(2,1)S(1)}, bf16[2,48,1152]{2,1,0:T(8,128)(2,1)S(1)}, u32[]{:S(2)}, u32[]{:S(2)}) collective-permute-start(bf16[2,48,1152]{2,1,0:T(8,128)(2,1)S(1)} %pad_maximum_fusion.2), channel_id=1, source_target_pairs={{0,4},{4,0},{8,12},{12,8},{16,20},{20,16},{24,28},{28,24},{1,5},{5... | collective-permute-start | bytes 663560 | tf_op jit(solution)/shard_map/ppermute | solution.py:19
  73.8 2.0 %collective-permute-done.21.refs_4_ = bf16[2,48,1024]{2,1,0:T(8,128)(2,1)S(1)} collective-permute-done((bf16[2,48,1024]{2,1,0:T(8,128)(2,1)S(1)}, bf16[2,48,1024]{2,1,0:T(8,128)(2,1)S(1)}, u32[]{:S(2)}, u32[]{:S(2)}) %collective-permute-start.21) | collective-permute-done | bytes 196640 | tf_op jit(solution)/shard_map/ppermute | solution.py:28
  78.0 1.9 %collective-permute-start.16 = (bf16[2,48,2176]{2,1,0:T(8,128)(2,1)S(1)}, bf16[2,48,2176]{2,1,0:T(8,128)(2,1)S(1)}, u32[]{:S(2)}, u32[]{:S(2)}) collective-permute-start(bf16[2,48,2176]{2,1,0:T(8,128)(2,1)S(1)} %pad_maximum_fusion.1), channel_id=1, source_target_pairs={{0,4},{4,0},{8,12},{12,8},{16,20},{20,16},{24,28},{28,24},{1,5},{5... | collective-permute-start | bytes 1253384 | tf_op jit(solution)/shard_map/ppermute | solution.py:19
  79.9 1.9 %collective-permute-done.18.refs_3_ = bf16[48,1152]{1,0:T(8,128)(2,1)S(1)} collective-permute-done((bf16[48,1152]{1,0:T(8,128)(2,1)S(1)}, bf16[48,1152]{1,0:T(8,128)(2,1)S(1)}, u32[]{:S(2)}, u32[]{:S(2)}) %collective-permute-start.18) | collective-permute-done | bytes 110624 | tf_op jit(solution)/shard_map/ppermute | solution.py:28
  84.7 6.0 %shard_map.123 = (bf16[2,48,1024]{2,1,0:T(8,128)(2,1)S(1)}, bf16[2,48,1024]{2,1,0:T(8,128)(2,1)S(1)}, bf16[2,48,1024]{2,1,0:T(8,128)(2,1)S(1)}, bf16[2,48,1024]{2,1,0:T(8,128)(2,1)S(1)}) custom-call(s32[1]{0:T(128)} %bitcast.19.first, bf16[48,1024]{1,0:T(8,128)(2,1)S(1)} %get-tuple-element.98.refs_0_, bf16[48,1152]{1,0:T(8,128)(2,1)S(1)} %get-tuple-element.99.refs_1_, ...), custom_call_target="tpu_custom_call" | custom-call | flops 2415919104 | bytes 14155776 | tf_op jit(solution)/shard_map/pallas_call | solution.py:212
  92.5 7.9 %shard_map.124 = (bf16[2,48,2048]{2,1,0:T(8,128)(2,1)S(1)}, bf16[2,48,2048]{2,1,0:T(8,128)(2,1)S(1)}, bf16[2,48,2048]{2,1,0:T(8,128)(2,1)S(1)}, bf16[2,48,2048]{2,1,0:T(8,128)(2,1)S(1)}) custom-call(s32[1]{0:T(128)} %bitcast.19.first, bf16[48,2176]{1,0:T(8,128)(2,1)S(1)} %collective-permute-done.9.refs_0_, ...), custom_call_target="tpu_custom_call" | custom-call | flops 4831838208 | bytes 15728640 | tf_op jit(solution)/shard_map/pallas_call | solution.py:212
  103.0 6.0 %shard_map.125 = (bf16[2,48,1024]{2,1,0:T(8,128)(2,1)S(1)}, bf16[2,48,1024]{2,1,0:T(8,128)(2,1)S(1)}, bf16[2,48,1024]{2,1,0:T(8,128)(2,1)S(1)}, bf16[2,48,1024]{2,1,0:T(8,128)(2,1)S(1)}) custom-call(s32[1]{0:T(128)} %bitcast.19.first, bf16[48,1024]{1,0:T(8,128)(2,1)S(1)} %collective-permute-done.10.refs_0_, ...), custom_call_target="tpu_custom_call" | custom-call | flops 2415919104 | bytes 14155776 | tf_op jit(solution)/shard_map/pallas_call | solution.py:212
  113.2 4.8 %collective-permute-done.31 = bf16[2,48,1024]{2,1,0:T(8,128)(2,1)S(1)} collective-permute-done((bf16[2,48,1024]{2,1,0:T(8,128)(2,1)S(1)}, bf16[2,48,1024]{2,1,0:T(8,128)(2,1)S(1)}, u32[]{:S(2)}, u32[]{:S(2)}) %collective-permute-start.31) | collective-permute-done | bytes 196640 | tf_op jit(solution)/shard_map/ppermute | solution.py:28
  125.6 2.1 %collective-permute-start.35 = (bf16[48,1024]{1,0:T(8,128)(2,1)S(1)}, bf16[48,1024]{1,0:T(8,128)(2,1)S(1)}, u32[]{:S(2)}, u32[]{:S(2)}) collective-permute-start(bf16[48,1024]{1,0:T(8,128)(2,1)S(1)} %slice_bitcast_fusion.3), channel_id=1, source_target_pairs={{0,4},{4,0},{8,12},{12,8},{16,20},{20,16},{24,28},{28,24},{1,5},{5... | collective-permute-start | bytes 294920 | tf_op jit(solution)/shard_map/ppermute | solution.py:19
  127.7 2.5 %collective-permute-start.40 = (bf16[48,2048]{1,0:T(8,128)(2,1)S(1)}, bf16[48,2048]{1,0:T(8,128)(2,1)S(1)}, u32[]{:S(2)}, u32[]{:S(2)}) collective-permute-start(bf16[48,2048]{1,0:T(8,128)(2,1)S(1)} %fusion.5), channel_id=1, source_target_pairs={{0,8},{4,12},{8,16},{12,20},{16,24},{20,28},{24,0},{28,4},{1,9},{5... | collective-permute-start | bytes 589832 | tf_op jit(solution)/shard_map/ppermute | solution.py:24
  132.6 2.8 %collective-permute-done.40 = bf16[48,2048]{1,0:T(8,128)(2,1)S(1)} collective-permute-done((bf16[48,2048]{1,0:T(8,128)(2,1)S(1)}, bf16[48,2048]{1,0:T(8,128)(2,1)S(1)}, u32[]{:S(2)}, u32[]{:S(2)}) %collective-permute-start.40) | collective-permute-done | bytes 196640 | tf_op jit(solution)/shard_map/ppermute | solution.py:24
  135.4 2.0 %collective-permute-done.38 = bf16[48,2048]{1,0:T(8,128)(2,1)S(1)} collective-permute-done((bf16[48,2048]{1,0:T(8,128)(2,1)S(1)}, bf16[48,2048]{1,0:T(8,128)(2,1)S(1)}, u32[]{:S(2)}, u32[]{:S(2)}) %collective-permute-start.38) | collective-permute-done | bytes 196640 | tf_op jit(solution)/shard_map/ppermute | solution.py:24
  (148 shorter events, 51.8 us)
Async XLA Ops:
  1.9 10.0 %collective-permute-start = (bf16[192,512]{1,0:T(8,128)(2,1)S(1)}, bf16[192,512]{1,0:T(8,128)(2,1)S(1)}, u32[]{:S(2)}, u32[]{:S(2)}) collective-permute-start(bf16[192,512]{1,0:T(8,128)(2,1)S(1)} %pad_maximum_fusion.4.refs_0_), channel_id=1, source_target_pairs={{0,8},{4,12},{8,16},{12,20},{16,24},{20,28},{24,0},{28,4},{1,9},{5... | collective-permute-start | bytes 589832 | tf_op jit(solution)/shard_map/ppermute | solution.py:24
  5.0 7.3 %collective-permute-start.1 = (bf16[192,512]{1,0:T(8,128)(2,1)S(1)}, bf16[192,512]{1,0:T(8,128)(2,1)S(1)}, u32[]{:S(2)}, u32[]{:S(2)}) collective-permute-start(bf16[192,512]{1,0:T(8,128)(2,1)S(1)} %pad_maximum_fusion.5), channel_id=1, source_target_pairs={{0,4},{4,0},{8,12},{12,8},{16,20},{20,16},{24,28},{28,24},{1,5},{5... | collective-permute-start | bytes 589832 | tf_op jit(solution)/shard_map/ppermute | solution.py:19
  8.2 7.9 %collective-permute-start.3 = (bf16[192,256]{1,0:T(8,128)(2,1)}, bf16[192,256]{1,0:T(8,128)(2,1)S(1)}, u32[]{:S(2)}, u32[]{:S(2)}) collective-permute-start(bf16[192,256]{1,0:T(8,128)(2,1)} %get-tuple-element.170), channel_id=1, source_target_pairs={{0,4},{4,0},{8,12},{12,8},{16,20},{20,16},{24,28},{28,24},{1,5},{5... | collective-permute-start | bytes 294920 | tf_op jit(solution)/shard_map/ppermute | solution.py:19
  12.3 9.6 %collective-permute-start.2 = (bf16[192,512]{1,0:T(8,128)(2,1)S(1)}, bf16[192,512]{1,0:T(8,128)(2,1)S(1)}, u32[]{:S(2)}, u32[]{:S(2)}) collective-permute-start(bf16[192,512]{1,0:T(8,128)(2,1)S(1)} %collective-permute-done.1.refs_1_), channel_id=1, source_target_pairs={{0,8},{4,12},{8,16},{12,20},{16,24},{20,28},{24,0},{28,4},{1,9},{5... | collective-permute-start | bytes 589832 | tf_op jit(solution)/shard_map/ppermute | solution.py:24
  14.6 11.5 %collective-permute-start.4 = (bf16[192,512]{1,0:T(8,128)(2,1)S(1)}, bf16[192,512]{1,0:T(8,128)(2,1)S(1)}, u32[]{:S(2)}, u32[]{:S(2)}) collective-permute-start(bf16[192,512]{1,0:T(8,128)(2,1)S(1)} %collective-permute-done.refs_2_), channel_id=1, source_target_pairs={{0,8},{4,12},{8,16},{12,20},{16,24},{20,28},{24,0},{28,4},{1,9},{5... | collective-permute-start | bytes 589832 | tf_op jit(solution)/shard_map/ppermute | solution.py:24
  21.9 7.5 %collective-permute-start.5 = (bf16[192,512]{1,0:T(8,128)(2,1)S(1)}, bf16[192,512]{1,0:T(8,128)(2,1)S(1)}, u32[]{:S(2)}, u32[]{:S(2)}) collective-permute-start(bf16[192,512]{1,0:T(8,128)(2,1)S(1)} %collective-permute-done.2.refs_3_), channel_id=1, source_target_pairs={{0,8},{4,12},{8,16},{12,20},{16,24},{20,28},{24,0},{28,4},{1,9},{5... | collective-permute-start | bytes 589832 | tf_op jit(solution)/shard_map/ppermute | solution.py:24
  47.2 37.4 %collective-permute-start.23 = (bf16[2,2,2048,256]{3,2,1,0:T(8,128)(2,1)}, bf16[2,2,2048,256]{3,2,1,0:T(8,128)(2,1)}, u32[]{:S(2)}, u32[]{:S(2)}) collective-permute-start(bf16[2,2,2048,256]{3,2,1,0:T(8,128)(2,1)} %bitcast.65.refs_6_), channel_id=1, source_target_pairs={{0,1},{1,0},{2,3},{3,2},{4,5},{5,4},{6,7},{7,6},{8,9},{9,8},{10,11... | collective-permute-start | bytes 12582920 | tf_op jit(solution)/shard_map/ppermute | solution.py:32
  47.5 35.5 %collective-permute-start.24 = (bf16[2,256,2048]{2,1,0:T(8,128)(2,1)}, bf16[2,256,2048]{2,1,0:T(8,128)(2,1)}, u32[]{:S(2)}, u32[]{:S(2)}) collective-permute-start(bf16[2,256,2048]{2,1,0:T(8,128)(2,1)} %refs_8_.2), channel_id=1, source_target_pairs={{0,1},{1,0},{2,3},{3,2},{4,5},{5,4},{6,7},{7,6},{8,9},{9,8},{10,11... | collective-permute-start | bytes 6291464 | tf_op jit(solution)/shard_map/ppermute | solution.py:32
  48.5 9.9 %collective-permute-start.9 = (bf16[48,2176]{1,0:T(8,128)(2,1)S(1)}, bf16[48,2176]{1,0:T(8,128)(2,1)S(1)}, u32[]{:S(2)}, u32[]{:S(2)}) collective-permute-start(bf16[48,2176]{1,0:T(8,128)(2,1)S(1)} %concatenate.29), channel_id=1, source_target_pairs={{0,8},{4,12},{8,16},{12,20},{16,24},{20,28},{24,0},{28,4},{1,9},{5... | collective-permute-start | bytes 626696 | tf_op jit(solution)/shard_map/ppermute | solution.py:24
  48.6 11.6 %collective-permute-start.11 = (bf16[48,2176]{1,0:T(8,128)(2,1)S(1)}, bf16[48,2176]{1,0:T(8,128)(2,1)S(1)}, u32[]{:S(2)}, u32[]{:S(2)}) collective-permute-start(bf16[48,2176]{1,0:T(8,128)(2,1)S(1)} %concatenate.29), channel_id=1, source_target_pairs={{0,24},{4,28},{8,0},{12,4},{16,8},{20,12},{24,16},{28,20},{1,25},{... | collective-permute-start | bytes 626696 | tf_op jit(solution)/shard_map/ppermute | solution.py:24
  52.4 7.3 %collective-permute-start.19 = (bf16[48,1024]{1,0:T(8,128)(2,1)S(1)}, bf16[48,1024]{1,0:T(8,128)(2,1)S(1)}, u32[]{:S(2)}, u32[]{:S(2)}) collective-permute-start(bf16[48,1024]{1,0:T(8,128)(2,1)S(1)} %get-tuple-element.98.refs_0_), channel_id=1, source_target_pairs={{0,4},{4,0},{8,12},{12,8},{16,20},{20,16},{24,28},{28,24},{1,5},{5... | collective-permute-start | bytes 294920 | tf_op jit(solution)/shard_map/ppermute | solution.py:19
  60.2 7.2 %collective-permute-start.12 = (bf16[48,1152]{1,0:T(8,128)(2,1)S(1)}, bf16[48,1152]{1,0:T(8,128)(2,1)S(1)}, u32[]{:S(2)}, u32[]{:S(2)}) collective-permute-start(bf16[48,1152]{1,0:T(8,128)(2,1)S(1)} %slice.122), channel_id=1, source_target_pairs={{0,24},{4,28},{8,0},{12,4},{16,8},{20,12},{24,16},{28,20},{1,25},{... | collective-permute-start | bytes 331784 | tf_op jit(solution)/shard_map/ppermute | solution.py:24
  67.4 8.5 %collective-permute-start.21 = (bf16[2,48,1024]{2,1,0:T(8,128)(2,1)S(1)}, bf16[2,48,1024]{2,1,0:T(8,128)(2,1)S(1)}, u32[]{:S(2)}, u32[]{:S(2)}) collective-permute-start(bf16[2,48,1024]{2,1,0:T(8,128)(2,1)S(1)} %pad_maximum_fusion.6), channel_id=1, source_target_pairs={{0,2},{1,3},{2,0},{3,1},{4,6},{5,7},{6,4},{7,5},{8,10},{9,11},{10,... | collective-permute-start | bytes 589832 | tf_op jit(solution)/shard_map/ppermute | solution.py:28
  77.0 13.7 %collective-permute-start.15 = (bf16[2,48,2176]{2,1,0:T(8,128)(2,1)S(1)}, bf16[2,48,2176]{2,1,0:T(8,128)(2,1)S(1)}, u32[]{:S(2)}, u32[]{:S(2)}) collective-permute-start(bf16[2,48,2176]{2,1,0:T(8,128)(2,1)S(1)} %pad_maximum_fusion), channel_id=1, source_target_pairs={{0,2},{1,3},{2,0},{3,1},{4,6},{5,7},{6,4},{7,5},{8,10},{9,11},{10,... | collective-permute-start | bytes 1253384 | tf_op jit(solution)/shard_map/ppermute | solution.py:28
  78.0 12.7 %collective-permute-start.16 = (bf16[2,48,2176]{2,1,0:T(8,128)(2,1)S(1)}, bf16[2,48,2176]{2,1,0:T(8,128)(2,1)S(1)}, u32[]{:S(2)}, u32[]{:S(2)}) collective-permute-start(bf16[2,48,2176]{2,1,0:T(8,128)(2,1)S(1)} %pad_maximum_fusion.1), channel_id=1, source_target_pairs={{0,4},{4,0},{8,12},{12,8},{16,20},{20,16},{24,28},{28,24},{1,5},{5... | collective-permute-start | bytes 1253384 | tf_op jit(solution)/shard_map/ppermute | solution.py:19
  81.9 18.7 %collective-permute-start.27 = (bf16[2,48,1024]{2,1,0:T(8,128)(2,1)S(1)}, bf16[2,48,1024]{2,1,0:T(8,128)(2,1)S(1)}, u32[]{:S(2)}, u32[]{:S(2)}) collective-permute-start(bf16[2,48,1024]{2,1,0:T(8,128)(2,1)S(1)} %pad_maximum_fusion.7), channel_id=1, source_target_pairs={{0,2},{1,3},{2,0},{3,1},{4,6},{5,7},{6,4},{7,5},{8,10},{9,11},{10,... | collective-permute-start | bytes 589832 | tf_op jit(solution)/shard_map/ppermute | solution.py:28
  83.0 17.6 %collective-permute-start.28 = (bf16[2,48,1152]{2,1,0:T(8,128)(2,1)S(1)}, bf16[2,48,1152]{2,1,0:T(8,128)(2,1)S(1)}, u32[]{:S(2)}, u32[]{:S(2)}) collective-permute-start(bf16[2,48,1152]{2,1,0:T(8,128)(2,1)S(1)} %pad_maximum_fusion.3), channel_id=1, source_target_pairs={{0,4},{4,0},{8,12},{12,8},{16,20},{20,16},{24,28},{28,24},{1,5},{5... | collective-permute-start | bytes 663560 | tf_op jit(solution)/shard_map/ppermute | solution.py:19
  90.7 9.8 %collective-permute-start.25 = (bf16[2,48,1024]{2,1,0:T(8,128)(2,1)S(1)}, bf16[2,48,1024]{2,1,0:T(8,128)(2,1)S(1)}, u32[]{:S(2)}, u32[]{:S(2)}) collective-permute-start(bf16[2,48,1024]{2,1,0:T(8,128)(2,1)S(1)} %get-tuple-element.111), channel_id=1, source_target_pairs={{0,2},{1,3},{2,0},{3,1},{4,6},{5,7},{6,4},{7,5},{8,10},{9,11},{10,... | collective-permute-start | bytes 589832 | tf_op jit(solution)/shard_map/ppermute | solution.py:28
  91.6 8.9 %collective-permute-start.26 = (bf16[2,48,1024]{2,1,0:T(8,128)(2,1)S(1)}, bf16[2,48,1024]{2,1,0:T(8,128)(2,1)S(1)}, u32[]{:S(2)}, u32[]{:S(2)}) collective-permute-start(bf16[2,48,1024]{2,1,0:T(8,128)(2,1)S(1)} %get-tuple-element.113), channel_id=1, source_target_pairs={{0,4},{4,0},{8,12},{12,8},{16,20},{20,16},{24,28},{28,24},{1,5},{5... | collective-permute-start | bytes 589832 | tf_op jit(solution)/shard_map/ppermute | solution.py:19
  100.6 9.8 %collective-permute-start.29 = (bf16[2,48,2048]{2,1,0:T(8,128)(2,1)S(1)}, bf16[2,48,2048]{2,1,0:T(8,128)(2,1)S(1)}, u32[]{:S(2)}, u32[]{:S(2)}) collective-permute-start(bf16[2,48,2048]{2,1,0:T(8,128)(2,1)S(1)} %get-tuple-element.145), channel_id=1, source_target_pairs={{0,2},{1,3},{2,0},{3,1},{4,6},{5,7},{6,4},{7,5},{8,10},{9,11},{10,... | collective-permute-start | bytes 1179656 | tf_op jit(solution)/shard_map/ppermute | solution.py:28
  102.2 9.1 %collective-permute-start.30 = (bf16[2,48,2048]{2,1,0:T(8,128)(2,1)S(1)}, bf16[2,48,2048]{2,1,0:T(8,128)(2,1)S(1)}, u32[]{:S(2)}, u32[]{:S(2)}) collective-permute-start(bf16[2,48,2048]{2,1,0:T(8,128)(2,1)S(1)} %get-tuple-element.147), channel_id=1, source_target_pairs={{0,4},{4,0},{8,12},{12,8},{16,20},{20,16},{24,28},{28,24},{1,5},{5... | collective-permute-start | bytes 1179656 | tf_op jit(solution)/shard_map/ppermute | solution.py:19
  121.3 8.9 %collective-permute-start.37 = (bf16[48,2048]{1,0:T(8,128)(2,1)S(1)}, bf16[48,2048]{1,0:T(8,128)(2,1)S(1)}, u32[]{:S(2)}, u32[]{:S(2)}) collective-permute-start(bf16[48,2048]{1,0:T(8,128)(2,1)S(1)} %slice_bitcast_fusion.1), channel_id=1, source_target_pairs={{0,4},{4,0},{8,12},{12,8},{16,20},{20,16},{24,28},{28,24},{1,5},{5... | collective-permute-start | bytes 589832 | tf_op jit(solution)/shard_map/ppermute | solution.py:19
  123.9 8.7 %collective-permute-start.41 = (bf16[48,2048]{1,0:T(8,128)(2,1)S(1)}, bf16[48,2048]{1,0:T(8,128)(2,1)S(1)}, u32[]{:S(2)}, u32[]{:S(2)}) collective-permute-start(bf16[48,2048]{1,0:T(8,128)(2,1)S(1)} %pad_maximum_fusion.8), channel_id=1, source_target_pairs={{0,16},{4,20},{8,24},{12,28},{16,0},{20,4},{24,8},{28,12},{1,17},{... | collective-permute-start | bytes 589832 | tf_op jit(solution)/shard_map/ppermute | solution.py:24
  127.7 7.7 %collective-permute-start.40 = (bf16[48,2048]{1,0:T(8,128)(2,1)S(1)}, bf16[48,2048]{1,0:T(8,128)(2,1)S(1)}, u32[]{:S(2)}, u32[]{:S(2)}) collective-permute-start(bf16[48,2048]{1,0:T(8,128)(2,1)S(1)} %fusion.5), channel_id=1, source_target_pairs={{0,8},{4,12},{8,16},{12,20},{16,24},{20,28},{24,0},{28,4},{1,9},{5... | collective-permute-start | bytes 589832 | tf_op jit(solution)/shard_map/ppermute | solution.py:24
  (27 other events, 250.9 us)

commit v5 on v4

--- a/solution.py
+++ b/solution.py
@@ -22,6 +22,11 @@
 def over_z(a, step):
     count = lax.axis_size("seq")
     return lax.ppermute(a, "seq", [(i, (i + 2 * step) % count) for i in range(count)])
+
+
+def across_z(a, k):
+    count = lax.axis_size("seq")
+    return lax.ppermute(a, "seq", [(i, i ^ (2 * k)) for i in range(count)])
 
 
 def over_x(a):
@@ -105,7 +110,7 @@
     )(bases, q, beside, pos, start, *blocks)
 
 
-def attention(queries, keys, values, lengths, seq, x, core):
+def attention(queries, keys, values, lengths, seq, x, core, held):
     ring = lax.axis_size("seq") // 2
     y, z = seq % 2, seq // 2
     rows, width = queries.shape
@@ -137,8 +142,9 @@
     pos = jnp.concatenate([seq * rows + local, (seq ^ 1) * rows + local])
     bounds = jnp.cumsum(lengths)
     start = jnp.max(jnp.where(bounds[None, :] <= pos[:, None], bounds[None, :], 0), axis=1)
+    blocks, held = lax.optimization_barrier((blocks, held))
     out = attend(q_own, q_beside, pos[:, None], start[:, None], bases, blocks)
-    return out[:rows], over_y(out[rows:])
+    return out[:rows], over_y(out[rows:]), held
 
 
 def expert_kernel(layout, ways, count, first, *refs):
@@ -260,15 +266,16 @@
     return a, b, y_a, x_b, over_x(jnp.stack([a, y_a])), over_y(jnp.stack([b, x_b]))
 
 
+def partners():
+    return [(3, 1)] + [(k, k + 1) for k in range(4, lax.axis_size("seq") // 2, 2)]
+
+
 def gather_tokens(unit, use_halves, use_groups):
-    half = lax.axis_size("seq") // 4
     middle = (unit.shape[1] - 128) // 2
     own = plane_first(unit[:, :middle], unit[:, middle:])
-    up, down, pairs = unit, unit, []
-    for _ in range(1, half):
-        up, down = over_z(up, 1), over_z(down, -1)
-        pairs.append((up, down))
-    far_a, far_b = over_z(up[:, :middle], 1), over_z(down[:, middle:], -1)
+    pairs = [[across_z(unit, k) for k in pair] for pair in partners()]
+    relayed = pairs[0][0]
+    far_a, far_b = across_z(relayed[:, :middle], 1), across_z(relayed[:, middle:], 1)
     own = plane_second(*own)
     pairs = [plane_first(*pair) for pair in pairs]
     far_a, far_b, pairs = lax.optimization_barrier((far_a, far_b, pairs))
@@ -285,12 +292,12 @@
     pairs = [scatter_first(*pair) for pair in pairs]
     far = use_halves(far)
     far, pairs = lax.optimization_barrier((far, pairs))
+    pairs = [scatter_second(*pair) for pair in pairs]
     far = scatter_first(*far)
-    far, pairs = lax.optimization_barrier((far, pairs))
+    own = scatter_second(*own)
+    far, own, pairs = lax.optimization_barrier((far, own, pairs))
     far = scatter_second(*far)
-    pairs = [scatter_second(*pair) for pair in pairs]
-    own, far = lax.optimization_barrier((own, far))
-    return scatter_second(*own), far, pairs
+    return own, far, pairs
 
 
 def scatter_first(a_keep, a_send, b_keep, b_send):
@@ -302,11 +309,11 @@
 
 
 def mix(own, far, pairs):
-    half = lax.axis_size("seq") // 4
     total = jnp.concatenate(own, 1).astype(F32)
-    for k, (low, high) in enumerate(pairs):
-        total = total + over_z(low, -1 - k).astype(F32) + over_z(high, 1 + k).astype(F32)
-    return (total + over_z(jnp.concatenate(far, 1), half).astype(F32)).astype(BF16)
+    for pair, ways in zip(pairs, partners()):
+        for part, k in zip(pair, ways):
+            total = total + across_z(part, k).astype(F32)
+    return (total + across_z(jnp.concatenate(far, 1), 2).astype(F32)).astype(BF16)
 
 
 def shards(
@@ -318,7 +325,9 @@
     owned = w_gate_up.shape[0]
     count = owned * lax.axis_size("seq")
 
-    own, other = attention(queries, keys, values, lengths, seq, x, core)
+    own, other, down_other = attention(
+        queries, keys, values, lengths, seq, x, core, over_core(w_down)
+    )
     heads = jnp.where(
         y == 0, jnp.concatenate([own, other], 1), jnp.concatenate([other, own], 1)
     )
@@ -338,8 +347,8 @@
     packed = jnp.concatenate([high, low, jnp.zeros((rows, pad), BF16)], 1)
 
     arrived = over_x(partial[rows:].astype(BF16))
-    arrived, w_in, w_down = lax.optimization_barrier((arrived, w_in, w_down))
-    weights = (w_in, over_core(w_in)), (w_down, over_core(w_down))
+    arrived, w_in = lax.optimization_barrier((arrived, w_in))
+    weights = (w_in, over_core(w_in)), (w_down, down_other)
     attended = (resid.astype(F32) + partial[:rows] + arrived.astype(F32)).astype(BF16)
     widened = attended.astype(F32)
     meansq = jnp.mean(widened * widened, axis=1, keepdims=True)

time: 138 us -> 136 us (0.986)
  starting transfers between devices: 53.2 us -> 45.9 us
  waiting for transfers between devices: 50.8 us -> 55.6 us
    ppermute x0 -> x7, waiting for transfers between devices: none -> 13.2 us  [across_z(): return lax.ppermute(a, 'seq', [(i, i ^ 2 * k) for i in range(count)])]
    ppermute x11 -> x4, starting transfers between devices: 18.7 us -> 5.91 us  [over_z(): lax.ppermute(a, 'seq', [(i, (i + 2 * step) % count) for i in range(count)])]
    ppermute x11 -> x4, waiting for transfers between devices: 28 us -> 16.7 us  [over_z(): lax.ppermute(a, 'seq', [(i, (i + 2 * step) % count) for i in range(count)])]
    ppermute x0 -> x7, starting transfers between devices: none -> 4.63 us  [across_z(): return lax.ppermute(a, 'seq', [(i, i ^ 2 * k) for i in range(count)])]
    ppermute x15, waiting for transfers between devices: 6.77 us -> 10.6 us  [over_y(): return lax.ppermute(a, 'seq', [(i, i ^ 1) for i in range(count)])]
    ppermute x13, starting transfers between devices: 13.9 us -> 17.1 us  [over_x(): return lax.ppermute(a, 'tp', [(i, i ^ 2) for i in range(4)])]
    ppermute x15, starting transfers between devices: 19.9 us -> 17.7 us  [over_y(): return lax.ppermute(a, 'seq', [(i, i ^ 1) for i in range(count)])]
  transfers between devices with their start and end apart: 42 -> 42, of which waited for: 24 -> 24; matrix products, arithmetic and copies ran while one was open for 5% -> 6% of each run, Pallas kernels for 14% -> 15%
where the time goes in v5:
time: 136 us
  waiting for transfers between devices  55.6 us (41%)
  starting transfers between devices  45.9 us (34%)
  Pallas kernels  23.2 us (17%)
  local copies, waits for them, and re-layouts  4.48 us (3%)
  other arithmetic  4.22 us (3%)
    pallas_call x3, Pallas kernels, experts(): pl.pallas_call(functools.partial(expert_kernel, layout, ways, count), out...  20 us
    ppermute x15, starting transfers between devices, over_y(): return lax.ppermute(a, 'seq', [(i, i ^ 1) for i in range(count)])  17.7 us
    ppermute x13, starting transfers between devices, over_x(): return lax.ppermute(a, 'tp', [(i, i ^ 2) for i in range(4)])  17.1 us
    ppermute x4, waiting for transfers between devices, over_z(): lax.ppermute(a, 'seq', [(i, (i + 2 * step) % count) for i in range(count)])  16.7 us
    ppermute x13, waiting for transfers between devices, over_x(): return lax.ppermute(a, 'tp', [(i, i ^ 2) for i in range(4)])  13.2 us
    ppermute x7, waiting for transfers between devices, across_z(): return lax.ppermute(a, 'seq', [(i, i ^ 2 * k) for i in range(count)])  13.2 us
    ppermute x15, waiting for transfers between devices, over_y(): return lax.ppermute(a, 'seq', [(i, i ^ 1) for i in range(count)])  10.6 us
    ppermute x4, starting transfers between devices, over_z(): lax.ppermute(a, 'seq', [(i, (i + 2 * step) % count) for i in range(count)])  5.91 us
  transfers between devices with their start and end apart: 42, of which 24 were waited for; matrix products, arithmetic and copies ran while one was open for 6% of the time, Pallas kernels for 15%

profile of v5, /device:TPU:0, one launch (start us, length us, event | category | flops | bytes accessed | tf_op | source)
XLA Modules:
  0.0 135.5 jit_solution(12088153449690498343)
XLA Ops:
  2.3 2.7 %collective-permute-start = (bf16[192,512]{1,0:T(8,128)(2,1)S(1)}, bf16[192,512]{1,0:T(8,128)(2,1)S(1)}, u32[]{:S(2)}, u32[]{:S(2)}) collective-permute-start(bf16[192,512]{1,0:T(8,128)(2,1)S(1)} %pad_maximum_fusion.4.refs_0_), channel_id=1, source_target_pairs={{0,8},{4,12},{8,16},{12,20},{16,24},{20,28},{24,0},{28,4},{1,9},{5... | collective-permute-start | bytes 589832 | tf_op jit(solution)/shard_map/ppermute | solution.py:24
  9.2 3.3 %collective-permute-done.refs_2_ = bf16[192,512]{1,0:T(8,128)(2,1)S(1)} collective-permute-done((bf16[192,512]{1,0:T(8,128)(2,1)S(1)}, bf16[192,512]{1,0:T(8,128)(2,1)S(1)}, u32[]{:S(2)}, u32[]{:S(2)}) %collective-permute-start) | collective-permute-done | bytes 196640 | tf_op jit(solution)/shard_map/ppermute | solution.py:24
  16.5 6.0 %collective-permute-done.2.refs_3_ = bf16[192,512]{1,0:T(8,128)(2,1)S(1)} collective-permute-done((bf16[192,512]{1,0:T(8,128)(2,1)S(1)}, bf16[192,512]{1,0:T(8,128)(2,1)S(1)}, u32[]{:S(2)}, u32[]{:S(2)}) %collective-permute-start.2) | collective-permute-done | bytes 196640 | tf_op jit(solution)/shard_map/ppermute | solution.py:24
  22.5 3.8 %collective-permute-done.4.refs_4_ = bf16[192,512]{1,0:T(8,128)(2,1)S(1)} collective-permute-done((bf16[192,512]{1,0:T(8,128)(2,1)S(1)}, bf16[192,512]{1,0:T(8,128)(2,1)S(1)}, u32[]{:S(2)}, u32[]{:S(2)}) %collective-permute-start.4) | collective-permute-done | bytes 196640 | tf_op jit(solution)/shard_map/ppermute | solution.py:24
  26.3 3.6 %collective-permute-done.5.refs_5_ = bf16[192,512]{1,0:T(8,128)(2,1)S(1)} collective-permute-done((bf16[192,512]{1,0:T(8,128)(2,1)S(1)}, bf16[192,512]{1,0:T(8,128)(2,1)S(1)}, u32[]{:S(2)}, u32[]{:S(2)}) %collective-permute-start.5) | collective-permute-done | bytes 196640 | tf_op jit(solution)/shard_map/ppermute | solution.py:24
  29.9 3.3 %shard_map.122 = bf16[384,256]{1,0:T(8,128)(2,1)S(1)} custom-call(s32[6]{0:T(128)S(1)} %broadcast_multiply_fusion.bases, bf16[192,256]{1,0:T(8,128)(2,1)S(1)} %get-tuple-element.179.q_own, bf16[192,256]{1,0:T(8,128)(2,1)S(1)} %collective-permute-done.3.q_beside, s32[384,1]{1,0:T(8,128)S(1)} %broadcast_in_dim.45.pos_ref, ...), custom_call_target="tpu_custom_call" | custom-call | flops 452984832 | bytes 1572864 | tf_op jit(solution)/shard_map/pallas_call | solution.py:99
  34.8 3.1 %collective-permute-done.7 = bf16[192,256]{1,0:T(8,128)(2,1)S(1)} collective-permute-done((bf16[192,256]{1,0:T(8,128)(2,1)S(1)}, bf16[192,256]{1,0:T(8,128)(2,1)S(1)}, u32[]{:S(2)}, u32[]{:S(2)}) %collective-permute-start.7) | collective-permute-done | bytes 98336 | tf_op jit(solution)/shard_map/ppermute | solution.py:19
  42.4 2.6 %copy.41 = bf16[2,2048,2,256]{3,1,2,0:T(8,128)(2,1)} copy(bf16[2,2048,2,256]{3,2,1,0:T(2,128)(2,1)S(1)} %copy-done.2) | data formatting | bytes 8388608 | tf_op jit(solution)/shard_map/optimization_barrier | solution.py:338
  45.0 2.9 %collective-permute-done.9 = bf16[48,2048]{1,0:T(8,128)(2,1)S(1)} collective-permute-done((bf16[48,2048]{1,0:T(8,128)(2,1)S(1)}, bf16[48,2048]{1,0:T(8,128)(2,1)S(1)}, u32[]{:S(2)}, u32[]{:S(2)}) %collective-permute-start.9) | collective-permute-done | bytes 196640 | tf_op jit(solution)/shard_map/ppermute | solution.py:33
  51.9 2.1 %collective-permute-done.18.refs_2_ = bf16[48,1024]{1,0:T(8,128)(2,1)S(1)} collective-permute-done((bf16[48,1024]{1,0:T(8,128)(2,1)S(1)}, bf16[48,1024]{1,0:T(8,128)(2,1)S(1)}, u32[]{:S(2)}, u32[]{:S(2)}) %collective-permute-start.18) | collective-permute-done | bytes 98336 | tf_op jit(solution)/shard_map/ppermute | solution.py:19
  54.0 4.4 %collective-permute-done.10.refs_0_ = bf16[48,2176]{1,0:T(8,128)(2,1)S(1)} collective-permute-done((bf16[48,2176]{1,0:T(8,128)(2,1)S(1)}, bf16[48,2176]{1,0:T(8,128)(2,1)S(1)}, u32[]{:S(2)}, u32[]{:S(2)}) %collective-permute-start.10) | collective-permute-done | bytes 208928 | tf_op jit(solution)/shard_map/ppermute | solution.py:29
  58.8 1.8 %collective-permute-start.11 = (bf16[48,1024]{1,0:T(8,128)(2,1)S(1)}, bf16[48,1024]{1,0:T(8,128)(2,1)S(1)}, u32[]{:S(2)}, u32[]{:S(2)}) collective-permute-start(bf16[48,1024]{1,0:T(8,128)(2,1)S(1)} %slice.121), channel_id=1, source_target_pairs={{0,8},{4,12},{8,0},{12,4},{16,24},{20,28},{24,16},{28,20},{1,9},{5... | collective-permute-start | bytes 294920 | tf_op jit(solution)/shard_map/ppermute | solution.py:29
  77.7 6.0 %shard_map.123 = (bf16[2,48,1024]{2,1,0:T(8,128)(2,1)S(1)}, bf16[2,48,1024]{2,1,0:T(8,128)(2,1)S(1)}, bf16[2,48,1024]{2,1,0:T(8,128)(2,1)S(1)}, bf16[2,48,1024]{2,1,0:T(8,128)(2,1)S(1)}) custom-call(s32[1]{0:T(128)} %bitcast.15.first, bf16[48,1024]{1,0:T(8,128)(2,1)S(1)} %get-tuple-element.112.refs_0_, bf16[48,1152]{1,0:T(8,128)(2,1)S(1)} %get-tuple-element.113.refs_1_, ...), custom_call_target="tpu_custom_call" | custom-call | flops 2415919104 | bytes 14155776 | tf_op jit(solution)/shard_map/pallas_call | solution.py:218
  83.8 2.2 %collective-permute-done.25.refs_5_ = bf16[2,48,2176]{2,1,0:T(8,128)(2,1)S(1)} collective-permute-done((bf16[2,48,2176]{2,1,0:T(8,128)(2,1)S(1)}, bf16[2,48,2176]{2,1,0:T(8,128)(2,1)S(1)}, u32[]{:S(2)}, u32[]{:S(2)}) %collective-permute-start.25) | collective-permute-done | bytes 417824 | tf_op jit(solution)/shard_map/ppermute | solution.py:19
  87.3 2.1 %collective-permute-start.27 = (bf16[2,48,1024]{2,1,0:T(8,128)(2,1)S(1)}, bf16[2,48,1024]{2,1,0:T(8,128)(2,1)S(1)}, u32[]{:S(2)}, u32[]{:S(2)}) collective-permute-start(bf16[2,48,1024]{2,1,0:T(8,128)(2,1)S(1)} %get-tuple-element.125), channel_id=1, source_target_pairs={{0,2},{1,3},{2,0},{3,1},{4,6},{5,7},{6,4},{7,5},{8,10},{9,11},{10,... | collective-permute-start | bytes 589832 | tf_op jit(solution)/shard_map/ppermute | solution.py:33
  89.4 7.9 %shard_map.124 = (bf16[2,48,2048]{2,1,0:T(8,128)(2,1)S(1)}, bf16[2,48,2048]{2,1,0:T(8,128)(2,1)S(1)}, bf16[2,48,2048]{2,1,0:T(8,128)(2,1)S(1)}, bf16[2,48,2048]{2,1,0:T(8,128)(2,1)S(1)}) custom-call(s32[1]{0:T(128)} %bitcast.15.first, bf16[48,2176]{1,0:T(8,128)(2,1)S(1)} %collective-permute-done.10.refs_0_, ...), custom_call_target="tpu_custom_call" | custom-call | flops 4831838208 | bytes 15728640 | tf_op jit(solution)/shard_map/pallas_call | solution.py:218
  98.4 2.1 %collective-permute-start.34 = (bf16[48,1024]{1,0:T(8,128)(2,1)S(1)}, bf16[48,1024]{1,0:T(8,128)(2,1)S(1)}, u32[]{:S(2)}, u32[]{:S(2)}) collective-permute-start(bf16[48,1024]{1,0:T(8,128)(2,1)S(1)} %slice_bitcast_fusion.4), channel_id=1, source_target_pairs={{0,2},{1,3},{2,0},{3,1},{4,6},{5,7},{6,4},{7,5},{8,10},{9,11},{10,... | collective-permute-start | bytes 294920 | tf_op jit(solution)/shard_map/ppermute | solution.py:33
  101.8 6.0 %shard_map.125 = (bf16[2,48,1024]{2,1,0:T(8,128)(2,1)S(1)}, bf16[2,48,1024]{2,1,0:T(8,128)(2,1)S(1)}, bf16[2,48,1024]{2,1,0:T(8,128)(2,1)S(1)}, bf16[2,48,1024]{2,1,0:T(8,128)(2,1)S(1)}) custom-call(s32[1]{0:T(128)} %bitcast.15.first, bf16[48,1024]{1,0:T(8,128)(2,1)S(1)} %collective-permute-done.11.refs_0_, ...), custom_call_target="tpu_custom_call" | custom-call | flops 2415919104 | bytes 14155776 | tf_op jit(solution)/shard_map/pallas_call | solution.py:218
  107.8 3.4 %collective-permute-done.34 = bf16[48,1024]{1,0:T(8,128)(2,1)S(1)} collective-permute-done((bf16[48,1024]{1,0:T(8,128)(2,1)S(1)}, bf16[48,1024]{1,0:T(8,128)(2,1)S(1)}, u32[]{:S(2)}, u32[]{:S(2)}) %collective-permute-start.34) | collective-permute-done | bytes 98336 | tf_op jit(solution)/shard_map/ppermute | solution.py:33
  113.7 2.0 %collective-permute-start.31 = (bf16[2,48,1024]{2,1,0:T(8,128)(2,1)S(1)}, bf16[2,48,1024]{2,1,0:T(8,128)(2,1)S(1)}, u32[]{:S(2)}, u32[]{:S(2)}) collective-permute-start(bf16[2,48,1024]{2,1,0:T(8,128)(2,1)S(1)} %get-tuple-element.157), channel_id=1, source_target_pairs={{0,2},{1,3},{2,0},{3,1},{4,6},{5,7},{6,4},{7,5},{8,10},{9,11},{10,... | collective-permute-start | bytes 589832 | tf_op jit(solution)/shard_map/ppermute | solution.py:33
  115.7 2.4 %collective-permute-done.36 = bf16[48,2048]{1,0:T(8,128)(2,1)S(1)} collective-permute-done((bf16[48,2048]{1,0:T(8,128)(2,1)S(1)}, bf16[48,2048]{1,0:T(8,128)(2,1)S(1)}, u32[]{:S(2)}, u32[]{:S(2)}) %collective-permute-start.36) | collective-permute-done | bytes 196640 | tf_op jit(solution)/shard_map/ppermute | solution.py:33
  127.5 3.0 %collective-permute-done.37 = bf16[48,2048]{1,0:T(8,128)(2,1)S(1)} collective-permute-done((bf16[48,2048]{1,0:T(8,128)(2,1)S(1)}, bf16[48,2048]{1,0:T(8,128)(2,1)S(1)}, u32[]{:S(2)}, u32[]{:S(2)}) %collective-permute-start.37) | collective-permute-done | bytes 196640 | tf_op jit(solution)/shard_map/ppermute | solution.py:29
  130.5 2.4 %collective-permute-done.38 = bf16[48,2048]{1,0:T(8,128)(2,1)S(1)} collective-permute-done((bf16[48,2048]{1,0:T(8,128)(2,1)S(1)}, bf16[48,2048]{1,0:T(8,128)(2,1)S(1)}, u32[]{:S(2)}, u32[]{:S(2)}) %collective-permute-start.38) | collective-permute-done | bytes 196640 | tf_op jit(solution)/shard_map/ppermute | solution.py:29
  132.9 1.8 %collective-permute-done.41 = bf16[48,2048]{1,0:T(8,128)(2,1)S(1)} collective-permute-done((bf16[48,2048]{1,0:T(8,128)(2,1)S(1)}, bf16[48,2048]{1,0:T(8,128)(2,1)S(1)}, u32[]{:S(2)}, u32[]{:S(2)}) %collective-permute-start.41) | collective-permute-done | bytes 196640 | tf_op jit(solution)/shard_map/ppermute | solution.py:29
  (148 shorter events, 53.4 us)
Async XLA Ops:
  0.7 29.3 %collective-permute-start.6 = (bf16[2,256,2048]{2,1,0:T(8,128)(2,1)}, bf16[2,256,2048]{2,1,0:T(8,128)(2,1)}, u32[]{:S(2)}, u32[]{:S(2)}) collective-permute-start(bf16[2,256,2048]{2,1,0:T(8,128)(2,1)} %refs_8_.5), channel_id=1, source_target_pairs={{0,1},{1,0},{2,3},{3,2},{4,5},{5,4},{6,7},{7,6},{8,9},{9,8},{10,11... | collective-permute-start | bytes 6291464 | tf_op jit(solution)/shard_map/ppermute | solution.py:37
  2.3 10.2 %collective-permute-start = (bf16[192,512]{1,0:T(8,128)(2,1)S(1)}, bf16[192,512]{1,0:T(8,128)(2,1)S(1)}, u32[]{:S(2)}, u32[]{:S(2)}) collective-permute-start(bf16[192,512]{1,0:T(8,128)(2,1)S(1)} %pad_maximum_fusion.4.refs_0_), channel_id=1, source_target_pairs={{0,8},{4,12},{8,16},{12,20},{16,24},{20,28},{24,0},{28,4},{1,9},{5... | collective-permute-start | bytes 589832 | tf_op jit(solution)/shard_map/ppermute | solution.py:24
  5.1 7.8 %collective-permute-start.1 = (bf16[192,512]{1,0:T(8,128)(2,1)S(1)}, bf16[192,512]{1,0:T(8,128)(2,1)S(1)}, u32[]{:S(2)}, u32[]{:S(2)}) collective-permute-start(bf16[192,512]{1,0:T(8,128)(2,1)S(1)} %pad_maximum_fusion.5), channel_id=1, source_target_pairs={{0,4},{4,0},{8,12},{12,8},{16,20},{20,16},{24,28},{28,24},{1,5},{5... | collective-permute-start | bytes 589832 | tf_op jit(solution)/shard_map/ppermute | solution.py:19
  8.3 8.2 %collective-permute-start.3 = (bf16[192,256]{1,0:T(8,128)(2,1)}, bf16[192,256]{1,0:T(8,128)(2,1)S(1)}, u32[]{:S(2)}, u32[]{:S(2)}) collective-permute-start(bf16[192,256]{1,0:T(8,128)(2,1)} %get-tuple-element.178), channel_id=1, source_target_pairs={{0,4},{4,0},{8,12},{12,8},{16,20},{20,16},{24,28},{28,24},{1,5},{5... | collective-permute-start | bytes 294920 | tf_op jit(solution)/shard_map/ppermute | solution.py:19
  12.8 9.6 %collective-permute-start.2 = (bf16[192,512]{1,0:T(8,128)(2,1)S(1)}, bf16[192,512]{1,0:T(8,128)(2,1)S(1)}, u32[]{:S(2)}, u32[]{:S(2)}) collective-permute-start(bf16[192,512]{1,0:T(8,128)(2,1)S(1)} %collective-permute-done.1.refs_1_), channel_id=1, source_target_pairs={{0,8},{4,12},{8,16},{12,20},{16,24},{20,28},{24,0},{28,4},{1,9},{5... | collective-permute-start | bytes 589832 | tf_op jit(solution)/shard_map/ppermute | solution.py:24
  14.9 11.4 %collective-permute-start.4 = (bf16[192,512]{1,0:T(8,128)(2,1)S(1)}, bf16[192,512]{1,0:T(8,128)(2,1)S(1)}, u32[]{:S(2)}, u32[]{:S(2)}) collective-permute-start(bf16[192,512]{1,0:T(8,128)(2,1)S(1)} %collective-permute-done.refs_2_), channel_id=1, source_target_pairs={{0,8},{4,12},{8,16},{12,20},{16,24},{20,28},{24,0},{28,4},{1,9},{5... | collective-permute-start | bytes 589832 | tf_op jit(solution)/shard_map/ppermute | solution.py:24
  47.9 29.9 %collective-permute-start.26 = (bf16[2,2,2048,256]{3,2,1,0:T(8,128)(2,1)}, bf16[2,2,2048,256]{3,2,1,0:T(8,128)(2,1)}, u32[]{:S(2)}, u32[]{:S(2)}) collective-permute-start(bf16[2,2,2048,256]{3,2,1,0:T(8,128)(2,1)} %bitcast.65.refs_6_), channel_id=1, source_target_pairs={{0,1},{1,0},{2,3},{3,2},{4,5},{5,4},{6,7},{7,6},{8,9},{9,8},{10,11... | collective-permute-start | bytes 12582920 | tf_op jit(solution)/shard_map/ppermute | solution.py:37
  48.5 9.9 %collective-permute-start.10 = (bf16[48,2176]{1,0:T(8,128)(2,1)S(1)}, bf16[48,2176]{1,0:T(8,128)(2,1)S(1)}, u32[]{:S(2)}, u32[]{:S(2)}) collective-permute-start(bf16[48,2176]{1,0:T(8,128)(2,1)S(1)} %concatenate.29), channel_id=1, source_target_pairs={{0,24},{4,28},{8,16},{12,20},{16,8},{20,12},{24,0},{28,4},{1,25},{... | collective-permute-start | bytes 626696 | tf_op jit(solution)/shard_map/ppermute | solution.py:29
  48.6 13.5 %collective-permute-start.13 = (bf16[48,2176]{1,0:T(8,128)(2,1)S(1)}, bf16[48,2176]{1,0:T(8,128)(2,1)S(1)}, u32[]{:S(2)}, u32[]{:S(2)}) collective-permute-start(bf16[48,2176]{1,0:T(8,128)(2,1)S(1)} %concatenate.29), channel_id=1, source_target_pairs={{0,8},{4,12},{8,0},{12,4},{16,24},{20,28},{24,16},{28,20},{1,9},{5... | collective-permute-start | bytes 626696 | tf_op jit(solution)/shard_map/ppermute | solution.py:29
  50.3 10.2 %collective-permute-start.19 = (bf16[48,1152]{1,0:T(8,128)(2,1)S(1)}, bf16[48,1152]{1,0:T(8,128)(2,1)S(1)}, u32[]{:S(2)}, u32[]{:S(2)}) collective-permute-start(bf16[48,1152]{1,0:T(8,128)(2,1)S(1)} %get-tuple-element.113.refs_1_), channel_id=1, source_target_pairs={{0,2},{1,3},{2,0},{3,1},{4,6},{5,7},{6,4},{7,5},{8,10},{9,11},{10,... | collective-permute-start | bytes 331784 | tf_op jit(solution)/shard_map/ppermute | solution.py:33
  58.4 8.3 %collective-permute-start.12 = (bf16[48,1152]{1,0:T(8,128)(2,1)S(1)}, bf16[48,1152]{1,0:T(8,128)(2,1)S(1)}, u32[]{:S(2)}, u32[]{:S(2)}) collective-permute-start(bf16[48,1152]{1,0:T(8,128)(2,1)S(1)} %slice.122), channel_id=1, source_target_pairs={{0,8},{4,12},{8,0},{12,4},{16,24},{20,28},{24,16},{28,20},{1,9},{5... | collective-permute-start | bytes 331784 | tf_op jit(solution)/shard_map/ppermute | solution.py:29
  65.2 8.1 %collective-permute-start.20 = (bf16[2,48,1024]{2,1,0:T(8,128)(2,1)S(1)}, bf16[2,48,1024]{2,1,0:T(8,128)(2,1)S(1)}, u32[]{:S(2)}, u32[]{:S(2)}) collective-permute-start(bf16[2,48,1024]{2,1,0:T(8,128)(2,1)S(1)} %pad_maximum_fusion.6), channel_id=1, source_target_pairs={{0,2},{1,3},{2,0},{3,1},{4,6},{5,7},{6,4},{7,5},{8,10},{9,11},{10,... | collective-permute-start | bytes 589832 | tf_op jit(solution)/shard_map/ppermute | solution.py:33
  73.3 12.6 %collective-permute-start.25 = (bf16[2,48,2176]{2,1,0:T(8,128)(2,1)S(1)}, bf16[2,48,2176]{2,1,0:T(8,128)(2,1)S(1)}, u32[]{:S(2)}, u32[]{:S(2)}) collective-permute-start(bf16[2,48,2176]{2,1,0:T(8,128)(2,1)S(1)} %pad_maximum_fusion.1), channel_id=1, source_target_pairs={{0,4},{4,0},{8,12},{12,8},{16,20},{20,16},{24,28},{28,24},{1,5},{5... | collective-permute-start | bytes 1253384 | tf_op jit(solution)/shard_map/ppermute | solution.py:19
  74.4 11.5 %collective-permute-start.24 = (bf16[2,48,2176]{2,1,0:T(8,128)(2,1)S(1)}, bf16[2,48,2176]{2,1,0:T(8,128)(2,1)S(1)}, u32[]{:S(2)}, u32[]{:S(2)}) collective-permute-start(bf16[2,48,2176]{2,1,0:T(8,128)(2,1)S(1)} %pad_maximum_fusion), channel_id=1, source_target_pairs={{0,2},{1,3},{2,0},{3,1},{4,6},{5,7},{6,4},{7,5},{8,10},{9,11},{10,... | collective-permute-start | bytes 1253384 | tf_op jit(solution)/shard_map/ppermute | solution.py:33
  76.5 21.0 %collective-permute-start.23 = (bf16[2,48,1152]{2,1,0:T(8,128)(2,1)S(1)}, bf16[2,48,1152]{2,1,0:T(8,128)(2,1)S(1)}, u32[]{:S(2)}, u32[]{:S(2)}) collective-permute-start(bf16[2,48,1152]{2,1,0:T(8,128)(2,1)S(1)} %pad_maximum_fusion.3), channel_id=1, source_target_pairs={{0,4},{4,0},{8,12},{12,8},{16,20},{20,16},{24,28},{28,24},{1,5},{5... | collective-permute-start | bytes 663560 | tf_op jit(solution)/shard_map/ppermute | solution.py:19
  77.6 19.9 %collective-permute-start.22 = (bf16[2,48,1024]{2,1,0:T(8,128)(2,1)S(1)}, bf16[2,48,1024]{2,1,0:T(8,128)(2,1)S(1)}, u32[]{:S(2)}, u32[]{:S(2)}) collective-permute-start(bf16[2,48,1024]{2,1,0:T(8,128)(2,1)S(1)} %pad_maximum_fusion.7), channel_id=1, source_target_pairs={{0,2},{1,3},{2,0},{3,1},{4,6},{5,7},{6,4},{7,5},{8,10},{9,11},{10,... | collective-permute-start | bytes 589832 | tf_op jit(solution)/shard_map/ppermute | solution.py:33
  85.9 11.5 %collective-permute-start.28 = (bf16[2,48,1024]{2,1,0:T(8,128)(2,1)S(1)}, bf16[2,48,1024]{2,1,0:T(8,128)(2,1)S(1)}, u32[]{:S(2)}, u32[]{:S(2)}) collective-permute-start(bf16[2,48,1024]{2,1,0:T(8,128)(2,1)S(1)} %get-tuple-element.127), channel_id=1, source_target_pairs={{0,4},{4,0},{8,12},{12,8},{16,20},{20,16},{24,28},{28,24},{1,5},{5... | collective-permute-start | bytes 589832 | tf_op jit(solution)/shard_map/ppermute | solution.py:19
  87.3 10.1 %collective-permute-start.27 = (bf16[2,48,1024]{2,1,0:T(8,128)(2,1)S(1)}, bf16[2,48,1024]{2,1,0:T(8,128)(2,1)S(1)}, u32[]{:S(2)}, u32[]{:S(2)}) collective-permute-start(bf16[2,48,1024]{2,1,0:T(8,128)(2,1)S(1)} %get-tuple-element.125), channel_id=1, source_target_pairs={{0,2},{1,3},{2,0},{3,1},{4,6},{5,7},{6,4},{7,5},{8,10},{9,11},{10,... | collective-permute-start | bytes 589832 | tf_op jit(solution)/shard_map/ppermute | solution.py:33
  97.5 13.8 %collective-permute-start.30 = (bf16[2,48,2048]{2,1,0:T(8,128)(2,1)S(1)}, bf16[2,48,2048]{2,1,0:T(8,128)(2,1)S(1)}, u32[]{:S(2)}, u32[]{:S(2)}) collective-permute-start(bf16[2,48,2048]{2,1,0:T(8,128)(2,1)S(1)} %get-tuple-element.155), channel_id=1, source_target_pairs={{0,4},{4,0},{8,12},{12,8},{16,20},{20,16},{24,28},{28,24},{1,5},{5... | collective-permute-start | bytes 1179656 | tf_op jit(solution)/shard_map/ppermute | solution.py:19
  98.4 13.0 %collective-permute-start.29 = (bf16[2,48,2048]{2,1,0:T(8,128)(2,1)S(1)}, bf16[2,48,2048]{2,1,0:T(8,128)(2,1)S(1)}, u32[]{:S(2)}, u32[]{:S(2)}) collective-permute-start(bf16[2,48,2048]{2,1,0:T(8,128)(2,1)S(1)} %get-tuple-element.153), channel_id=1, source_target_pairs={{0,2},{1,3},{2,0},{3,1},{4,6},{5,7},{6,4},{7,5},{8,10},{9,11},{10,... | collective-permute-start | bytes 1179656 | tf_op jit(solution)/shard_map/ppermute | solution.py:33
  98.4 12.8 %collective-permute-start.34 = (bf16[48,1024]{1,0:T(8,128)(2,1)S(1)}, bf16[48,1024]{1,0:T(8,128)(2,1)S(1)}, u32[]{:S(2)}, u32[]{:S(2)}) collective-permute-start(bf16[48,1024]{1,0:T(8,128)(2,1)S(1)} %slice_bitcast_fusion.4), channel_id=1, source_target_pairs={{0,2},{1,3},{2,0},{3,1},{4,6},{5,7},{6,4},{7,5},{8,10},{9,11},{10,... | collective-permute-start | bytes 294920 | tf_op jit(solution)/shard_map/ppermute | solution.py:33
  100.5 10.7 %collective-permute-start.33 = (bf16[48,1024]{1,0:T(8,128)(2,1)S(1)}, bf16[48,1024]{1,0:T(8,128)(2,1)S(1)}, u32[]{:S(2)}, u32[]{:S(2)}) collective-permute-start(bf16[48,1024]{1,0:T(8,128)(2,1)S(1)} %slice_bitcast_fusion.5), channel_id=1, source_target_pairs={{0,4},{4,0},{8,12},{12,8},{16,20},{20,16},{24,28},{28,24},{1,5},{5... | collective-permute-start | bytes 294920 | tf_op jit(solution)/shard_map/ppermute | solution.py:19
  123.0 9.9 %collective-permute-start.38 = (bf16[48,2048]{1,0:T(8,128)(2,1)S(1)}, bf16[48,2048]{1,0:T(8,128)(2,1)S(1)}, u32[]{:S(2)}, u32[]{:S(2)}) collective-permute-start(bf16[48,2048]{1,0:T(8,128)(2,1)S(1)} %fusion.5), channel_id=1, source_target_pairs={{0,8},{4,12},{8,0},{12,4},{16,24},{20,28},{24,16},{28,20},{1,9},{5... | collective-permute-start | bytes 589832 | tf_op jit(solution)/shard_map/ppermute | solution.py:29
  126.0 8.7 %collective-permute-start.41 = (bf16[48,2048]{1,0:T(8,128)(2,1)S(1)}, bf16[48,2048]{1,0:T(8,128)(2,1)S(1)}, u32[]{:S(2)}, u32[]{:S(2)}) collective-permute-start(bf16[48,2048]{1,0:T(8,128)(2,1)S(1)} %pad_maximum_fusion.8), channel_id=1, source_target_pairs={{0,16},{4,20},{8,24},{12,28},{16,0},{20,4},{24,8},{28,12},{1,17},{... | collective-permute-start | bytes 589832 | tf_op jit(solution)/shard_map/ppermute | solution.py:29
  (27 other events, 242.6 us)

commit v6 on v5

--- a/solution.py
+++ b/solution.py
@@ -122,7 +122,7 @@
 
     (k_own, k_other), (v_own, v_other) = split(keys), split(values)
     own, beside = jnp.concatenate([k_own, v_own], 1), jnp.concatenate([k_other, v_other], 1)
-    own, beside, queries = lax.optimization_barrier((own, beside, queries))
+    own, beside, queries, held = lax.optimization_barrier((own, beside, queries, held))
     q_own, q_other = split(relative_rows(queries, x, core))
     beside = over_y(beside)
     blocks, shard = [own, beside], [2 * z + y, 2 * z + 1 - y]
@@ -142,7 +142,7 @@
     pos = jnp.concatenate([seq * rows + local, (seq ^ 1) * rows + local])
     bounds = jnp.cumsum(lengths)
     start = jnp.max(jnp.where(bounds[None, :] <= pos[:, None], bounds[None, :], 0), axis=1)
-    blocks, held = lax.optimization_barrier((blocks, held))
+    blocks, held = lax.optimization_barrier((blocks, over_core(held)))
     out = attend(q_own, q_beside, pos[:, None], start[:, None], bases, blocks)
     return out[:rows], over_y(out[rows:]), held
 
@@ -286,18 +286,16 @@
     own = use_halves(own)
     pairs, own = lax.optimization_barrier((pairs, own))
     pairs = [use_groups(pair) for pair in pairs]
-    own = scatter_first(*own)
-    own, pairs = lax.optimization_barrier((own, pairs))
     far, pairs = lax.optimization_barrier((far, pairs))
     pairs = [scatter_first(*pair) for pair in pairs]
     far = use_halves(far)
     far, pairs = lax.optimization_barrier((far, pairs))
     pairs = [scatter_second(*pair) for pair in pairs]
     far = scatter_first(*far)
-    own = scatter_second(*own)
-    far, own, pairs = lax.optimization_barrier((far, own, pairs))
+    far, pairs = lax.optimization_barrier((far, pairs))
     far = scatter_second(*far)
-    return own, far, pairs
+    far, own = lax.optimization_barrier((far, own))
+    return scatter_second(*scatter_first(*own)), far, pairs
 
 
 def scatter_first(a_keep, a_send, b_keep, b_send):
@@ -326,7 +324,7 @@
     count = owned * lax.axis_size("seq")
 
     own, other, down_other = attention(
-        queries, keys, values, lengths, seq, x, core, over_core(w_down)
+        queries, keys, values, lengths, seq, x, core, w_down
     )
     heads = jnp.where(
         y == 0, jnp.concatenate([own, other], 1), jnp.concatenate([other, own], 1)

time: 136 us -> 135 us (level)
    ppermute x7, waiting for transfers between devices: 13.2 us -> 5.96 us  [across_z(): return lax.ppermute(a, 'seq', [(i, i ^ 2 * k) for i in range(count)])]
    ppermute x15, waiting for transfers between devices: 10.6 us -> 15.4 us  [over_y(): return lax.ppermute(a, 'seq', [(i, i ^ 1) for i in range(count)])]
    ppermute x13, starting transfers between devices: 17.1 us -> 15.3 us  [over_x(): return lax.ppermute(a, 'tp', [(i, i ^ 2) for i in range(4)])]
    ppermute x13, waiting for transfers between devices: 13.2 us -> 14.7 us  [over_x(): return lax.ppermute(a, 'tp', [(i, i ^ 2) for i in range(4)])]
  transfers between devices with their start and end apart: 42 -> 42, of which waited for: 24 -> 24; matrix products, arithmetic and copies ran while one was open for 6% -> 5% of each run, Pallas kernels for 15% -> 15%
where the time goes in v6:
time: 135 us
  waiting for transfers between devices  54.5 us (40%)
  starting transfers between devices  45.9 us (34%)
  Pallas kernels  23.2 us (17%)
  local copies, waits for them, and re-layouts  4.48 us (3%)
  other arithmetic  4.34 us (3%)
    pallas_call x3, Pallas kernels, experts(): pl.pallas_call(functools.partial(expert_kernel, layout, ways, count), out...  20 us
    ppermute x15, starting transfers between devices, over_y(): return lax.ppermute(a, 'seq', [(i, i ^ 1) for i in range(count)])  18.3 us
    ppermute x4, waiting for transfers between devices, over_z(): lax.ppermute(a, 'seq', [(i, (i + 2 * step) % count) for i in range(count)])  16.8 us
    ppermute x15, waiting for transfers between devices, over_y(): return lax.ppermute(a, 'seq', [(i, i ^ 1) for i in range(count)])  15.4 us
    ppermute x13, starting transfers between devices, over_x(): return lax.ppermute(a, 'tp', [(i, i ^ 2) for i in range(4)])  15.3 us
    ppermute x13, waiting for transfers between devices, over_x(): return lax.ppermute(a, 'tp', [(i, i ^ 2) for i in range(4)])  14.7 us
    ppermute x7, waiting for transfers between devices, across_z(): return lax.ppermute(a, 'seq', [(i, i ^ 2 * k) for i in range(count)])  5.96 us
    ppermute x4, starting transfers between devices, over_z(): lax.ppermute(a, 'seq', [(i, (i + 2 * step) % count) for i in range(count)])  5.8 us
  transfers between devices with their start and end apart: 42, of which 24 were waited for; matrix products, arithmetic and copies ran while one was open for 5% of the time, Pallas kernels for 15%

profile of v6, /device:TPU:0, one launch (start us, length us, event | category | flops | bytes accessed | tf_op | source)
XLA Modules:
  0.0 134.6 jit_solution(13818140146234360587)
XLA Ops:
  2.5 2.6 %collective-permute-start = (bf16[192,512]{1,0:T(8,128)(2,1)S(1)}, bf16[192,512]{1,0:T(8,128)(2,1)S(1)}, u32[]{:S(2)}, u32[]{:S(2)}) collective-permute-start(bf16[192,512]{1,0:T(8,128)(2,1)S(1)} %pad_maximum_fusion.4.refs_0_), channel_id=1, source_target_pairs={{0,8},{4,12},{8,16},{12,20},{16,24},{20,28},{24,0},{28,4},{1,9},{5... | collective-permute-start | bytes 589832 | tf_op jit(solution)/shard_map/ppermute | solution.py:24
  9.2 3.4 %collective-permute-done.refs_2_ = bf16[192,512]{1,0:T(8,128)(2,1)S(1)} collective-permute-done((bf16[192,512]{1,0:T(8,128)(2,1)S(1)}, bf16[192,512]{1,0:T(8,128)(2,1)S(1)}, u32[]{:S(2)}, u32[]{:S(2)}) %collective-permute-start) | collective-permute-done | bytes 196640 | tf_op jit(solution)/shard_map/ppermute | solution.py:24
  16.5 6.0 %collective-permute-done.2.refs_3_ = bf16[192,512]{1,0:T(8,128)(2,1)S(1)} collective-permute-done((bf16[192,512]{1,0:T(8,128)(2,1)S(1)}, bf16[192,512]{1,0:T(8,128)(2,1)S(1)}, u32[]{:S(2)}, u32[]{:S(2)}) %collective-permute-start.2) | collective-permute-done | bytes 196640 | tf_op jit(solution)/shard_map/ppermute | solution.py:24
  22.5 3.8 %collective-permute-done.4.refs_4_ = bf16[192,512]{1,0:T(8,128)(2,1)S(1)} collective-permute-done((bf16[192,512]{1,0:T(8,128)(2,1)S(1)}, bf16[192,512]{1,0:T(8,128)(2,1)S(1)}, u32[]{:S(2)}, u32[]{:S(2)}) %collective-permute-start.4) | collective-permute-done | bytes 196640 | tf_op jit(solution)/shard_map/ppermute | solution.py:24
  26.3 3.6 %collective-permute-done.5.refs_5_ = bf16[192,512]{1,0:T(8,128)(2,1)S(1)} collective-permute-done((bf16[192,512]{1,0:T(8,128)(2,1)S(1)}, bf16[192,512]{1,0:T(8,128)(2,1)S(1)}, u32[]{:S(2)}, u32[]{:S(2)}) %collective-permute-start.5) | collective-permute-done | bytes 196640 | tf_op jit(solution)/shard_map/ppermute | solution.py:24
  29.9 3.2 %shard_map.122 = bf16[384,256]{1,0:T(8,128)(2,1)S(1)} custom-call(s32[6]{0:T(128)S(1)} %broadcast_multiply_fusion.bases, bf16[192,256]{1,0:T(8,128)(2,1)S(1)} %get-tuple-element.177.q_own, bf16[192,256]{1,0:T(8,128)(2,1)S(1)} %collective-permute-done.3.q_beside, s32[384,1]{1,0:T(8,128)S(1)} %broadcast_in_dim.45.pos_ref, ...), custom_call_target="tpu_custom_call" | custom-call | flops 452984832 | bytes 1572864 | tf_op jit(solution)/shard_map/pallas_call | solution.py:99
  34.8 3.1 %collective-permute-done.7 = bf16[192,256]{1,0:T(8,128)(2,1)S(1)} collective-permute-done((bf16[192,256]{1,0:T(8,128)(2,1)S(1)}, bf16[192,256]{1,0:T(8,128)(2,1)S(1)}, u32[]{:S(2)}, u32[]{:S(2)}) %collective-permute-start.7) | collective-permute-done | bytes 98336 | tf_op jit(solution)/shard_map/ppermute | solution.py:19
  38.5 1.7 %collective-permute-done.8 = bf16[96,2048]{1,0:T(8,128)(2,1)S(1)} collective-permute-done((bf16[96,2048]{1,0:T(8,128)(2,1)S(1)}, bf16[96,2048]{1,0:T(8,128)(2,1)S(1)}, u32[]{:S(2)}, u32[]{:S(2)}) %collective-permute-start.8) | collective-permute-done | bytes 393248 | tf_op jit(solution)/shard_map/ppermute | solution.py:37
  42.3 2.6 %copy.41 = bf16[2,2048,2,256]{3,1,2,0:T(8,128)(2,1)} copy(bf16[2,2048,2,256]{3,2,1,0:T(2,128)(2,1)S(1)} %copy-done.2) | data formatting | bytes 8388608 | tf_op jit(solution)/shard_map/optimization_barrier | solution.py:336
  44.9 2.9 %collective-permute-done.9 = bf16[48,2048]{1,0:T(8,128)(2,1)S(1)} collective-permute-done((bf16[48,2048]{1,0:T(8,128)(2,1)S(1)}, bf16[48,2048]{1,0:T(8,128)(2,1)S(1)}, u32[]{:S(2)}, u32[]{:S(2)}) %collective-permute-start.9) | collective-permute-done | bytes 196640 | tf_op jit(solution)/shard_map/ppermute | solution.py:33
  51.8 2.1 %collective-permute-done.18.refs_2_ = bf16[48,1024]{1,0:T(8,128)(2,1)S(1)} collective-permute-done((bf16[48,1024]{1,0:T(8,128)(2,1)S(1)}, bf16[48,1024]{1,0:T(8,128)(2,1)S(1)}, u32[]{:S(2)}, u32[]{:S(2)}) %collective-permute-start.18) | collective-permute-done | bytes 98336 | tf_op jit(solution)/shard_map/ppermute | solution.py:19
  53.9 4.4 %collective-permute-done.10.refs_0_ = bf16[48,2176]{1,0:T(8,128)(2,1)S(1)} collective-permute-done((bf16[48,2176]{1,0:T(8,128)(2,1)S(1)}, bf16[48,2176]{1,0:T(8,128)(2,1)S(1)}, u32[]{:S(2)}, u32[]{:S(2)}) %collective-permute-start.10) | collective-permute-done | bytes 208928 | tf_op jit(solution)/shard_map/ppermute | solution.py:29
  58.9 1.6 %collective-permute-start.11 = (bf16[48,1024]{1,0:T(8,128)(2,1)S(1)}, bf16[48,1024]{1,0:T(8,128)(2,1)S(1)}, u32[]{:S(2)}, u32[]{:S(2)}) collective-permute-start(bf16[48,1024]{1,0:T(8,128)(2,1)S(1)} %slice.121), channel_id=1, source_target_pairs={{0,8},{4,12},{8,0},{12,4},{16,24},{20,28},{24,16},{28,20},{1,9},{5... | collective-permute-start | bytes 294920 | tf_op jit(solution)/shard_map/ppermute | solution.py:29
  71.5 1.7 %collective-permute-done.20.refs_4_ = bf16[2,48,1024]{2,1,0:T(8,128)(2,1)S(1)} collective-permute-done((bf16[2,48,1024]{2,1,0:T(8,128)(2,1)S(1)}, bf16[2,48,1024]{2,1,0:T(8,128)(2,1)S(1)}, u32[]{:S(2)}, u32[]{:S(2)}) %collective-permute-start.20) | collective-permute-done | bytes 196640 | tf_op jit(solution)/shard_map/ppermute | solution.py:33
  77.7 6.0 %shard_map.123 = (bf16[2,48,1024]{2,1,0:T(8,128)(2,1)S(1)}, bf16[2,48,1024]{2,1,0:T(8,128)(2,1)S(1)}, bf16[2,48,1024]{2,1,0:T(8,128)(2,1)S(1)}, bf16[2,48,1024]{2,1,0:T(8,128)(2,1)S(1)}) custom-call(s32[1]{0:T(128)} %bitcast.15.first, bf16[48,1024]{1,0:T(8,128)(2,1)S(1)} %get-tuple-element.112.refs_0_, bf16[48,1152]{1,0:T(8,128)(2,1)S(1)} %get-tuple-element.113.refs_1_, ...), custom_call_target="tpu_custom_call" | custom-call | flops 2415919104 | bytes 14155776 | tf_op jit(solution)/shard_map/pallas_call | solution.py:218
  83.7 2.1 %collective-permute-done.25.refs_5_ = bf16[2,48,2176]{2,1,0:T(8,128)(2,1)S(1)} collective-permute-done((bf16[2,48,2176]{2,1,0:T(8,128)(2,1)S(1)}, bf16[2,48,2176]{2,1,0:T(8,128)(2,1)S(1)}, u32[]{:S(2)}, u32[]{:S(2)}) %collective-permute-start.25) | collective-permute-done | bytes 417824 | tf_op jit(solution)/shard_map/ppermute | solution.py:19
  85.8 7.9 %shard_map.124 = (bf16[2,48,2048]{2,1,0:T(8,128)(2,1)S(1)}, bf16[2,48,2048]{2,1,0:T(8,128)(2,1)S(1)}, bf16[2,48,2048]{2,1,0:T(8,128)(2,1)S(1)}, bf16[2,48,2048]{2,1,0:T(8,128)(2,1)S(1)}) custom-call(s32[1]{0:T(128)} %bitcast.15.first, bf16[48,2176]{1,0:T(8,128)(2,1)S(1)} %collective-permute-done.10.refs_0_, ...), custom_call_target="tpu_custom_call" | custom-call | flops 4831838208 | bytes 15728640 | tf_op jit(solution)/shard_map/pallas_call | solution.py:218
  96.2 6.0 %shard_map.125 = (bf16[2,48,1024]{2,1,0:T(8,128)(2,1)S(1)}, bf16[2,48,1024]{2,1,0:T(8,128)(2,1)S(1)}, bf16[2,48,1024]{2,1,0:T(8,128)(2,1)S(1)}, bf16[2,48,1024]{2,1,0:T(8,128)(2,1)S(1)}) custom-call(s32[1]{0:T(128)} %bitcast.15.first, bf16[48,1024]{1,0:T(8,128)(2,1)S(1)} %collective-permute-done.11.refs_0_, ...), custom_call_target="tpu_custom_call" | custom-call | flops 2415919104 | bytes 14155776 | tf_op jit(solution)/shard_map/pallas_call | solution.py:218
  102.3 2.6 %collective-permute-done.27 = bf16[2,48,2048]{2,1,0:T(8,128)(2,1)S(1)} collective-permute-done((bf16[2,48,2048]{2,1,0:T(8,128)(2,1)S(1)}, bf16[2,48,2048]{2,1,0:T(8,128)(2,1)S(1)}, u32[]{:S(2)}, u32[]{:S(2)}) %collective-permute-start.27) | collective-permute-done | bytes 393248 | tf_op jit(solution)/shard_map/ppermute | solution.py:33
  106.4 2.0 %collective-permute-start.31 = (bf16[48,2048]{1,0:T(8,128)(2,1)S(1)}, bf16[48,2048]{1,0:T(8,128)(2,1)S(1)}, u32[]{:S(2)}, u32[]{:S(2)}) collective-permute-start(bf16[48,2048]{1,0:T(8,128)(2,1)S(1)} %slice_bitcast_fusion.1), channel_id=1, source_target_pairs={{0,4},{4,0},{8,12},{12,8},{16,20},{20,16},{24,28},{28,24},{1,5},{5... | collective-permute-start | bytes 589832 | tf_op jit(solution)/shard_map/ppermute | solution.py:19
  109.2 2.6 %collective-permute-done.32 = bf16[48,2048]{1,0:T(8,128)(2,1)S(1)} collective-permute-done((bf16[48,2048]{1,0:T(8,128)(2,1)S(1)}, bf16[48,2048]{1,0:T(8,128)(2,1)S(1)}, u32[]{:S(2)}, u32[]{:S(2)}) %collective-permute-start.32) | collective-permute-done | bytes 196640 | tf_op jit(solution)/shard_map/ppermute | solution.py:33
  113.2 2.1 %collective-permute-done.30 = bf16[2,48,1024]{2,1,0:T(8,128)(2,1)S(1)} collective-permute-done((bf16[2,48,1024]{2,1,0:T(8,128)(2,1)S(1)}, bf16[2,48,1024]{2,1,0:T(8,128)(2,1)S(1)}, u32[]{:S(2)}, u32[]{:S(2)}) %collective-permute-start.30) | collective-permute-done | bytes 196640 | tf_op jit(solution)/shard_map/ppermute | solution.py:19
  125.3 2.2 %collective-permute-done.35 = bf16[2,48,1024]{2,1,0:T(8,128)(2,1)S(1)} collective-permute-done((bf16[2,48,1024]{2,1,0:T(8,128)(2,1)S(1)}, bf16[2,48,1024]{2,1,0:T(8,128)(2,1)S(1)}, u32[]{:S(2)}, u32[]{:S(2)}) %collective-permute-start.35) | collective-permute-done | bytes 196640 | tf_op jit(solution)/shard_map/ppermute | solution.py:33
  130.0 2.3 %collective-permute-done.36 = bf16[48,1024]{1,0:T(8,128)(2,1)S(1)} collective-permute-done((bf16[48,1024]{1,0:T(8,128)(2,1)S(1)}, bf16[48,1024]{1,0:T(8,128)(2,1)S(1)}, u32[]{:S(2)}, u32[]{:S(2)}) %collective-permute-start.36) | collective-permute-done | bytes 98336 | tf_op jit(solution)/shard_map/ppermute | solution.py:19
  (148 shorter events, 54.8 us)
Async XLA Ops:
  1.9 28.0 %collective-permute-start.6 = (bf16[2,256,2048]{2,1,0:T(8,128)(2,1)}, bf16[2,256,2048]{2,1,0:T(8,128)(2,1)}, u32[]{:S(2)}, u32[]{:S(2)}) collective-permute-start(bf16[2,256,2048]{2,1,0:T(8,128)(2,1)} %refs_8_.5), channel_id=1, source_target_pairs={{0,1},{1,0},{2,3},{3,2},{4,5},{5,4},{6,7},{7,6},{8,9},{9,8},{10,11... | collective-permute-start | bytes 6291464 | tf_op jit(solution)/shard_map/ppermute | solution.py:37
  2.5 10.2 %collective-permute-start = (bf16[192,512]{1,0:T(8,128)(2,1)S(1)}, bf16[192,512]{1,0:T(8,128)(2,1)S(1)}, u32[]{:S(2)}, u32[]{:S(2)}) collective-permute-start(bf16[192,512]{1,0:T(8,128)(2,1)S(1)} %pad_maximum_fusion.4.refs_0_), channel_id=1, source_target_pairs={{0,8},{4,12},{8,16},{12,20},{16,24},{20,28},{24,0},{28,4},{1,9},{5... | collective-permute-start | bytes 589832 | tf_op jit(solution)/shard_map/ppermute | solution.py:24
  5.1 7.7 %collective-permute-start.1 = (bf16[192,512]{1,0:T(8,128)(2,1)S(1)}, bf16[192,512]{1,0:T(8,128)(2,1)S(1)}, u32[]{:S(2)}, u32[]{:S(2)}) collective-permute-start(bf16[192,512]{1,0:T(8,128)(2,1)S(1)} %pad_maximum_fusion.5), channel_id=1, source_target_pairs={{0,4},{4,0},{8,12},{12,8},{16,20},{20,16},{24,28},{28,24},{1,5},{5... | collective-permute-start | bytes 589832 | tf_op jit(solution)/shard_map/ppermute | solution.py:19
  8.3 8.2 %collective-permute-start.3 = (bf16[192,256]{1,0:T(8,128)(2,1)}, bf16[192,256]{1,0:T(8,128)(2,1)S(1)}, u32[]{:S(2)}, u32[]{:S(2)}) collective-permute-start(bf16[192,256]{1,0:T(8,128)(2,1)} %get-tuple-element.176), channel_id=1, source_target_pairs={{0,4},{4,0},{8,12},{12,8},{16,20},{20,16},{24,28},{28,24},{1,5},{5... | collective-permute-start | bytes 294920 | tf_op jit(solution)/shard_map/ppermute | solution.py:19
  12.8 9.6 %collective-permute-start.2 = (bf16[192,512]{1,0:T(8,128)(2,1)S(1)}, bf16[192,512]{1,0:T(8,128)(2,1)S(1)}, u32[]{:S(2)}, u32[]{:S(2)}) collective-permute-start(bf16[192,512]{1,0:T(8,128)(2,1)S(1)} %collective-permute-done.1.refs_1_), channel_id=1, source_target_pairs={{0,8},{4,12},{8,16},{12,20},{16,24},{20,28},{24,0},{28,4},{1,9},{5... | collective-permute-start | bytes 589832 | tf_op jit(solution)/shard_map/ppermute | solution.py:24
  14.9 11.4 %collective-permute-start.4 = (bf16[192,512]{1,0:T(8,128)(2,1)S(1)}, bf16[192,512]{1,0:T(8,128)(2,1)S(1)}, u32[]{:S(2)}, u32[]{:S(2)}) collective-permute-start(bf16[192,512]{1,0:T(8,128)(2,1)S(1)} %collective-permute-done.refs_2_), channel_id=1, source_target_pairs={{0,8},{4,12},{8,16},{12,20},{16,24},{20,28},{24,0},{28,4},{1,9},{5... | collective-permute-start | bytes 589832 | tf_op jit(solution)/shard_map/ppermute | solution.py:24
  22.5 7.5 %collective-permute-start.5 = (bf16[192,512]{1,0:T(8,128)(2,1)S(1)}, bf16[192,512]{1,0:T(8,128)(2,1)S(1)}, u32[]{:S(2)}, u32[]{:S(2)}) collective-permute-start(bf16[192,512]{1,0:T(8,128)(2,1)S(1)} %collective-permute-done.2.refs_3_), channel_id=1, source_target_pairs={{0,8},{4,12},{8,16},{12,20},{16,24},{20,28},{24,0},{28,4},{1,9},{5... | collective-permute-start | bytes 589832 | tf_op jit(solution)/shard_map/ppermute | solution.py:24
  47.8 29.9 %collective-permute-start.26 = (bf16[2,2,2048,256]{3,2,1,0:T(8,128)(2,1)}, bf16[2,2,2048,256]{3,2,1,0:T(8,128)(2,1)}, u32[]{:S(2)}, u32[]{:S(2)}) collective-permute-start(bf16[2,2,2048,256]{3,2,1,0:T(8,128)(2,1)} %bitcast.69.refs_6_), channel_id=1, source_target_pairs={{0,1},{1,0},{2,3},{3,2},{4,5},{5,4},{6,7},{7,6},{8,9},{9,8},{10,11... | collective-permute-start | bytes 12582920 | tf_op jit(solution)/shard_map/ppermute | solution.py:37
  48.5 9.9 %collective-permute-start.10 = (bf16[48,2176]{1,0:T(8,128)(2,1)S(1)}, bf16[48,2176]{1,0:T(8,128)(2,1)S(1)}, u32[]{:S(2)}, u32[]{:S(2)}) collective-permute-start(bf16[48,2176]{1,0:T(8,128)(2,1)S(1)} %concatenate.29), channel_id=1, source_target_pairs={{0,24},{4,28},{8,16},{12,20},{16,8},{20,12},{24,0},{28,4},{1,25},{... | collective-permute-start | bytes 626696 | tf_op jit(solution)/shard_map/ppermute | solution.py:29
  48.5 13.5 %collective-permute-start.13 = (bf16[48,2176]{1,0:T(8,128)(2,1)S(1)}, bf16[48,2176]{1,0:T(8,128)(2,1)S(1)}, u32[]{:S(2)}, u32[]{:S(2)}) collective-permute-start(bf16[48,2176]{1,0:T(8,128)(2,1)S(1)} %concatenate.29), channel_id=1, source_target_pairs={{0,8},{4,12},{8,0},{12,4},{16,24},{20,28},{24,16},{28,20},{1,9},{5... | collective-permute-start | bytes 626696 | tf_op jit(solution)/shard_map/ppermute | solution.py:29
  50.3 10.2 %collective-permute-start.19 = (bf16[48,1152]{1,0:T(8,128)(2,1)S(1)}, bf16[48,1152]{1,0:T(8,128)(2,1)S(1)}, u32[]{:S(2)}, u32[]{:S(2)}) collective-permute-start(bf16[48,1152]{1,0:T(8,128)(2,1)S(1)} %get-tuple-element.113.refs_1_), channel_id=1, source_target_pairs={{0,2},{1,3},{2,0},{3,1},{4,6},{5,7},{6,4},{7,5},{8,10},{9,11},{10,... | collective-permute-start | bytes 331784 | tf_op jit(solution)/shard_map/ppermute | solution.py:33
  58.3 8.3 %collective-permute-start.12 = (bf16[48,1152]{1,0:T(8,128)(2,1)S(1)}, bf16[48,1152]{1,0:T(8,128)(2,1)S(1)}, u32[]{:S(2)}, u32[]{:S(2)}) collective-permute-start(bf16[48,1152]{1,0:T(8,128)(2,1)S(1)} %slice.122), channel_id=1, source_target_pairs={{0,8},{4,12},{8,0},{12,4},{16,24},{20,28},{24,16},{28,20},{1,9},{5... | collective-permute-start | bytes 331784 | tf_op jit(solution)/shard_map/ppermute | solution.py:29
  60.5 7.7 %collective-permute-start.14 = (bf16[48,2176]{1,0:T(8,128)(2,1)S(1)}, bf16[48,2176]{1,0:T(8,128)(2,1)S(1)}, u32[]{:S(2)}, u32[]{:S(2)}) collective-permute-start(bf16[48,2176]{1,0:T(8,128)(2,1)S(1)} %collective-permute-done.10.refs_0_), channel_id=1, source_target_pairs={{0,4},{4,0},{8,12},{12,8},{16,20},{20,16},{24,28},{28,24},{1,5},{5... | collective-permute-start | bytes 626696 | tf_op jit(solution)/shard_map/ppermute | solution.py:19
  65.1 8.1 %collective-permute-start.20 = (bf16[2,48,1024]{2,1,0:T(8,128)(2,1)S(1)}, bf16[2,48,1024]{2,1,0:T(8,128)(2,1)S(1)}, u32[]{:S(2)}, u32[]{:S(2)}) collective-permute-start(bf16[2,48,1024]{2,1,0:T(8,128)(2,1)S(1)} %pad_maximum_fusion.6), channel_id=1, source_target_pairs={{0,2},{1,3},{2,0},{3,1},{4,6},{5,7},{6,4},{7,5},{8,10},{9,11},{10,... | collective-permute-start | bytes 589832 | tf_op jit(solution)/shard_map/ppermute | solution.py:33
  66.6 7.7 %collective-permute-start.21 = (bf16[2,48,1152]{2,1,0:T(8,128)(2,1)S(1)}, bf16[2,48,1152]{2,1,0:T(8,128)(2,1)S(1)}, u32[]{:S(2)}, u32[]{:S(2)}) collective-permute-start(bf16[2,48,1152]{2,1,0:T(8,128)(2,1)S(1)} %pad_maximum_fusion.2), channel_id=1, source_target_pairs={{0,4},{4,0},{8,12},{12,8},{16,20},{20,16},{24,28},{28,24},{1,5},{5... | collective-permute-start | bytes 663560 | tf_op jit(solution)/shard_map/ppermute | solution.py:19
  73.3 12.6 %collective-permute-start.25 = (bf16[2,48,2176]{2,1,0:T(8,128)(2,1)S(1)}, bf16[2,48,2176]{2,1,0:T(8,128)(2,1)S(1)}, u32[]{:S(2)}, u32[]{:S(2)}) collective-permute-start(bf16[2,48,2176]{2,1,0:T(8,128)(2,1)S(1)} %pad_maximum_fusion.1), channel_id=1, source_target_pairs={{0,4},{4,0},{8,12},{12,8},{16,20},{20,16},{24,28},{28,24},{1,5},{5... | collective-permute-start | bytes 1253384 | tf_op jit(solution)/shard_map/ppermute | solution.py:19
  74.4 11.5 %collective-permute-start.24 = (bf16[2,48,2176]{2,1,0:T(8,128)(2,1)S(1)}, bf16[2,48,2176]{2,1,0:T(8,128)(2,1)S(1)}, u32[]{:S(2)}, u32[]{:S(2)}) collective-permute-start(bf16[2,48,2176]{2,1,0:T(8,128)(2,1)S(1)} %pad_maximum_fusion), channel_id=1, source_target_pairs={{0,2},{1,3},{2,0},{3,1},{4,6},{5,7},{6,4},{7,5},{8,10},{9,11},{10,... | collective-permute-start | bytes 1253384 | tf_op jit(solution)/shard_map/ppermute | solution.py:33
  76.4 17.4 %collective-permute-start.23 = (bf16[2,48,1152]{2,1,0:T(8,128)(2,1)S(1)}, bf16[2,48,1152]{2,1,0:T(8,128)(2,1)S(1)}, u32[]{:S(2)}, u32[]{:S(2)}) collective-permute-start(bf16[2,48,1152]{2,1,0:T(8,128)(2,1)S(1)} %pad_maximum_fusion.3), channel_id=1, source_target_pairs={{0,4},{4,0},{8,12},{12,8},{16,20},{20,16},{24,28},{28,24},{1,5},{5... | collective-permute-start | bytes 663560 | tf_op jit(solution)/shard_map/ppermute | solution.py:19
  77.6 16.2 %collective-permute-start.22 = (bf16[2,48,1024]{2,1,0:T(8,128)(2,1)S(1)}, bf16[2,48,1024]{2,1,0:T(8,128)(2,1)S(1)}, u32[]{:S(2)}, u32[]{:S(2)}) collective-permute-start(bf16[2,48,1024]{2,1,0:T(8,128)(2,1)S(1)} %pad_maximum_fusion.7), channel_id=1, source_target_pairs={{0,2},{1,3},{2,0},{3,1},{4,6},{5,7},{6,4},{7,5},{8,10},{9,11},{10,... | collective-permute-start | bytes 589832 | tf_op jit(solution)/shard_map/ppermute | solution.py:33
  93.8 8.4 %collective-permute-start.28 = (bf16[2,48,2048]{2,1,0:T(8,128)(2,1)S(1)}, bf16[2,48,2048]{2,1,0:T(8,128)(2,1)S(1)}, u32[]{:S(2)}, u32[]{:S(2)}) collective-permute-start(bf16[2,48,2048]{2,1,0:T(8,128)(2,1)S(1)} %get-tuple-element.147), channel_id=1, source_target_pairs={{0,4},{4,0},{8,12},{12,8},{16,20},{20,16},{24,28},{28,24},{1,5},{5... | collective-permute-start | bytes 1179656 | tf_op jit(solution)/shard_map/ppermute | solution.py:19
  95.0 9.8 %collective-permute-start.27 = (bf16[2,48,2048]{2,1,0:T(8,128)(2,1)S(1)}, bf16[2,48,2048]{2,1,0:T(8,128)(2,1)S(1)}, u32[]{:S(2)}, u32[]{:S(2)}) collective-permute-start(bf16[2,48,2048]{2,1,0:T(8,128)(2,1)S(1)} %get-tuple-element.145), channel_id=1, source_target_pairs={{0,2},{1,3},{2,0},{3,1},{4,6},{5,7},{6,4},{7,5},{8,10},{9,11},{10,... | collective-permute-start | bytes 1179656 | tf_op jit(solution)/shard_map/ppermute | solution.py:33
  117.8 16.0 %collective-permute-start.39 = (bf16[48,2048]{1,0:T(8,128)(2,1)S(1)}, bf16[48,2048]{1,0:T(8,128)(2,1)S(1)}, u32[]{:S(2)}, u32[]{:S(2)}) collective-permute-start(bf16[48,2048]{1,0:T(8,128)(2,1)S(1)} %fusion.6), channel_id=1, source_target_pairs={{0,24},{4,28},{8,16},{12,20},{16,8},{20,12},{24,0},{28,4},{1,25},{... | collective-permute-start | bytes 589832 | tf_op jit(solution)/shard_map/ppermute | solution.py:29
  118.6 15.2 %collective-permute-start.40 = (bf16[48,2048]{1,0:T(8,128)(2,1)S(1)}, bf16[48,2048]{1,0:T(8,128)(2,1)S(1)}, u32[]{:S(2)}, u32[]{:S(2)}) collective-permute-start(bf16[48,2048]{1,0:T(8,128)(2,1)S(1)} %fusion.5), channel_id=1, source_target_pairs={{0,8},{4,12},{8,0},{12,4},{16,24},{20,28},{24,16},{28,20},{1,9},{5... | collective-permute-start | bytes 589832 | tf_op jit(solution)/shard_map/ppermute | solution.py:29
  124.1 9.7 %collective-permute-start.41 = (bf16[48,2048]{1,0:T(8,128)(2,1)S(1)}, bf16[48,2048]{1,0:T(8,128)(2,1)S(1)}, u32[]{:S(2)}, u32[]{:S(2)}) collective-permute-start(bf16[48,2048]{1,0:T(8,128)(2,1)S(1)} %pad_maximum_fusion.8), channel_id=1, source_target_pairs={{0,16},{4,20},{8,24},{12,28},{16,0},{20,4},{24,8},{28,12},{1,17},{... | collective-permute-start | bytes 589832 | tf_op jit(solution)/shard_map/ppermute | solution.py:29
  (27 other events, 234.8 us)

commit v7 on v6

--- a/solution.py
+++ b/solution.py
@@ -122,7 +122,7 @@
 
     (k_own, k_other), (v_own, v_other) = split(keys), split(values)
     own, beside = jnp.concatenate([k_own, v_own], 1), jnp.concatenate([k_other, v_other], 1)
-    own, beside, queries, held = lax.optimization_barrier((own, beside, queries, held))
+    own, beside, queries = lax.optimization_barrier((own, beside, queries))
     q_own, q_other = split(relative_rows(queries, x, core))
     beside = over_y(beside)
     blocks, shard = [own, beside], [2 * z + y, 2 * z + 1 - y]
@@ -132,7 +132,7 @@
         if k == 1:
             own, beside = lax.optimization_barrier((own, beside))
         if k == 2:
-            beside, q_beside = lax.optimization_barrier((beside, q_beside))
+            beside, q_beside, held = lax.optimization_barrier((beside, q_beside, held))
         beside = over_z(beside, 1)
         blocks += [own, beside]
         shard += [2 * (z - k) + y, 2 * (z - k) + 1 - y]

time: 135 us -> 139 us (1.030)
  waiting for transfers between devices: 54.5 us -> 62 us
  starting transfers between devices: 45.9 us -> 42.9 us
    ppermute x15, waiting for transfers between devices: 15.4 us -> 18.9 us  [over_y(): return lax.ppermute(a, 'seq', [(i, i ^ 1) for i in range(count)])]
    ppermute x4, waiting for transfers between devices: 16.8 us -> 19.5 us  [over_z(): lax.ppermute(a, 'seq', [(i, (i + 2 * step) % count) for i in range(count)])]
  transfers between devices with their start and end apart: 42 -> 42, of which waited for: 24 -> 24; matrix products, arithmetic and copies ran while one was open for 5% -> 4% of each run, Pallas kernels for 15% -> 14%
where the time goes in v7:
time: 139 us; the launch traced here: 138 us
  waiting for transfers between devices  62 us (45%)
  starting transfers between devices  42.9 us (31%)
  Pallas kernels  23.2 us (17%)
  local copies, waits for them, and re-layouts  4.48 us (3%)
  other arithmetic  3.7 us (3%)
    pallas_call x3, Pallas kernels, experts(): pl.pallas_call(functools.partial(expert_kernel, layout, ways, count), out...  20 us
    ppermute x4, waiting for transfers between devices, over_z(): lax.ppermute(a, 'seq', [(i, (i + 2 * step) % count) for i in range(count)])  19.5 us
    ppermute x15, waiting for transfers between devices, over_y(): return lax.ppermute(a, 'seq', [(i, i ^ 1) for i in range(count)])  18.9 us
    ppermute x15, starting transfers between devices, over_y(): return lax.ppermute(a, 'seq', [(i, i ^ 1) for i in range(count)])  18.6 us
    ppermute x13, waiting for transfers between devices, over_x(): return lax.ppermute(a, 'tp', [(i, i ^ 2) for i in range(4)])  15.7 us
    ppermute x13, starting transfers between devices, over_x(): return lax.ppermute(a, 'tp', [(i, i ^ 2) for i in range(4)])  15.1 us
    ppermute x7, waiting for transfers between devices, across_z(): return lax.ppermute(a, 'seq', [(i, i ^ 2 * k) for i in range(count)])  6.22 us
    ppermute x7, starting transfers between devices, across_z(): return lax.ppermute(a, 'seq', [(i, i ^ 2 * k) for i in range(count)])  4.72 us
  transfers between devices with their start and end apart: 42, of which 24 were waited for; matrix products, arithmetic and copies ran while one was open for 4% of the time, Pallas kernels for 14%

profile of v7, /device:TPU:0, one launch (start us, length us, event | category | flops | bytes accessed | tf_op | source)
XLA Modules:
  0.0 138.5 jit_solution(7672224374777291820)
XLA Ops:
  1.9 3.1 %collective-permute-start = (bf16[192,512]{1,0:T(8,128)(2,1)S(1)}, bf16[192,512]{1,0:T(8,128)(2,1)S(1)}, u32[]{:S(2)}, u32[]{:S(2)}) collective-permute-start(bf16[192,512]{1,0:T(8,128)(2,1)S(1)} %pad_maximum_fusion.4.refs_0_), channel_id=1, source_target_pairs={{0,8},{4,12},{8,16},{12,20},{16,24},{20,28},{24,0},{28,4},{1,9},{5... | collective-permute-start | bytes 589832 | tf_op jit(solution)/shard_map/ppermute | solution.py:24
  7.6 4.3 %collective-permute-done.refs_2_ = bf16[192,512]{1,0:T(8,128)(2,1)S(1)} collective-permute-done((bf16[192,512]{1,0:T(8,128)(2,1)S(1)}, bf16[192,512]{1,0:T(8,128)(2,1)S(1)}, u32[]{:S(2)}, u32[]{:S(2)}) %collective-permute-start) | collective-permute-done | bytes 196640 | tf_op jit(solution)/shard_map/ppermute | solution.py:24
  14.6 3.1 %collective-permute-done.3.q_beside = bf16[192,256]{1,0:T(8,128)(2,1)S(1)} collective-permute-done((bf16[192,256]{1,0:T(8,128)(2,1)S(1)}, bf16[192,256]{1,0:T(8,128)(2,1)S(1)}, u32[]{:S(2)}, u32[]{:S(2)}) %collective-permute-start.3) | collective-permute-done | bytes 98336 | tf_op jit(solution)/shard_map/ppermute | solution.py:19
  17.7 2.2 %collective-permute-done.2.refs_3_ = bf16[192,512]{1,0:T(8,128)(2,1)S(1)} collective-permute-done((bf16[192,512]{1,0:T(8,128)(2,1)S(1)}, bf16[192,512]{1,0:T(8,128)(2,1)S(1)}, u32[]{:S(2)}, u32[]{:S(2)}) %collective-permute-start.2) | collective-permute-done | bytes 196640 | tf_op jit(solution)/shard_map/ppermute | solution.py:24
  21.1 9.1 %collective-permute-done.4.refs_4_ = bf16[192,512]{1,0:T(8,128)(2,1)S(1)} collective-permute-done((bf16[192,512]{1,0:T(8,128)(2,1)S(1)}, bf16[192,512]{1,0:T(8,128)(2,1)S(1)}, u32[]{:S(2)}, u32[]{:S(2)}) %collective-permute-start.4) | collective-permute-done | bytes 196640 | tf_op jit(solution)/shard_map/ppermute | solution.py:24
  30.2 3.8 %collective-permute-done.5.refs_5_ = bf16[192,512]{1,0:T(8,128)(2,1)S(1)} collective-permute-done((bf16[192,512]{1,0:T(8,128)(2,1)S(1)}, bf16[192,512]{1,0:T(8,128)(2,1)S(1)}, u32[]{:S(2)}, u32[]{:S(2)}) %collective-permute-start.5) | collective-permute-done | bytes 196640 | tf_op jit(solution)/shard_map/ppermute | solution.py:24
  34.1 3.2 %shard_map.122 = bf16[384,256]{1,0:T(8,128)(2,1)S(1)} custom-call(s32[6]{0:T(128)S(1)} %broadcast_multiply_fusion.bases, bf16[192,256]{1,0:T(8,128)(2,1)S(1)} %get-tuple-element.177.q_own, bf16[192,256]{1,0:T(8,128)(2,1)S(1)} %collective-permute-done.3.q_beside, s32[384,1]{1,0:T(8,128)S(1)} %broadcast_in_dim.45.pos_ref, ...), custom_call_target="tpu_custom_call" | custom-call | flops 452984832 | bytes 1572864 | tf_op jit(solution)/shard_map/pallas_call | solution.py:99
  38.6 3.3 %collective-permute-done.7 = bf16[192,256]{1,0:T(8,128)(2,1)S(1)} collective-permute-done((bf16[192,256]{1,0:T(8,128)(2,1)S(1)}, bf16[192,256]{1,0:T(8,128)(2,1)S(1)}, u32[]{:S(2)}, u32[]{:S(2)}) %collective-permute-start.7) | collective-permute-done | bytes 98336 | tf_op jit(solution)/shard_map/ppermute | solution.py:19
  42.6 1.7 %collective-permute-done.8 = bf16[96,2048]{1,0:T(8,128)(2,1)S(1)} collective-permute-done((bf16[96,2048]{1,0:T(8,128)(2,1)S(1)}, bf16[96,2048]{1,0:T(8,128)(2,1)S(1)}, u32[]{:S(2)}, u32[]{:S(2)}) %collective-permute-start.8) | collective-permute-done | bytes 393248 | tf_op jit(solution)/shard_map/ppermute | solution.py:37
  46.2 2.6 %copy.41 = bf16[2,2048,2,256]{3,1,2,0:T(8,128)(2,1)} copy(bf16[2,2048,2,256]{3,2,1,0:T(2,128)(2,1)S(1)} %copy-done.2) | data formatting | bytes 8388608 | tf_op jit(solution)/shard_map/optimization_barrier | solution.py:336
  48.8 3.1 %collective-permute-done.9 = bf16[48,2048]{1,0:T(8,128)(2,1)S(1)} collective-permute-done((bf16[48,2048]{1,0:T(8,128)(2,1)S(1)}, bf16[48,2048]{1,0:T(8,128)(2,1)S(1)}, u32[]{:S(2)}, u32[]{:S(2)}) %collective-permute-start.9) | collective-permute-done | bytes 196640 | tf_op jit(solution)/shard_map/ppermute | solution.py:33
  55.7 2.4 %collective-permute-done.18.refs_2_ = bf16[48,1024]{1,0:T(8,128)(2,1)S(1)} collective-permute-done((bf16[48,1024]{1,0:T(8,128)(2,1)S(1)}, bf16[48,1024]{1,0:T(8,128)(2,1)S(1)}, u32[]{:S(2)}, u32[]{:S(2)}) %collective-permute-start.18) | collective-permute-done | bytes 98336 | tf_op jit(solution)/shard_map/ppermute | solution.py:19
  58.1 4.4 %collective-permute-done.10.refs_0_ = bf16[48,2176]{1,0:T(8,128)(2,1)S(1)} collective-permute-done((bf16[48,2176]{1,0:T(8,128)(2,1)S(1)}, bf16[48,2176]{1,0:T(8,128)(2,1)S(1)}, u32[]{:S(2)}, u32[]{:S(2)}) %collective-permute-start.10) | collective-permute-done | bytes 208928 | tf_op jit(solution)/shard_map/ppermute | solution.py:29
  67.4 1.8 %collective-permute-done.11.refs_0_ = bf16[48,1024]{1,0:T(8,128)(2,1)S(1)} collective-permute-done((bf16[48,1024]{1,0:T(8,128)(2,1)S(1)}, bf16[48,1024]{1,0:T(8,128)(2,1)S(1)}, u32[]{:S(2)}, u32[]{:S(2)}) %collective-permute-start.11) | collective-permute-done | bytes 98336 | tf_op jit(solution)/shard_map/ppermute | solution.py:29
  72.9 1.8 %collective-permute-start.17 = (bf16[48,1152]{1,0:T(8,128)(2,1)S(1)}, bf16[48,1152]{1,0:T(8,128)(2,1)S(1)}, u32[]{:S(2)}, u32[]{:S(2)}) collective-permute-start(bf16[48,1152]{1,0:T(8,128)(2,1)S(1)} %collective-permute-done.12.refs_1_), channel_id=1, source_target_pairs={{0,2},{1,3},{2,0},{3,1},{4,6},{5,7},{6,4},{7,5},{8,10},{9,11},{10,... | collective-permute-start | bytes 331784 | tf_op jit(solution)/shard_map/ppermute | solution.py:33
  81.5 6.0 %shard_map.123 = (bf16[2,48,1024]{2,1,0:T(8,128)(2,1)S(1)}, bf16[2,48,1024]{2,1,0:T(8,128)(2,1)S(1)}, bf16[2,48,1024]{2,1,0:T(8,128)(2,1)S(1)}, bf16[2,48,1024]{2,1,0:T(8,128)(2,1)S(1)}) custom-call(s32[1]{0:T(128)} %bitcast.15.first, bf16[48,1024]{1,0:T(8,128)(2,1)S(1)} %get-tuple-element.112.refs_0_, bf16[48,1152]{1,0:T(8,128)(2,1)S(1)} %get-tuple-element.113.refs_1_, ...), custom_call_target="tpu_custom_call" | custom-call | flops 2415919104 | bytes 14155776 | tf_op jit(solution)/shard_map/pallas_call | solution.py:218
  87.6 2.1 %collective-permute-done.25.refs_5_ = bf16[2,48,2176]{2,1,0:T(8,128)(2,1)S(1)} collective-permute-done((bf16[2,48,2176]{2,1,0:T(8,128)(2,1)S(1)}, bf16[2,48,2176]{2,1,0:T(8,128)(2,1)S(1)}, u32[]{:S(2)}, u32[]{:S(2)}) %collective-permute-start.25) | collective-permute-done | bytes 417824 | tf_op jit(solution)/shard_map/ppermute | solution.py:19
  89.6 7.9 %shard_map.124 = (bf16[2,48,2048]{2,1,0:T(8,128)(2,1)S(1)}, bf16[2,48,2048]{2,1,0:T(8,128)(2,1)S(1)}, bf16[2,48,2048]{2,1,0:T(8,128)(2,1)S(1)}, bf16[2,48,2048]{2,1,0:T(8,128)(2,1)S(1)}) custom-call(s32[1]{0:T(128)} %bitcast.15.first, bf16[48,2176]{1,0:T(8,128)(2,1)S(1)} %collective-permute-done.10.refs_0_, ...), custom_call_target="tpu_custom_call" | custom-call | flops 4831838208 | bytes 15728640 | tf_op jit(solution)/shard_map/pallas_call | solution.py:218
  100.0 6.0 %shard_map.125 = (bf16[2,48,1024]{2,1,0:T(8,128)(2,1)S(1)}, bf16[2,48,1024]{2,1,0:T(8,128)(2,1)S(1)}, bf16[2,48,1024]{2,1,0:T(8,128)(2,1)S(1)}, bf16[2,48,1024]{2,1,0:T(8,128)(2,1)S(1)}) custom-call(s32[1]{0:T(128)} %bitcast.15.first, bf16[48,1024]{1,0:T(8,128)(2,1)S(1)} %collective-permute-done.11.refs_0_, ...), custom_call_target="tpu_custom_call" | custom-call | flops 2415919104 | bytes 14155776 | tf_op jit(solution)/shard_map/pallas_call | solution.py:218
  106.2 2.6 %collective-permute-done.27 = bf16[2,48,2048]{2,1,0:T(8,128)(2,1)S(1)} collective-permute-done((bf16[2,48,2048]{2,1,0:T(8,128)(2,1)S(1)}, bf16[2,48,2048]{2,1,0:T(8,128)(2,1)S(1)}, u32[]{:S(2)}, u32[]{:S(2)}) %collective-permute-start.27) | collective-permute-done | bytes 393248 | tf_op jit(solution)/shard_map/ppermute | solution.py:33
  113.1 2.6 %collective-permute-done.32 = bf16[48,2048]{1,0:T(8,128)(2,1)S(1)} collective-permute-done((bf16[48,2048]{1,0:T(8,128)(2,1)S(1)}, bf16[48,2048]{1,0:T(8,128)(2,1)S(1)}, u32[]{:S(2)}, u32[]{:S(2)}) %collective-permute-start.32) | collective-permute-done | bytes 196640 | tf_op jit(solution)/shard_map/ppermute | solution.py:33
  117.1 2.1 %collective-permute-done.30 = bf16[2,48,1024]{2,1,0:T(8,128)(2,1)S(1)} collective-permute-done((bf16[2,48,1024]{2,1,0:T(8,128)(2,1)S(1)}, bf16[2,48,1024]{2,1,0:T(8,128)(2,1)S(1)}, u32[]{:S(2)}, u32[]{:S(2)}) %collective-permute-start.30) | collective-permute-done | bytes 196640 | tf_op jit(solution)/shard_map/ppermute | solution.py:19
  128.4 3.0 %collective-permute-done.35 = bf16[2,48,1024]{2,1,0:T(8,128)(2,1)S(1)} collective-permute-done((bf16[2,48,1024]{2,1,0:T(8,128)(2,1)S(1)}, bf16[2,48,1024]{2,1,0:T(8,128)(2,1)S(1)}, u32[]{:S(2)}, u32[]{:S(2)}) %collective-permute-start.35) | collective-permute-done | bytes 196640 | tf_op jit(solution)/shard_map/ppermute | solution.py:33
  133.8 2.4 %collective-permute-done.36 = bf16[48,1024]{1,0:T(8,128)(2,1)S(1)} collective-permute-done((bf16[48,1024]{1,0:T(8,128)(2,1)S(1)}, bf16[48,1024]{1,0:T(8,128)(2,1)S(1)}, u32[]{:S(2)}, u32[]{:S(2)}) %collective-permute-start.36) | collective-permute-done | bytes 98336 | tf_op jit(solution)/shard_map/ppermute | solution.py:19
  (148 shorter events, 52.5 us)
Async XLA Ops:
  1.9 10.0 %collective-permute-start = (bf16[192,512]{1,0:T(8,128)(2,1)S(1)}, bf16[192,512]{1,0:T(8,128)(2,1)S(1)}, u32[]{:S(2)}, u32[]{:S(2)}) collective-permute-start(bf16[192,512]{1,0:T(8,128)(2,1)S(1)} %pad_maximum_fusion.4.refs_0_), channel_id=1, source_target_pairs={{0,8},{4,12},{8,16},{12,20},{16,24},{20,28},{24,0},{28,4},{1,9},{5... | collective-permute-start | bytes 589832 | tf_op jit(solution)/shard_map/ppermute | solution.py:24
  11.9 7.9 %collective-permute-start.2 = (bf16[192,512]{1,0:T(8,128)(2,1)S(1)}, bf16[192,512]{1,0:T(8,128)(2,1)S(1)}, u32[]{:S(2)}, u32[]{:S(2)}) collective-permute-start(bf16[192,512]{1,0:T(8,128)(2,1)S(1)} %collective-permute-done.1.refs_1_), channel_id=1, source_target_pairs={{0,8},{4,12},{8,16},{12,20},{16,24},{20,28},{24,0},{28,4},{1,9},{5... | collective-permute-start | bytes 589832 | tf_op jit(solution)/shard_map/ppermute | solution.py:24
  19.8 14.2 %collective-permute-start.6 = (bf16[2,256,2048]{2,1,0:T(8,128)(2,1)}, bf16[2,256,2048]{2,1,0:T(8,128)(2,1)}, u32[]{:S(2)}, u32[]{:S(2)}) collective-permute-start(bf16[2,256,2048]{2,1,0:T(8,128)(2,1)} %refs_8_.5), channel_id=1, source_target_pairs={{0,1},{1,0},{2,3},{3,2},{4,5},{5,4},{6,7},{7,6},{8,9},{9,8},{10,11... | collective-permute-start | bytes 6291464 | tf_op jit(solution)/shard_map/ppermute | solution.py:37
  20.7 9.5 %collective-permute-start.4 = (bf16[192,512]{1,0:T(8,128)(2,1)S(1)}, bf16[192,512]{1,0:T(8,128)(2,1)S(1)}, u32[]{:S(2)}, u32[]{:S(2)}) collective-permute-start(bf16[192,512]{1,0:T(8,128)(2,1)S(1)} %collective-permute-done.refs_2_), channel_id=1, source_target_pairs={{0,8},{4,12},{8,16},{12,20},{16,24},{20,28},{24,0},{28,4},{1,9},{5... | collective-permute-start | bytes 589832 | tf_op jit(solution)/shard_map/ppermute | solution.py:24
  20.7 13.3 %collective-permute-start.5 = (bf16[192,512]{1,0:T(8,128)(2,1)S(1)}, bf16[192,512]{1,0:T(8,128)(2,1)S(1)}, u32[]{:S(2)}, u32[]{:S(2)}) collective-permute-start(bf16[192,512]{1,0:T(8,128)(2,1)S(1)} %collective-permute-done.2.refs_3_), channel_id=1, source_target_pairs={{0,8},{4,12},{8,16},{12,20},{16,24},{20,28},{24,0},{28,4},{1,9},{5... | collective-permute-start | bytes 589832 | tf_op jit(solution)/shard_map/ppermute | solution.py:24
  51.9 29.6 %collective-permute-start.26 = (bf16[2,2,2048,256]{3,2,1,0:T(8,128)(2,1)}, bf16[2,2,2048,256]{3,2,1,0:T(8,128)(2,1)}, u32[]{:S(2)}, u32[]{:S(2)}) collective-permute-start(bf16[2,2,2048,256]{3,2,1,0:T(8,128)(2,1)} %bitcast.69.refs_6_), channel_id=1, source_target_pairs={{0,1},{1,0},{2,3},{3,2},{4,5},{5,4},{6,7},{7,6},{8,9},{9,8},{10,11... | collective-permute-start | bytes 12582920 | tf_op jit(solution)/shard_map/ppermute | solution.py:37
  52.6 9.9 %collective-permute-start.10 = (bf16[48,2176]{1,0:T(8,128)(2,1)S(1)}, bf16[48,2176]{1,0:T(8,128)(2,1)S(1)}, u32[]{:S(2)}, u32[]{:S(2)}) collective-permute-start(bf16[48,2176]{1,0:T(8,128)(2,1)S(1)} %concatenate.29), channel_id=1, source_target_pairs={{0,24},{4,28},{8,16},{12,20},{16,8},{20,12},{24,0},{28,4},{1,25},{... | collective-permute-start | bytes 626696 | tf_op jit(solution)/shard_map/ppermute | solution.py:29
  52.7 13.2 %collective-permute-start.13 = (bf16[48,2176]{1,0:T(8,128)(2,1)S(1)}, bf16[48,2176]{1,0:T(8,128)(2,1)S(1)}, u32[]{:S(2)}, u32[]{:S(2)}) collective-permute-start(bf16[48,2176]{1,0:T(8,128)(2,1)S(1)} %concatenate.29), channel_id=1, source_target_pairs={{0,8},{4,12},{8,0},{12,4},{16,24},{20,28},{24,16},{28,20},{1,9},{5... | collective-permute-start | bytes 626696 | tf_op jit(solution)/shard_map/ppermute | solution.py:29
  54.2 10.5 %collective-permute-start.19 = (bf16[48,1152]{1,0:T(8,128)(2,1)S(1)}, bf16[48,1152]{1,0:T(8,128)(2,1)S(1)}, u32[]{:S(2)}, u32[]{:S(2)}) collective-permute-start(bf16[48,1152]{1,0:T(8,128)(2,1)S(1)} %get-tuple-element.113.refs_1_), channel_id=1, source_target_pairs={{0,2},{1,3},{2,0},{3,1},{4,6},{5,7},{6,4},{7,5},{8,10},{9,11},{10,... | collective-permute-start | bytes 331784 | tf_op jit(solution)/shard_map/ppermute | solution.py:33
  62.5 8.0 %collective-permute-start.12 = (bf16[48,1152]{1,0:T(8,128)(2,1)S(1)}, bf16[48,1152]{1,0:T(8,128)(2,1)S(1)}, u32[]{:S(2)}, u32[]{:S(2)}) collective-permute-start(bf16[48,1152]{1,0:T(8,128)(2,1)S(1)} %slice.122), channel_id=1, source_target_pairs={{0,8},{4,12},{8,0},{12,4},{16,24},{20,28},{24,16},{28,20},{1,9},{5... | collective-permute-start | bytes 331784 | tf_op jit(solution)/shard_map/ppermute | solution.py:29
  64.6 7.4 %collective-permute-start.14 = (bf16[48,2176]{1,0:T(8,128)(2,1)S(1)}, bf16[48,2176]{1,0:T(8,128)(2,1)S(1)}, u32[]{:S(2)}, u32[]{:S(2)}) collective-permute-start(bf16[48,2176]{1,0:T(8,128)(2,1)S(1)} %collective-permute-done.10.refs_0_), channel_id=1, source_target_pairs={{0,4},{4,0},{8,12},{12,8},{16,20},{20,16},{24,28},{28,24},{1,5},{5... | collective-permute-start | bytes 626696 | tf_op jit(solution)/shard_map/ppermute | solution.py:19
  69.3 7.8 %collective-permute-start.20 = (bf16[2,48,1024]{2,1,0:T(8,128)(2,1)S(1)}, bf16[2,48,1024]{2,1,0:T(8,128)(2,1)S(1)}, u32[]{:S(2)}, u32[]{:S(2)}) collective-permute-start(bf16[2,48,1024]{2,1,0:T(8,128)(2,1)S(1)} %pad_maximum_fusion.6), channel_id=1, source_target_pairs={{0,2},{1,3},{2,0},{3,1},{4,6},{5,7},{6,4},{7,5},{8,10},{9,11},{10,... | collective-permute-start | bytes 589832 | tf_op jit(solution)/shard_map/ppermute | solution.py:33
  70.5 7.7 %collective-permute-start.21 = (bf16[2,48,1152]{2,1,0:T(8,128)(2,1)S(1)}, bf16[2,48,1152]{2,1,0:T(8,128)(2,1)S(1)}, u32[]{:S(2)}, u32[]{:S(2)}) collective-permute-start(bf16[2,48,1152]{2,1,0:T(8,128)(2,1)S(1)} %pad_maximum_fusion.2), channel_id=1, source_target_pairs={{0,4},{4,0},{8,12},{12,8},{16,20},{20,16},{24,28},{28,24},{1,5},{5... | collective-permute-start | bytes 663560 | tf_op jit(solution)/shard_map/ppermute | solution.py:19
  72.9 7.4 %collective-permute-start.17 = (bf16[48,1152]{1,0:T(8,128)(2,1)S(1)}, bf16[48,1152]{1,0:T(8,128)(2,1)S(1)}, u32[]{:S(2)}, u32[]{:S(2)}) collective-permute-start(bf16[48,1152]{1,0:T(8,128)(2,1)S(1)} %collective-permute-done.12.refs_1_), channel_id=1, source_target_pairs={{0,2},{1,3},{2,0},{3,1},{4,6},{5,7},{6,4},{7,5},{8,10},{9,11},{10,... | collective-permute-start | bytes 331784 | tf_op jit(solution)/shard_map/ppermute | solution.py:33
  77.1 12.6 %collective-permute-start.25 = (bf16[2,48,2176]{2,1,0:T(8,128)(2,1)S(1)}, bf16[2,48,2176]{2,1,0:T(8,128)(2,1)S(1)}, u32[]{:S(2)}, u32[]{:S(2)}) collective-permute-start(bf16[2,48,2176]{2,1,0:T(8,128)(2,1)S(1)} %pad_maximum_fusion.1), channel_id=1, source_target_pairs={{0,4},{4,0},{8,12},{12,8},{16,20},{20,16},{24,28},{28,24},{1,5},{5... | collective-permute-start | bytes 1253384 | tf_op jit(solution)/shard_map/ppermute | solution.py:19
  78.3 11.4 %collective-permute-start.24 = (bf16[2,48,2176]{2,1,0:T(8,128)(2,1)S(1)}, bf16[2,48,2176]{2,1,0:T(8,128)(2,1)S(1)}, u32[]{:S(2)}, u32[]{:S(2)}) collective-permute-start(bf16[2,48,2176]{2,1,0:T(8,128)(2,1)S(1)} %pad_maximum_fusion), channel_id=1, source_target_pairs={{0,2},{1,3},{2,0},{3,1},{4,6},{5,7},{6,4},{7,5},{8,10},{9,11},{10,... | collective-permute-start | bytes 1253384 | tf_op jit(solution)/shard_map/ppermute | solution.py:33
  80.3 17.3 %collective-permute-start.23 = (bf16[2,48,1152]{2,1,0:T(8,128)(2,1)S(1)}, bf16[2,48,1152]{2,1,0:T(8,128)(2,1)S(1)}, u32[]{:S(2)}, u32[]{:S(2)}) collective-permute-start(bf16[2,48,1152]{2,1,0:T(8,128)(2,1)S(1)} %pad_maximum_fusion.3), channel_id=1, source_target_pairs={{0,4},{4,0},{8,12},{12,8},{16,20},{20,16},{24,28},{28,24},{1,5},{5... | collective-permute-start | bytes 663560 | tf_op jit(solution)/shard_map/ppermute | solution.py:19
  81.4 16.2 %collective-permute-start.22 = (bf16[2,48,1024]{2,1,0:T(8,128)(2,1)S(1)}, bf16[2,48,1024]{2,1,0:T(8,128)(2,1)S(1)}, u32[]{:S(2)}, u32[]{:S(2)}) collective-permute-start(bf16[2,48,1024]{2,1,0:T(8,128)(2,1)S(1)} %pad_maximum_fusion.7), channel_id=1, source_target_pairs={{0,2},{1,3},{2,0},{3,1},{4,6},{5,7},{6,4},{7,5},{8,10},{9,11},{10,... | collective-permute-start | bytes 589832 | tf_op jit(solution)/shard_map/ppermute | solution.py:33
  97.6 8.4 %collective-permute-start.28 = (bf16[2,48,2048]{2,1,0:T(8,128)(2,1)S(1)}, bf16[2,48,2048]{2,1,0:T(8,128)(2,1)S(1)}, u32[]{:S(2)}, u32[]{:S(2)}) collective-permute-start(bf16[2,48,2048]{2,1,0:T(8,128)(2,1)S(1)} %get-tuple-element.147), channel_id=1, source_target_pairs={{0,4},{4,0},{8,12},{12,8},{16,20},{20,16},{24,28},{28,24},{1,5},{5... | collective-permute-start | bytes 1179656 | tf_op jit(solution)/shard_map/ppermute | solution.py:19
  98.9 9.9 %collective-permute-start.27 = (bf16[2,48,2048]{2,1,0:T(8,128)(2,1)S(1)}, bf16[2,48,2048]{2,1,0:T(8,128)(2,1)S(1)}, u32[]{:S(2)}, u32[]{:S(2)}) collective-permute-start(bf16[2,48,2048]{2,1,0:T(8,128)(2,1)S(1)} %get-tuple-element.145), channel_id=1, source_target_pairs={{0,2},{1,3},{2,0},{3,1},{4,6},{5,7},{6,4},{7,5},{8,10},{9,11},{10,... | collective-permute-start | bytes 1179656 | tf_op jit(solution)/shard_map/ppermute | solution.py:33
  111.6 7.5 %collective-permute-start.30 = (bf16[2,48,1024]{2,1,0:T(8,128)(2,1)S(1)}, bf16[2,48,1024]{2,1,0:T(8,128)(2,1)S(1)}, u32[]{:S(2)}, u32[]{:S(2)}) collective-permute-start(bf16[2,48,1024]{2,1,0:T(8,128)(2,1)S(1)} %get-tuple-element.151), channel_id=1, source_target_pairs={{0,4},{4,0},{8,12},{12,8},{16,20},{20,16},{24,28},{28,24},{1,5},{5... | collective-permute-start | bytes 589832 | tf_op jit(solution)/shard_map/ppermute | solution.py:19
  121.6 16.0 %collective-permute-start.39 = (bf16[48,2048]{1,0:T(8,128)(2,1)S(1)}, bf16[48,2048]{1,0:T(8,128)(2,1)S(1)}, u32[]{:S(2)}, u32[]{:S(2)}) collective-permute-start(bf16[48,2048]{1,0:T(8,128)(2,1)S(1)} %fusion.6), channel_id=1, source_target_pairs={{0,24},{4,28},{8,16},{12,20},{16,8},{20,12},{24,0},{28,4},{1,25},{... | collective-permute-start | bytes 589832 | tf_op jit(solution)/shard_map/ppermute | solution.py:29
  122.6 15.0 %collective-permute-start.40 = (bf16[48,2048]{1,0:T(8,128)(2,1)S(1)}, bf16[48,2048]{1,0:T(8,128)(2,1)S(1)}, u32[]{:S(2)}, u32[]{:S(2)}) collective-permute-start(bf16[48,2048]{1,0:T(8,128)(2,1)S(1)} %fusion.5), channel_id=1, source_target_pairs={{0,8},{4,12},{8,0},{12,4},{16,24},{20,28},{24,16},{28,20},{1,9},{5... | collective-permute-start | bytes 589832 | tf_op jit(solution)/shard_map/ppermute | solution.py:29
  127.9 9.8 %collective-permute-start.41 = (bf16[48,2048]{1,0:T(8,128)(2,1)S(1)}, bf16[48,2048]{1,0:T(8,128)(2,1)S(1)}, u32[]{:S(2)}, u32[]{:S(2)}) collective-permute-start(bf16[48,2048]{1,0:T(8,128)(2,1)S(1)} %pad_maximum_fusion.8), channel_id=1, source_target_pairs={{0,16},{4,20},{8,24},{12,28},{16,0},{20,4},{24,8},{28,12},{1,17},{... | collective-permute-start | bytes 589832 | tf_op jit(solution)/shard_map/ppermute | solution.py:29
  (27 other events, 246.2 us)
